TPU v7x, 128 devices: a whole 4x4x4 slice. The times are simulated.
128 devices in a mesh: gx: 8 (over x, core), gy: 16 (over z, y).
Axes of the slice: x: 4, y: 4, z: 4, core: 2. Of those that a mesh axis runs over, the one named last changes fastest.
Arguments:
- local_pos: float32 [8192, 3, 128], P(('gx', 'gy')), may hold values from -1 to 1
- charges: float32 [8192, 8, 128], P(('gx', 'gy')), may hold values from -0.6 to 0.6
- counts: int32 [8192], P(('gx', 'gy')), may hold values from 1 to 128, as said below
- box_centers: float32 [3, 8192], P(None, ('gx', 'gy')), may hold values from -1 to 65
- far_list: int32 [8192, 8], P(('gx', 'gy')), may hold values from 0 to 8191, as said below
- near_list: int32 [8192, 9], P(('gx', 'gy')), may hold values from 0 to 8191, as said below
Outputs:
- product: float32 [8192, 8, 128], P(('gx', 'gy'))
- curvature: float32 [8], replicated
Inputs may be any that keep to these rules, and one draw needn't show every extreme that they name: `counts`: boxes of devices whose index along gx+gy is a multiple of 4 hold at least 64 points; box 0 holds 128. `far_list`: the 64 boxes of each device name together exactly 4 entries held on each device (its own included), box b being held by device b // 64. Entry 0 of near_list[b] is b. The other entries of the 64 boxes of each device name together exactly 4 entries held on each device (its own included), box b being held by device b // 64.
All inputs are finite; a program needn't handle non-finite values.
Results may differ from a plain program's by a relative error of at most 0.0003.
Values sent between devices are 32-bit elements; how exact they have to be, the bound alone decides.
No kernel may reach another device: no remote copies, remote signals or barrier semaphores. Data moves between devices by JAX's collectives and lax.ppermute only.
A program may use at most 64 MiB of HBM per device.

v0:
```python
import math

import jax
import jax.numpy as jnp
from jax import lax
from jax.sharding import PartitionSpec as P

NODES = 4


HALF = 0.5
ELL = 1.0
NOISE = 1.0
ROOT3 = 1.7320508075688772


def matern(dist2):
    scaled = ROOT3 * jnp.sqrt(dist2) / ELL
    return (1.0 + scaled) * jnp.exp(-scaled)


def node_values(order):
    theta = (2.0 * jnp.arange(order, dtype=jnp.float32) + 1.0) * (math.pi / (2.0 * order))
    return theta


def cheb_table(local_pos, order):
    theta = node_values(order)
    poly = [jnp.ones_like(local_pos), local_pos]
    for level in range(2, order):
        poly.append(2.0 * local_pos * poly[-1] - poly[-2])
    accum = jnp.full(local_pos.shape[:1] + (order,) + local_pos.shape[1:], 1.0 / order, jnp.float32)
    for level in range(1, order):
        accum = (
            accum
            + 2.0 / order * jnp.cos(level * theta)[None, :, None, None] * poly[level][:, None, :, :]
        )
    full = jnp.einsum("bip,bjp,blp->bijlp", accum[:, :, 0], accum[:, :, 1], accum[:, :, 2])
    return full.reshape(local_pos.shape[0], order**3, local_pos.shape[2])


def node_coords(order):
    nodes = jnp.cos(node_values(order))
    index = jnp.arange(order**3)
    return jnp.stack(
        [nodes[index // (order * order)], nodes[index // order % order], nodes[index % order]]
    )


def one_box(
    tgt_pos, tgt_center, table, q_tgt, far_w, far_center, near_pos, near_q, near_center, nodes
):
    gap = tgt_center[None, :] - far_center
    spread = HALF * (nodes[:, :, None] - nodes[:, None, :])
    dist2 = jnp.zeros((far_w.shape[0],) + spread.shape[1:], jnp.float32)
    for dim in range(3):
        dist2 = dist2 + (gap[:, dim][:, None, None] + spread[dim][None]) ** 2
    local_w = jnp.einsum("frn,fmn->rm", far_w, matern(dist2), precision=lax.Precision.HIGHEST)
    far_out = jnp.dot(local_w, table, precision=lax.Precision.HIGHEST)
    tgt_abs = tgt_center[:, None] + HALF * tgt_pos
    src_abs = near_center[:, :, None] + HALF * near_pos
    near2 = jnp.zeros((near_pos.shape[0], tgt_pos.shape[1], near_pos.shape[2]), jnp.float32)
    for dim in range(3):
        near2 = near2 + (tgt_abs[dim][None, :, None] - src_abs[:, dim][:, None, :]) ** 2
    near_out = jnp.einsum("fpq,frq->rp", matern(near2), near_q, precision=lax.Precision.HIGHEST)
    return far_out + near_out + NOISE * q_tgt


def bucket_ids(id_list, per_device, device_count):
    flat = id_list.reshape(-1)
    owner = flat // per_device
    within = flat % per_device
    onehot = (owner[:, None] == jnp.arange(device_count)[None, :]).astype(jnp.int32)
    rank = jnp.sum(onehot * (jnp.cumsum(onehot, axis=0) - 1), axis=1)
    per_peer = flat.shape[0] // device_count
    position = owner * per_peer + rank
    wanted = jnp.zeros((device_count * per_peer,), jnp.int32).at[position].set(within)
    return (wanted.reshape(device_count, per_peer), position)


def on_device(local_pos, charges, counts, box_centers, far_list, near_list):
    count_x = lax.axis_size("gx")
    count_y = lax.axis_size("gy")
    device_count = count_x * count_y
    nboxes = local_pos.shape[0]
    slots = local_pos.shape[2]
    live = (jnp.arange(slots)[None, :] < counts[:, None]).astype(jnp.float32)
    masked = charges * live[:, None, :]
    table = cheb_table(local_pos, NODES)
    weights = jnp.einsum("brp,bkp->brk", masked, table, precision=lax.Precision.HIGHEST)
    centers = box_centers.T
    nodes = node_coords(NODES)
    near_rest = near_list[:, 1:]
    others = near_rest.shape[1]
    far_wanted, far_place = bucket_ids(far_list, nboxes, device_count)
    near_wanted, near_place = bucket_ids(near_rest, nboxes, device_count)
    served_far, served_near = (
        lax.all_to_all(far_wanted, ("gx", "gy"), split_axis=0, concat_axis=0, tiled=True),
        lax.all_to_all(near_wanted, ("gx", "gy"), split_axis=0, concat_axis=0, tiled=True),
    )
    width_w = weights.shape[1] * weights.shape[2]
    outgoing = (
        weights[served_far].reshape(served_far.shape + (width_w,)),
        centers[served_far],
        local_pos[served_near],
        masked[served_near],
        centers[served_near],
    )
    arrived = (
        lax.all_to_all(outgoing[0], ("gx", "gy"), split_axis=0, concat_axis=0, tiled=True),
        lax.all_to_all(outgoing[1], ("gx", "gy"), split_axis=0, concat_axis=0, tiled=True),
        lax.all_to_all(outgoing[2], ("gx", "gy"), split_axis=0, concat_axis=0, tiled=True),
        lax.all_to_all(outgoing[3], ("gx", "gy"), split_axis=0, concat_axis=0, tiled=True),
        lax.all_to_all(outgoing[4], ("gx", "gy"), split_axis=0, concat_axis=0, tiled=True),
    )
    got_w, got_far_c, got_pos, got_q, got_near_c = arrived
    flatten = lambda arr: arr.reshape((arr.shape[0] * arr.shape[1],) + arr.shape[2:])
    far_w = flatten(got_w)[far_place].reshape(
        nboxes, far_list.shape[1], weights.shape[1], weights.shape[2]
    )
    far_c = flatten(got_far_c)[far_place].reshape(nboxes, far_list.shape[1], 3)
    rest_pos = flatten(got_pos)[near_place].reshape((nboxes, others) + local_pos.shape[1:])
    rest_q = flatten(got_q)[near_place].reshape((nboxes, others) + masked.shape[1:])
    rest_c = flatten(got_near_c)[near_place].reshape(nboxes, others, 3)
    near_pos = jnp.concatenate([local_pos[:, None], rest_pos], axis=1)
    near_q = jnp.concatenate([masked[:, None], rest_q], axis=1)
    near_c = jnp.concatenate([centers[:, None], rest_c], axis=1)
    block = math.gcd(nboxes, 8)
    grouped = lambda arr: arr.reshape((nboxes // block, block) + arr.shape[1:])
    result = lax.map(
        lambda items: jax.vmap(one_box, in_axes=(0, 0, 0, 0, 0, 0, 0, 0, 0, None))(*items, nodes),
        (
            grouped(local_pos),
            grouped(centers),
            grouped(table),
            grouped(masked),
            grouped(far_w),
            grouped(far_c),
            grouped(near_pos),
            grouped(near_q),
            grouped(near_c),
        ),
    )
    product = result.reshape(masked.shape) * live[:, None, :]
    terms = jnp.sum(masked * product, axis=(0, 2))
    total = lax.psum(terms, ("gx", "gy"))
    curvature = total / (device_count * nboxes * slots)
    return (product, curvature)


def solution(mesh):
    in_specs = (
        P(("gx", "gy"), None, None),
        P(("gx", "gy"), None, None),
        P(("gx", "gy")),
        P(None, ("gx", "gy")),
        P(("gx", "gy"), None),
        P(("gx", "gy"), None),
    )
    out_specs = (P(("gx", "gy"), None, None), P())
    return jax.shard_map(
        on_device, mesh=mesh, in_specs=in_specs, out_specs=out_specs, check_vma=False
    )
```

profile of v0, /device:TPU:1, one launch (start us, length us, event | category | flops | bytes accessed | tf_op | source)
XLA Modules:
  0.0 352.7 jit_solution(12423078795634616503)
XLA Ops:
  2.5 2.4 scatter_custom_fusion
  5.7 11.5 %all-to-all-start = ((s32[128,1,4]{2,1,0:T(1,128)}), s32[128,1,4]{2,1,0:T(1,128)S(1)}, u32[]{:S(2)}, u32[]{:S(2)}) async-start(s32[128,1,4]{2,1,0:T(1,128)} %bitcast.39), calls=%async_computation | async-start | bytes 131072 | tf_op jit(solution)/shard_map/all_to_all | solution.py:98
  19.5 2.4 scatter_custom_fusion.1
  22.8 4.1 %all-to-all-done = s32[128,1,4]{2,1,0:T(1,128)S(1)} async-done(((s32[128,1,4]{2,1,0:T(1,128)}), s32[128,1,4]{2,1,0:T(1,128)S(1)}, u32[]{:S(2)}, u32[]{:S(2)}) %all-to-all-start) | async-done | bytes 2080 | tf_op jit(solution)/shard_map/all_to_all | solution.py:98
  26.9 5.7 %all-to-all-start.3 = ((s32[128,1,4]{2,1,0:T(1,128)}), s32[128,1,4]{2,1,0:T(1,128)S(1)}, u32[]{:S(2)}, u32[]{:S(2)}) async-start(s32[128,1,4]{2,1,0:T(1,128)} %bitcast.61), calls=%async_computation.3 | async-start | bytes 131072 | tf_op jit(solution)/shard_map/all_to_all | solution.py:99
  32.7 9.7 %all-to-all-done.3 = s32[128,1,4]{2,1,0:T(1,128)S(1)} async-done(((s32[128,1,4]{2,1,0:T(1,128)}), s32[128,1,4]{2,1,0:T(1,128)S(1)}, u32[]{:S(2)}, u32[]{:S(2)}) %all-to-all-start.3) | async-done | bytes 2080 | tf_op jit(solution)/shard_map/all_to_all | solution.py:99
  42.5 1.6 gather_fusion.6
  44.1 4.3 %all-to-all-start.5 = ((f32[128,4,3]{2,1,0:T(4,128)}), f32[128,4,3]{2,1,0:T(4,128)S(1)}, u32[]{:S(2)}, u32[]{:S(2)}) async-start(f32[128,4,3]{2,1,0:T(4,128)} %bitcast.68), calls=%async_computation.5 | async-start | bytes 524288 | tf_op jit(solution)/shard_map/all_to_all | solution.py:114
  48.4 1.6 gather_fusion.2
  50.1 9.9 %all-to-all-done.5 = f32[128,4,3]{2,1,0:T(4,128)S(1)} async-done(((f32[128,4,3]{2,1,0:T(4,128)}), f32[128,4,3]{2,1,0:T(4,128)S(1)}, u32[]{:S(2)}, u32[]{:S(2)}) %all-to-all-start.5) | async-done | bytes 6176 | tf_op jit(solution)/shard_map/all_to_all | solution.py:114
  60.0 4.0 %all-to-all-start.2 = ((f32[128,4,3]{2,1,0:T(4,128)}), f32[128,4,3]{2,1,0:T(4,128)S(1)}, u32[]{:S(2)}, u32[]{:S(2)}) async-start(f32[128,4,3]{2,1,0:T(4,128)} %bitcast.43), calls=%async_computation.2 | async-start | bytes 524288 | tf_op jit(solution)/shard_map/all_to_all | solution.py:111
  64.1 2.3 gather_fusion.8
  67.4 8.1 %all-to-all-done.2 = f32[128,4,3]{2,1,0:T(4,128)S(1)} async-done(((f32[128,4,3]{2,1,0:T(4,128)}), f32[128,4,3]{2,1,0:T(4,128)S(1)}, u32[]{:S(2)}, u32[]{:S(2)}) %all-to-all-start.2) | async-done | bytes 6176 | tf_op jit(solution)/shard_map/all_to_all | solution.py:111
  75.5 4.9 %all-to-all-start.6 = ((f32[128,4,3,128]{3,1,2,0:T(4,128)}), f32[128,4,3,128]{3,1,2,0:T(4,128)}, u32[]{:S(2)}, u32[]{:S(2)}) async-start(f32[128,4,3,128]{3,1,2,0:T(4,128)} %copy.51), calls=%async_computation.6 | async-start | bytes 1572864 | tf_op jit(solution)/shard_map/all_to_all | solution.py:112
  82.0 3.4 fusion.99
  85.4 2.7 gather_fusion
  88.1 2.8 reshape.576
  90.9 6.0 %all-to-all-done.6 = f32[128,4,3,128]{3,1,2,0:T(4,128)} async-done(((f32[128,4,3,128]{3,1,2,0:T(4,128)}), f32[128,4,3,128]{3,1,2,0:T(4,128)}, u32[]{:S(2)}, u32[]{:S(2)}) %all-to-all-start.6) | async-done | bytes 786464 | tf_op jit(solution)/shard_map/all_to_all | solution.py:112
  96.9 5.2 %all-to-all-start.1 = ((f32[128,4,512]{2,1,0:T(4,128)}), f32[128,4,512]{2,1,0:T(4,128)}, u32[]{:S(2)}, u32[]{:S(2)}) async-start(f32[128,4,512]{2,1,0:T(4,128)} %reshape.576), calls=%async_computation.1 | async-start | bytes 2097152 | tf_op jit(solution)/shard_map/all_to_all | solution.py:110
  102.2 2.7 gather_fusion.4
  104.9 15.9 %all-to-all-done.1 = f32[128,4,512]{2,1,0:T(4,128)} async-done(((f32[128,4,512]{2,1,0:T(4,128)}), f32[128,4,512]{2,1,0:T(4,128)}, u32[]{:S(2)}, u32[]{:S(2)}) %all-to-all-start.1) | async-done | bytes 1048608 | tf_op jit(solution)/shard_map/all_to_all | solution.py:110
  120.8 5.8 %all-to-all-start.4 = ((f32[128,4,8,128]{3,2,1,0:T(8,128)}), f32[128,4,8,128]{3,2,1,0:T(8,128)}, u32[]{:S(2)}, u32[]{:S(2)}) async-start(f32[128,4,8,128]{3,2,1,0:T(8,128)} %bitcast.207), calls=%async_computation.4 | async-start | bytes 4194304 | tf_op jit(solution)/shard_map/all_to_all | solution.py:113
  127.9 2.6 fusion.96
  130.5 2.6 fusion.94
  138.9 2.6 gather_fusion.9
  145.8 2.3 gather_fusion.1
  148.1 2.8 reshape_reshape.9
  150.9 4.7 %all-to-all-done.4 = f32[128,4,8,128]{3,2,1,0:T(8,128)} async-done(((f32[128,4,8,128]{3,2,1,0:T(8,128)}), f32[128,4,8,128]{3,2,1,0:T(8,128)}, u32[]{:S(2)}, u32[]{:S(2)}) %all-to-all-start.4) | async-done | bytes 2097184 | tf_op jit(solution)/shard_map/all_to_all | solution.py:113
  155.6 3.9 %gather_fusion.5 = f32[512,8,128]{2,1,0:T(8,128)} fusion(f32[512,8,128]{2,1,0:T(8,128)} %bitcast.64, s32[1024]{0:T(1024)S(1)} %pad_clamp_fusion), kind=kCustom, calls=%fused_computation.5 | custom fusion | bytes 4196352 | tf_op jit(solution)/shard_map/gather | solution.py:123
  159.5 3.2 pad_maximum_fusion
  162.7 124.5 %while.10 = (s32[]{:T(128)}, f32[8,8,8,128]{3,2,1,0:T(8,128)S(1)}, f32[8,8,8,8,64]{4,3,2,1,0:T(8,128)}, f32[8,8,3]{1,2,0:T(4,128)S(1)}, f32[8,8,8,3]{2,1,3,0:T(8...) while((s32[]{:T(128)}, f32[8,8,8,128]{3,2,1,0:T(8,128)S(1)}, ...), condition=%wide.region_9.10_spmd, body=%wide.region_8.9_spmd.sunk | while | flops 162107584 | bytes 1820209 | solution.py:130
  163.7 4.2 %fusion.125 = f32[8,8,64]{2,1,0:T(8,128)S(1)} fusion(f32[64,64]{1,0:T(8,128)S(1)} %get-tuple-element.247, f32[8,8]{1,0:T(8,128)S(1)} %get-tuple-element.248, f32[64,64]{1,0:T(8,128)S(1)} %get-tuple-element.249, f32[8,8]{1,0:T(8,128)S(1)} %get-tuple-element.250, f32[64,64]{1,0:T(8,128)S(1)} %get-tuple-element.251, ...), kind=kOutput, calls=%fused_computation.55.clone.1 | convolution fusion | flops 28311552 | bytes 328960 | tf_op jit(solution)/shard_map/while/body/eval_jaxpr/vmap(frn,fmn->rm)/dot_general | solution.py:58
  169.7 8.2 %fusion.124 = f32[8,8,128]{2,1,0:T(8,128)S(1)} fusion(f32[8,9,128]{2,1,0:T(8,128)S(1)} %get-tuple-element.241, f32[8,128]{1,0:T(8,128)S(1)} %get-tuple-element.242, f32[8,9,128]{2,1,0:T(8,128)S(1)} %get-tuple-element.243, f32[8,128]{1,0:T(8,128)S(1)} %get-tuple-element.244, f32[8,9,128]{2,1,0:T(8,128)S(1)} %get-tuple-element.245, ...), kind=kOutput, calls=%fused_computation.50.clone.1 | convolution fusion | flops 127401984 | bytes 451072 | tf_op jit(solution)/shard_map/while/body/eval_jaxpr/vmap(fpq,frq->rp)/dot_general | solution.py:65
  179.2 4.2 %fusion.125 = f32[8,8,64]{2,1,0:T(8,128)S(1)} fusion(f32[64,64]{1,0:T(8,128)S(1)} %get-tuple-element.247, f32[8,8]{1,0:T(8,128)S(1)} %get-tuple-element.248, f32[64,64]{1,0:T(8,128)S(1)} %get-tuple-element.249, f32[8,8]{1,0:T(8,128)S(1)} %get-tuple-element.250, f32[64,64]{1,0:T(8,128)S(1)} %get-tuple-element.251, ...), kind=kOutput, calls=%fused_computation.55.clone.1 | convolution fusion | flops 28311552 | bytes 328960 | tf_op jit(solution)/shard_map/while/body/eval_jaxpr/vmap(frn,fmn->rm)/dot_general | solution.py:58
  185.3 8.2 %fusion.124 = f32[8,8,128]{2,1,0:T(8,128)S(1)} fusion(f32[8,9,128]{2,1,0:T(8,128)S(1)} %get-tuple-element.241, f32[8,128]{1,0:T(8,128)S(1)} %get-tuple-element.242, f32[8,9,128]{2,1,0:T(8,128)S(1)} %get-tuple-element.243, f32[8,128]{1,0:T(8,128)S(1)} %get-tuple-element.244, f32[8,9,128]{2,1,0:T(8,128)S(1)} %get-tuple-element.245, ...), kind=kOutput, calls=%fused_computation.50.clone.1 | convolution fusion | flops 127401984 | bytes 451072 | tf_op jit(solution)/shard_map/while/body/eval_jaxpr/vmap(fpq,frq->rp)/dot_general | solution.py:65
  194.8 4.2 %fusion.125 = f32[8,8,64]{2,1,0:T(8,128)S(1)} fusion(f32[64,64]{1,0:T(8,128)S(1)} %get-tuple-element.247, f32[8,8]{1,0:T(8,128)S(1)} %get-tuple-element.248, f32[64,64]{1,0:T(8,128)S(1)} %get-tuple-element.249, f32[8,8]{1,0:T(8,128)S(1)} %get-tuple-element.250, f32[64,64]{1,0:T(8,128)S(1)} %get-tuple-element.251, ...), kind=kOutput, calls=%fused_computation.55.clone.1 | convolution fusion | flops 28311552 | bytes 328960 | tf_op jit(solution)/shard_map/while/body/eval_jaxpr/vmap(frn,fmn->rm)/dot_general | solution.py:58
  200.8 8.2 %fusion.124 = f32[8,8,128]{2,1,0:T(8,128)S(1)} fusion(f32[8,9,128]{2,1,0:T(8,128)S(1)} %get-tuple-element.241, f32[8,128]{1,0:T(8,128)S(1)} %get-tuple-element.242, f32[8,9,128]{2,1,0:T(8,128)S(1)} %get-tuple-element.243, f32[8,128]{1,0:T(8,128)S(1)} %get-tuple-element.244, f32[8,9,128]{2,1,0:T(8,128)S(1)} %get-tuple-element.245, ...), kind=kOutput, calls=%fused_computation.50.clone.1 | convolution fusion | flops 127401984 | bytes 451072 | tf_op jit(solution)/shard_map/while/body/eval_jaxpr/vmap(fpq,frq->rp)/dot_general | solution.py:65
  210.3 4.2 %fusion.125 = f32[8,8,64]{2,1,0:T(8,128)S(1)} fusion(f32[64,64]{1,0:T(8,128)S(1)} %get-tuple-element.247, f32[8,8]{1,0:T(8,128)S(1)} %get-tuple-element.248, f32[64,64]{1,0:T(8,128)S(1)} %get-tuple-element.249, f32[8,8]{1,0:T(8,128)S(1)} %get-tuple-element.250, f32[64,64]{1,0:T(8,128)S(1)} %get-tuple-element.251, ...), kind=kOutput, calls=%fused_computation.55.clone.1 | convolution fusion | flops 28311552 | bytes 328960 | tf_op jit(solution)/shard_map/while/body/eval_jaxpr/vmap(frn,fmn->rm)/dot_general | solution.py:58
  216.4 8.2 %fusion.124 = f32[8,8,128]{2,1,0:T(8,128)S(1)} fusion(f32[8,9,128]{2,1,0:T(8,128)S(1)} %get-tuple-element.241, f32[8,128]{1,0:T(8,128)S(1)} %get-tuple-element.242, f32[8,9,128]{2,1,0:T(8,128)S(1)} %get-tuple-element.243, f32[8,128]{1,0:T(8,128)S(1)} %get-tuple-element.244, f32[8,9,128]{2,1,0:T(8,128)S(1)} %get-tuple-element.245, ...), kind=kOutput, calls=%fused_computation.50.clone.1 | convolution fusion | flops 127401984 | bytes 451072 | tf_op jit(solution)/shard_map/while/body/eval_jaxpr/vmap(fpq,frq->rp)/dot_general | solution.py:65
  225.9 4.2 %fusion.125 = f32[8,8,64]{2,1,0:T(8,128)S(1)} fusion(f32[64,64]{1,0:T(8,128)S(1)} %get-tuple-element.247, f32[8,8]{1,0:T(8,128)S(1)} %get-tuple-element.248, f32[64,64]{1,0:T(8,128)S(1)} %get-tuple-element.249, f32[8,8]{1,0:T(8,128)S(1)} %get-tuple-element.250, f32[64,64]{1,0:T(8,128)S(1)} %get-tuple-element.251, ...), kind=kOutput, calls=%fused_computation.55.clone.1 | convolution fusion | flops 28311552 | bytes 328960 | tf_op jit(solution)/shard_map/while/body/eval_jaxpr/vmap(frn,fmn->rm)/dot_general | solution.py:58
  232.0 8.2 %fusion.124 = f32[8,8,128]{2,1,0:T(8,128)S(1)} fusion(f32[8,9,128]{2,1,0:T(8,128)S(1)} %get-tuple-element.241, f32[8,128]{1,0:T(8,128)S(1)} %get-tuple-element.242, f32[8,9,128]{2,1,0:T(8,128)S(1)} %get-tuple-element.243, f32[8,128]{1,0:T(8,128)S(1)} %get-tuple-element.244, f32[8,9,128]{2,1,0:T(8,128)S(1)} %get-tuple-element.245, ...), kind=kOutput, calls=%fused_computation.50.clone.1 | convolution fusion | flops 127401984 | bytes 451072 | tf_op jit(solution)/shard_map/while/body/eval_jaxpr/vmap(fpq,frq->rp)/dot_general | solution.py:65
  241.4 4.2 %fusion.125 = f32[8,8,64]{2,1,0:T(8,128)S(1)} fusion(f32[64,64]{1,0:T(8,128)S(1)} %get-tuple-element.247, f32[8,8]{1,0:T(8,128)S(1)} %get-tuple-element.248, f32[64,64]{1,0:T(8,128)S(1)} %get-tuple-element.249, f32[8,8]{1,0:T(8,128)S(1)} %get-tuple-element.250, f32[64,64]{1,0:T(8,128)S(1)} %get-tuple-element.251, ...), kind=kOutput, calls=%fused_computation.55.clone.1 | convolution fusion | flops 28311552 | bytes 328960 | tf_op jit(solution)/shard_map/while/body/eval_jaxpr/vmap(frn,fmn->rm)/dot_general | solution.py:58
  247.5 8.2 %fusion.124 = f32[8,8,128]{2,1,0:T(8,128)S(1)} fusion(f32[8,9,128]{2,1,0:T(8,128)S(1)} %get-tuple-element.241, f32[8,128]{1,0:T(8,128)S(1)} %get-tuple-element.242, f32[8,9,128]{2,1,0:T(8,128)S(1)} %get-tuple-element.243, f32[8,128]{1,0:T(8,128)S(1)} %get-tuple-element.244, f32[8,9,128]{2,1,0:T(8,128)S(1)} %get-tuple-element.245, ...), kind=kOutput, calls=%fused_computation.50.clone.1 | convolution fusion | flops 127401984 | bytes 451072 | tf_op jit(solution)/shard_map/while/body/eval_jaxpr/vmap(fpq,frq->rp)/dot_general | solution.py:65
  257.0 4.2 %fusion.125 = f32[8,8,64]{2,1,0:T(8,128)S(1)} fusion(f32[64,64]{1,0:T(8,128)S(1)} %get-tuple-element.247, f32[8,8]{1,0:T(8,128)S(1)} %get-tuple-element.248, f32[64,64]{1,0:T(8,128)S(1)} %get-tuple-element.249, f32[8,8]{1,0:T(8,128)S(1)} %get-tuple-element.250, f32[64,64]{1,0:T(8,128)S(1)} %get-tuple-element.251, ...), kind=kOutput, calls=%fused_computation.55.clone.1 | convolution fusion | flops 28311552 | bytes 328960 | tf_op jit(solution)/shard_map/while/body/eval_jaxpr/vmap(frn,fmn->rm)/dot_general | solution.py:58
  263.1 8.2 %fusion.124 = f32[8,8,128]{2,1,0:T(8,128)S(1)} fusion(f32[8,9,128]{2,1,0:T(8,128)S(1)} %get-tuple-element.241, f32[8,128]{1,0:T(8,128)S(1)} %get-tuple-element.242, f32[8,9,128]{2,1,0:T(8,128)S(1)} %get-tuple-element.243, f32[8,128]{1,0:T(8,128)S(1)} %get-tuple-element.244, f32[8,9,128]{2,1,0:T(8,128)S(1)} %get-tuple-element.245, ...), kind=kOutput, calls=%fused_computation.50.clone.1 | convolution fusion | flops 127401984 | bytes 451072 | tf_op jit(solution)/shard_map/while/body/eval_jaxpr/vmap(fpq,frq->rp)/dot_general | solution.py:65
  272.5 4.2 %fusion.125 = f32[8,8,64]{2,1,0:T(8,128)S(1)} fusion(f32[64,64]{1,0:T(8,128)S(1)} %get-tuple-element.247, f32[8,8]{1,0:T(8,128)S(1)} %get-tuple-element.248, f32[64,64]{1,0:T(8,128)S(1)} %get-tuple-element.249, f32[8,8]{1,0:T(8,128)S(1)} %get-tuple-element.250, f32[64,64]{1,0:T(8,128)S(1)} %get-tuple-element.251, ...), kind=kOutput, calls=%fused_computation.55.clone.1 | convolution fusion | flops 28311552 | bytes 328960 | tf_op jit(solution)/shard_map/while/body/eval_jaxpr/vmap(frn,fmn->rm)/dot_general | solution.py:58
  278.6 8.2 %fusion.124 = f32[8,8,128]{2,1,0:T(8,128)S(1)} fusion(f32[8,9,128]{2,1,0:T(8,128)S(1)} %get-tuple-element.241, f32[8,128]{1,0:T(8,128)S(1)} %get-tuple-element.242, f32[8,9,128]{2,1,0:T(8,128)S(1)} %get-tuple-element.243, f32[8,128]{1,0:T(8,128)S(1)} %get-tuple-element.244, f32[8,9,128]{2,1,0:T(8,128)S(1)} %get-tuple-element.245, ...), kind=kOutput, calls=%fused_computation.50.clone.1 | convolution fusion | flops 127401984 | bytes 451072 | tf_op jit(solution)/shard_map/while/body/eval_jaxpr/vmap(fpq,frq->rp)/dot_general | solution.py:65
  288.0 64.1 %psum.7 = f32[8]{0:T(128)S(1)} all-reduce(f32[8]{0:T(128)S(1)} %get-tuple-element.125), channel_id=1, replica_groups=mesh['gx'=8,'gy'=16] {'gx','gy'}, use_global_device_ids=true, to_apply=%region_11.12 | all-reduce | flops 8 | bytes 64 | tf_op jit(solution)/shard_map/psum | solution.py:146
  (175 shorter events, 46.0 us)
Async XLA Ops:
  0.6 16.7 %copy-start.7 = (s32[64,9]{0,1:T(8,128)S(1)}, s32[64,9]{0,1:T(8,128)}, u32[]{:S(2)}) copy-start(s32[64,9]{0,1:T(8,128)} %param.13) | copy-start | bytes 6916
  0.6 17.0 %copy-start = (f32[64,3,128]{2,0,1:T(8,128)S(1)}, f32[64,3,128]{2,0,1:T(8,128)}, u32[]{:S(2)}) copy-start(f32[64,3,128]{2,0,1:T(8,128)} %param.8) | copy-start | bytes 294916
  5.7 21.2 %all-to-all-start = ((s32[128,1,4]{2,1,0:T(1,128)}), s32[128,1,4]{2,1,0:T(1,128)S(1)}, u32[]{:S(2)}, u32[]{:S(2)}) async-start(s32[128,1,4]{2,1,0:T(1,128)} %bitcast.39), calls=%async_computation | async-start | bytes 131072 | tf_op jit(solution)/shard_map/all_to_all | solution.py:98
  17.7 5.0 %copy-start.6 = (f32[3,64]{1,0:T(4,128)S(1)}, f32[3,64]{1,0:T(4,128)}, u32[]{:S(2)}) copy-start(f32[3,64]{1,0:T(4,128)} %param.11) | copy-start | bytes 2308
  26.9 15.5 %all-to-all-start.3 = ((s32[128,1,4]{2,1,0:T(1,128)}), s32[128,1,4]{2,1,0:T(1,128)S(1)}, u32[]{:S(2)}, u32[]{:S(2)}) async-start(s32[128,1,4]{2,1,0:T(1,128)} %bitcast.61), calls=%async_computation.3 | async-start | bytes 131072 | tf_op jit(solution)/shard_map/all_to_all | solution.py:99
  44.1 19.9 %copy-start.8 = (s32[64]{0:T(128)S(1)}, s32[64]{0:T(128)}, u32[]{:S(2)}) copy-start(s32[64]{0:T(128)} %param.10) | copy-start | bytes 772
  44.1 15.9 %all-to-all-start.5 = ((f32[128,4,3]{2,1,0:T(4,128)}), f32[128,4,3]{2,1,0:T(4,128)S(1)}, u32[]{:S(2)}, u32[]{:S(2)}) async-start(f32[128,4,3]{2,1,0:T(4,128)} %bitcast.68), calls=%async_computation.5 | async-start | bytes 524288 | tf_op jit(solution)/shard_map/all_to_all | solution.py:114
  60.0 15.5 %all-to-all-start.2 = ((f32[128,4,3]{2,1,0:T(4,128)}), f32[128,4,3]{2,1,0:T(4,128)S(1)}, u32[]{:S(2)}, u32[]{:S(2)}) async-start(f32[128,4,3]{2,1,0:T(4,128)} %bitcast.43), calls=%async_computation.2 | async-start | bytes 524288 | tf_op jit(solution)/shard_map/all_to_all | solution.py:111
  64.1 16.4 %copy-start.3 = (f32[64,128]{1,0:T(8,128)}, f32[64,128]{1,0:T(8,128)S(1)}, u32[]{:S(2)}) copy-start(f32[64,128]{1,0:T(8,128)S(1)} %fusion.83) | copy-start | bytes 98308
  66.4 14.1 %copy-start.1 = (f32[64,8,128]{2,1,0:T(8,128)S(1)}, f32[64,8,128]{2,1,0:T(8,128)}, u32[]{:S(2)}) copy-start(f32[64,8,128]{2,1,0:T(8,128)} %param.9) | copy-start | bytes 786436
  75.5 21.4 %all-to-all-start.6 = ((f32[128,4,3,128]{3,1,2,0:T(4,128)}), f32[128,4,3,128]{3,1,2,0:T(4,128)}, u32[]{:S(2)}, u32[]{:S(2)}) async-start(f32[128,4,3,128]{3,1,2,0:T(4,128)} %copy.51), calls=%async_computation.6 | async-start | bytes 1572864 | tf_op jit(solution)/shard_map/all_to_all | solution.py:112
  96.9 23.8 %all-to-all-start.1 = ((f32[128,4,512]{2,1,0:T(4,128)}), f32[128,4,512]{2,1,0:T(4,128)}, u32[]{:S(2)}, u32[]{:S(2)}) async-start(f32[128,4,512]{2,1,0:T(4,128)} %reshape.576), calls=%async_computation.1 | async-start | bytes 2097152 | tf_op jit(solution)/shard_map/all_to_all | solution.py:110
  120.8 34.8 %all-to-all-start.4 = ((f32[128,4,8,128]{3,2,1,0:T(8,128)}), f32[128,4,8,128]{3,2,1,0:T(8,128)}, u32[]{:S(2)}, u32[]{:S(2)}) async-start(f32[128,4,8,128]{3,2,1,0:T(8,128)} %bitcast.207), calls=%async_computation.4 | async-start | bytes 4194304 | tf_op jit(solution)/shard_map/all_to_all | solution.py:113
  159.5 3.2 copy-start.5
  162.7 124.5 %copy-start.2 = (f32[64,8,128]{2,1,0:T(8,128)S(1)}, f32[64,8,128]{2,1,0:T(8,128)}, u32[]{:S(2)}) copy-start(f32[64,8,128]{2,1,0:T(8,128)} %param.9) | copy-start | bytes 786436
  162.7 124.5 %copy-start.4 = (f32[64,128]{1,0:T(8,128)S(1)}, f32[64,128]{1,0:T(8,128)}, u32[]{:S(2)}) copy-start(f32[64,128]{1,0:T(8,128)} %copy-done.3) | copy-start | bytes 98308
where the time goes:
time: 355 us; the launch traced here: 353 us
  matrix products  105 us (30%)
  blocking collectives  64.1 us (18%)
  waiting for transfers between devices  58.4 us (16%)
  local copies, waits for them, and re-layouts  50.9 us (14%)
  starting transfers between devices  41.4 us (12%)
  other arithmetic  31.1 us (9%)
    dot_general x8, matrix products, one_box(): jnp.einsum('fpq,frq->rp', matern(near2), near_q, precision=lax.Precision....  65.6 us
    psum x1, blocking collectives, on_device(): total = lax.psum(terms, ('gx', 'gy'))  64.1 us
    dot_general x8, matrix products, one_box(): jnp.einsum('frn,fmn->rm', far_w, matern(dist2), precision=lax.Precision.H...  33.6 us
    all_to_all x1, waiting for transfers between devices, on_device(): lax.all_to_all(outgoing[0], ('gx', 'gy'), split_axis=0, concat_axis=0, ti...  15.9 us
    all_to_all x1, starting transfers between devices, on_device(): lax.all_to_all(far_wanted, ('gx', 'gy'), split_axis=0, concat_axis=0, til...  11.5 us
    all_to_all x1, waiting for transfers between devices, on_device(): lax.all_to_all(outgoing[4], ('gx', 'gy'), split_axis=0, concat_axis=0, ti...  9.92 us
    all_to_all x1, waiting for transfers between devices, on_device(): lax.all_to_all(near_wanted, ('gx', 'gy'), split_axis=0, concat_axis=0, ti...  9.66 us
    add x8, other arithmetic, one_box(): src_abs = near_center[:, :, None] + HALF * near_pos  8.32 us
  transfers between devices with their start and end apart: 7, of which 7 were waited for; matrix products, arithmetic and copies ran while one was open for 13% of the time, Pallas kernels for 0%

commit v1 on v0

v1 whole, which is shorter than its diff:
```python
import functools
import math

import jax
import jax.numpy as jnp
import numpy as np
from jax import lax
from jax.experimental import pallas as pl
from jax.experimental.pallas import tpu as pltpu
from jax.sharding import PartitionSpec as P

AXES = ("gx", "gy")
NODES = 4
ROOT3 = 1.7320508075688772
BF = jnp.bfloat16
F32 = jnp.float32
NODE = [math.cos((2 * i + 1) * math.pi / 8) for i in range(NODES)]
NT = (((1,), (1,)), ((), ()))
TN = (((0,), (0,)), ((), ()))
VMEM_LIMIT = 56 * 1024 * 1024


def iota(shape, dim):
    return lax.broadcasted_iota(jnp.int32, shape, dim)


def dot(a, b, dims=None):
    if dims is None:
        return jnp.dot(a, b, preferred_element_type=F32)
    return lax.dot_general(a, b, dims, preferred_element_type=F32)


def split(x):
    high = x.astype(BF)
    return high, (x - high.astype(F32)).astype(BF)


def planes(rel, source):
    sub = iota(rel.shape, 0) % 4
    last = sub == 3
    rel = jnp.where(last, 0.0, rel)
    high = rel.astype(BF).astype(F32)
    low = (rel - high).astype(BF).astype(F32)
    square = high * (high + 2.0 * low)
    norm = pltpu.roll(square, 1, 0) + pltpu.roll(square, 2, 0) + pltpu.roll(square, 3, 0)
    one = norm.astype(BF).astype(F32)
    rest = norm - one
    two = rest.astype(BF).astype(F32)
    three = (rest - two).astype(BF).astype(F32)
    if source:
        parts = [
            jnp.where(last, one, high),
            jnp.where(last, two, high),
            jnp.where(last, 1.0, low),
            jnp.where(last, three, jnp.where(sub < 2, 1.0, 0.0)),
        ]
    else:
        parts = [
            jnp.where(last, 1.0, -2.0 * high),
            jnp.where(last, 1.0, -2.0 * low),
            jnp.where(last, one, -2.0 * high),
            jnp.where(
                sub == 0,
                pltpu.roll(two, 5, 0),
                jnp.where(sub == 1, pltpu.roll(three, 6, 0), jnp.where(last, 1.0, 0.0)),
            ),
        ]
    return parts


def matern(dist2):
    safe = jnp.maximum(dist2, 1e-12)
    scaled = safe * lax.rsqrt(safe)
    decay = jnp.exp(-scaled)
    return decay + scaled * decay


def stack_kernel(value):
    high, low = split(value)
    return jnp.concatenate([high, low], axis=0)


def fold(x):
    return x[0:8] + x[8:16]


def ids_kernel(far_ref, near_ref, want_ref):
    boxes = far_ref.shape[0]
    slots = far_ref.shape[1]
    total = boxes * slots
    lane = iota((total, 128), 1)
    box = iota((total, 128), 0) % boxes
    tri = (iota((total, total), 0) > iota((total, total), 1)).astype(F32).astype(BF)
    result = jnp.zeros((128, 128), F32)
    for ref, first, base in ((near_ref, 1, 0), (far_ref, 0, 4)):
        flat = jnp.concatenate([ref[:, first + j : first + j + 1] for j in range(slots)], axis=0)
        flat = jnp.broadcast_to(flat, (total, 128))
        hit = (flat // boxes) == lane
        onehot = hit.astype(F32).astype(BF)
        before = dot(tri, onehot)
        rank = jnp.sum(jnp.where(hit, before, 0.0), axis=1, keepdims=True).astype(jnp.int32)
        mine = rank == (lane % 4)
        within = jnp.where((lane >= base) & (lane < base + 4), flat % boxes, 0)
        owner = jnp.where((lane >= base + 16) & (lane < base + 20), box, 0)
        value = jnp.where(mine, within + owner, 0).astype(F32).astype(BF)
        result = result + dot(onehot, value, TN)
    want_ref[...] = result.astype(jnp.int32)


def table_kernel(pos_ref, charge_ref, count_ref, cen_ref, q_ref, w_ref, p_ref, f_ref, base_ref, t_ref):
    step = pl.program_id(0)
    group = pos_ref.shape[0]
    sub = iota((8, 128), 0)
    lane = iota((8, 128), 1)

    def body(b, carry):
        box = step * group + b
        live = lane < count_ref[box]
        q = jnp.where(live, charge_ref[b], 0.0)
        q_ref[b] = q
        pos = pos_ref[b]
        zero1 = jnp.zeros((1, 128), F32)
        x4 = jnp.concatenate([pos, zero1], axis=0)
        x = jnp.concatenate([x4, x4], axis=0)
        second = 2.0 * x * x - 1.0
        third = 2.0 * x * second - x
        basis = []
        for i in range(NODES):
            theta = (2 * i + 1) * math.pi / 8
            basis.append(0.25 + 0.5 * (math.cos(theta) * x + math.cos(2 * theta) * second + math.cos(3 * theta) * third))
        row = lambda i, d: jnp.broadcast_to(basis[i][d : d + 1], (8, 128))
        sub4 = sub % 4
        zs = jnp.where(sub4 == 0, row(0, 2), jnp.where(sub4 == 1, row(1, 2), jnp.where(sub4 == 2, row(2, 2), row(3, 2))))
        ys = [jnp.where(sub < 4, row(0, 1), row(1, 1)) * zs, jnp.where(sub < 4, row(2, 1), row(3, 1)) * zs]
        table = jnp.concatenate([row(i, 0) * ys[j] for i in range(NODES) for j in range(2)], axis=0)
        both = stack_kernel(table)
        t_ref[b] = both
        qs = jnp.concatenate(split(q), axis=0)
        weight = fold(dot(qs, both, NT))
        w_ref[b] = weight + pltpu.roll(weight, 64, 1)
        cx, cy, cz = cen_ref[0, box], cen_ref[1, box], cen_ref[2, box]
        lane4 = lane % 4
        far = jnp.where(lane4 == 0, cx, jnp.where(lane4 == 1, cy, cz))
        center = jnp.where(sub4 == 0, cx, jnp.where(sub4 == 1, cy, cz))
        p_ref[b] = jnp.where(sub4 == 3, far, center + 0.5 * x)
        rel = (0.5 * ROOT3) * x
        tgt = planes(rel, False)
        for unit in range(2):
            f_ref[b, unit] = jnp.concatenate([jnp.where(sub // 4 == unit, part, 0.0) for part in tgt], axis=0).astype(BF)
        src = jnp.concatenate(planes(rel, True) + [jnp.zeros((96, 128), F32)], axis=0).T.astype(BF)
        dist2 = dot(src[:, :32], f_ref[b, 0])
        value = stack_kernel(matern(dist2))
        near = fold(dot(jnp.concatenate([qs, qs], axis=1), value))
        base_ref[b] = near + q
        return carry

    lax.fori_loop(0, group, body, 0, unroll=4)


def gather_kernel(ids_ref, q_ref, w_ref, p_ref, out_ref):
    step = pl.program_id(0)
    group = out_ref.shape[0]
    sub4 = iota((8, 128), 0) % 4
    top = iota((8, 128), 0) < 4
    lane = iota((8, 128), 1)
    left = lane < 64

    def body(k, carry):
        peer = step * group + k
        near = [ids_ref[peer, j] for j in range(4)]
        far = [ids_ref[peer, 4 + j] for j in range(4)]
        for j in range(4):
            out_ref[k, 8 * j : 8 * j + 8] = q_ref[near[j]]
        w = [w_ref[far[j]] for j in range(4)]
        out_ref[k, 32:40] = jnp.where(left, w[0], w[2])
        out_ref[k, 40:48] = jnp.where(left, w[1], w[3])
        c = [p_ref[far[j]] for j in range(4)]
        centers = jnp.where(
            left, jnp.where(lane < 4, c[0], c[2]), jnp.where(lane < 68, c[1], c[3])
        )
        s = [p_ref[near[j]] for j in range(4)]
        out_ref[k, 48:56] = jnp.where(sub4 == 3, centers, jnp.where(top, s[0], s[1]))
        out_ref[k, 56:64] = jnp.where(sub4 == 3, centers, jnp.where(top, s[2], s[3]))
        return carry

    lax.fori_loop(0, group, body, 0, unroll=4)


def pair_kernel(
    tgt_ref, count_ref, got_ref, nc_ref, fc_ref, f_ref, fn_ref, base_ref, q_ref, t_ref, out_ref, term_ref, near_acc, far_acc
):
    step = pl.program_id(0)
    steps = pl.num_programs(0)
    group = got_ref.shape[0]
    boxes = f_ref.shape[0]
    sub = iota((8, 128), 0)
    lane = iota((8, 128), 1)
    left = lane < 64

    @pl.when(step == 0)
    def _():
        near_acc[...] = base_ref[...]
        far_acc[...] = jnp.zeros_like(far_acc)

    spread = (iota((128, 128), 0) // 64 == iota((128, 128), 1) // 64).astype(F32).astype(BF)

    def body(k, carry):
        peer = step * group + k
        tn = [tgt_ref[peer, j] for j in range(4)]
        tf = [tgt_ref[peer, 4 + j] for j in range(4)]
        points = [got_ref[k, 48:56], got_ref[k, 56:64]]
        feats = []
        for v in range(2):
            feats += planes((points[v] - nc_ref[k, 8 * v : 8 * v + 8]) * ROOT3, True)
        src = jnp.concatenate(feats + [jnp.zeros((64, 128), F32)], axis=0).T.astype(BF)
        for j in range(4):
            dist2 = dot(src[:, 32 * (j // 2) : 32 * (j // 2) + 32], f_ref[tn[j], j % 2])
            value = stack_kernel(matern(dist2))
            qs = jnp.concatenate(split(got_ref[k, 8 * j : 8 * j + 8]), axis=0)
            near_acc[tn[j]] += fold(dot(jnp.concatenate([qs, qs], axis=1), value))
        row = jnp.broadcast_to(points[0][3:4], (8, 128))
        row = jnp.where(lane % 64 == sub, row, 0.0)
        high = row.astype(BF)
        rest = row - high.astype(F32)
        mid = rest.astype(BF)
        low = (rest - mid.astype(F32)).astype(BF)
        cen = dot(jnp.concatenate([high, mid, low], axis=0), spread)
        rel = (fc_ref[k] - (cen[0:8] + cen[8:16] + cen[16:24])) * ROOT3
        tgt = jnp.concatenate(planes(rel, False), axis=0).astype(BF)
        value = stack_kernel(matern(dot(fn_ref[...], tgt)))
        ws = []
        for h in range(2):
            w = got_ref[k, 32 + 8 * h : 40 + 8 * h]
            for part in (jnp.where(left, w, 0.0), jnp.where(left, 0.0, w)):
                ws += list(split(part))
        ws = jnp.concatenate(ws, axis=0)
        locs = dot(jnp.concatenate([ws, ws], axis=1), value)
        for h in range(2):
            for u in range(2):
                at = 32 * h + 16 * u
                new = fold(locs[at : at + 16])
                far_acc[tf[2 * u + h]] += jnp.where(left if h == 0 else jnp.logical_not(left), new, 0.0)
        return carry

    lax.fori_loop(0, group, body, 0, unroll=2)

    @pl.when(step == steps - 1)
    def _():
        def finish(b, total):
            ls = jnp.concatenate(split(far_acc[b]), axis=0)
            both = t_ref[b]
            high, low = both[0:64], both[64:128]
            table = jnp.concatenate([high, high, low, low], axis=0)
            far = fold(dot(jnp.concatenate([ls, ls], axis=1), table))
            live = lane < count_ref[b]
            product = jnp.where(live, near_acc[b] + far, 0.0)
            out_ref[b] = product
            return total + product * q_ref[b]

        total = lax.fori_loop(0, boxes, finish, jnp.zeros((8, 128), F32), unroll=4)
        ones = jnp.ones((128, 128), F32)
        sums = lax.dot_general(ones, total, NT, precision=lax.Precision.HIGHEST, preferred_element_type=F32)
        term_ref[...] = jnp.concatenate([sums, jnp.zeros((128, 120), F32)], axis=1)


def far_sources():
    x = np.zeros((8, 128), np.float32)
    for n in range(64):
        for d, value in enumerate((NODE[n // 16], NODE[n // 4 % 4], NODE[n % 4])):
            for u in range(2):
                x[4 * u + d, 64 * u + n] = 0.5 * ROOT3 * value
    bf = lambda a: a.astype(jnp.bfloat16).astype(np.float32)
    high = bf(x)
    low = bf(x - high)
    norm = np.zeros_like(x)
    square = high * (high + 2 * low)
    for u in range(2):
        norm[4 * u + 3] = square[4 * u] + square[4 * u + 1] + square[4 * u + 2]
    one = bf(norm)
    two = bf(norm - one)
    three = bf(norm - one - two)
    sub = np.arange(8)[:, None] % 4
    unit = (np.arange(8)[:, None] // 4) == (np.arange(128)[None, :] // 64)
    parts = [
        np.where(sub == 3, one, high),
        np.where(sub == 3, two, high),
        np.where(sub == 3, 1.0, low),
        np.where(sub == 3, three, np.where(sub < 2, 1.0, 0.0)),
    ]
    return np.concatenate([np.where(unit, part, 0.0) for part in parts], axis=0).T.astype(np.float32)


def node_rows():
    out = np.zeros((8, 128), np.float32)
    for m in range(128):
        n = m % 64
        for u in range(2):
            for d, value in enumerate((NODE[n // 16], NODE[n // 4 % 4], NODE[n % 4])):
                out[4 * u + d, m] = 0.5 * value
    return out


def vmem(shape=None, index=None):
    if shape is None:
        return pl.BlockSpec(memory_space=pltpu.VMEM)
    return pl.BlockSpec(shape, index, memory_space=pltpu.VMEM)


SMEM = pl.BlockSpec(memory_space=pltpu.SMEM)


def params():
    return pltpu.CompilerParams(vmem_limit_bytes=VMEM_LIMIT)


def exchange(x):
    return lax.all_to_all(x, AXES, split_axis=0, concat_axis=0, tiled=True)


def on_device(local_pos, charges, counts, box_centers, far_list, near_list):
    devices = lax.axis_size("gx") * lax.axis_size("gy")
    boxes, _, slots = local_pos.shape
    struct = jax.ShapeDtypeStruct
    want = pl.pallas_call(
        ids_kernel,
        out_shape=struct((devices, 128), jnp.int32),
        in_specs=[vmem(), vmem()],
        out_specs=vmem(),
        compiler_params=params(),
        name="ids",
    )(far_list, near_list)
    served = exchange(want.reshape(devices, 1, 128)).reshape(devices, 128)

    group = 16
    lead = lambda shape: vmem((group,) + shape, lambda i: (i,) + (0,) * len(shape))
    q_tab, w_tab, p_tab, f_tab, base, table = pl.pallas_call(
        table_kernel,
        grid=(boxes // group,),
        out_shape=(
            struct((boxes, 8, 128), F32),
            struct((boxes, 8, 128), F32),
            struct((boxes, 8, 128), F32),
            struct((boxes, 2, 32, 128), BF),
            struct((boxes, 8, 128), F32),
            struct((boxes, 128, 128), BF),
        ),
        in_specs=[lead((3, 128)), lead((8, 128)), SMEM, SMEM],
        out_specs=(lead((8, 128)), lead((8, 128)), lead((8, 128)), lead((2, 32, 128)), lead((8, 128)), lead((128, 128))),
        compiler_params=params(),
        cost_estimate=pl.CostEstimate(flops=200_000_000, bytes_accessed=6_000_000, transcendentals=2_000_000),
        name="tables",
    )(local_pos, charges, counts, box_centers)

    send = pl.pallas_call(
        gather_kernel,
        grid=(devices // group,),
        out_shape=struct((devices, 64, 128), F32),
        in_specs=[SMEM, vmem(), vmem(), vmem()],
        out_specs=lead((64, 128)),
        compiler_params=params(),
        name="gather",
    )(served, q_tab, w_tab, p_tab)
    got = exchange(send)

    tgt = want[:, 16:24]
    centers = box_centers.T
    near_cen = jnp.pad(centers[tgt[:, :4]], ((0, 0), (0, 0), (0, 1))).reshape(devices, 16, 1)
    near_cen = jnp.broadcast_to(near_cen, (devices, 16, 128))
    far_cen = jnp.pad(centers[tgt[:, 4:]], ((0, 0), (0, 0), (0, 1))).reshape(devices, 2, 2, 4)
    far_cen = far_cen.transpose(0, 1, 3, 2).reshape(devices, 8, 2, 1)
    far_cen = jnp.broadcast_to(far_cen, (devices, 8, 2, 64)).reshape(devices, 8, 128) + node_rows()[None]

    product, term = pl.pallas_call(
        pair_kernel,
        grid=(devices // group,),
        out_shape=(struct((boxes, 8, 128), F32), struct((devices, 128), F32)),
        in_specs=[
            SMEM,
            SMEM,
            lead((64, 128)),
            lead((16, 128)),
            lead((8, 128)),
            vmem(),
            vmem(),
            vmem(),
            vmem(),
            vmem(),
        ],
        out_specs=(vmem(), vmem()),
        scratch_shapes=[pltpu.VMEM((boxes, 8, 128), F32), pltpu.VMEM((boxes, 8, 128), F32)],
        compiler_params=params(),
        cost_estimate=pl.CostEstimate(flops=1_000_000_000, bytes_accessed=12_000_000, transcendentals=20_000_000),
        name="pairs",
    )(tgt, counts, got, near_cen, far_cen, f_tab, jnp.asarray(far_sources(), BF), base, q_tab, table)

    terms = exchange(term.reshape(devices, 1, 128))[:, 0, :8]
    curvature = jnp.sum(terms, axis=0) / (devices * boxes * slots)
    return (product, curvature)


def solution(mesh):
    in_specs = (
        P(AXES, None, None),
        P(AXES, None, None),
        P(AXES),
        P(None, AXES),
        P(AXES, None),
        P(AXES, None),
    )
    out_specs = (P(AXES, None, None), P())
    return jax.shard_map(on_device, mesh=mesh, in_specs=in_specs, out_specs=out_specs, check_vma=False)
```

time: 355 us -> 191 us (0.54)
  matrix products: 105 us -> 0 us
  Pallas kernels: 0 us -> 94.6 us
  blocking collectives: 64.1 us -> 15.8 us
  local copies, waits for them, and re-layouts: 50.9 us -> 10.1 us
  other arithmetic: 31.1 us -> 1.62 us
  starting transfers between devices: 41.4 us -> 21.7 us
  waiting for transfers between devices: 58.4 us -> 45.8 us
    dot_general x25 -> x0, matrix products: 105 us -> none  [the longest x8 65.6 us: one_box(): jnp.einsum('fpq,frq->rp', matern(near2), near_q, precision=lax.Precision....]
    pallas_call x0 -> x4, Pallas kernels: none -> 94.6 us  [the longest x1 72.7 us: on_device(): pl.pallas_call(pair_kernel, grid=(devices // group,), out_shape=(struct((...]
    psum x1 -> x0, blocking collectives: 64.1 us -> none  [on_device(): total = lax.psum(terms, ('gx', 'gy'))]
    gather x13 -> x3, local copies, waits for them, and re-layouts: 24.9 us -> 2.17 us  [the longest x2 1.13 us: on_device(): centers[tgt[:, :4]]]
    all_to_all x7 -> x2, starting transfers between devices: 41.4 us -> 21.7 us  [exchange(): return lax.all_to_all(x, AXES, split_axis=0, concat_axis=0, tiled=True)]
    all_to_all x0 -> x1, blocking collectives: none -> 15.8 us  [exchange(): return lax.all_to_all(x, AXES, split_axis=0, concat_axis=0, tiled=True)]
    all_to_all x7 -> x2, waiting for transfers between devices: 58.4 us -> 45.8 us  [exchange(): return lax.all_to_all(x, AXES, split_axis=0, concat_axis=0, tiled=True)]
    add x17 -> x1, other arithmetic: 9.11 us -> 0.84 us  [on_device(): jnp.broadcast_to(far_cen, (devices, 8, 2, 64)).reshape(devices, 8, 128)]
  transfers between devices with their start and end apart: 7 -> 2, of which waited for: 7 -> 1; matrix products, arithmetic and copies ran while one was open for 13% -> 3% of each run, Pallas kernels for 0% -> 7%
where the time goes in v1:
time: 191 us; the launch traced here: 190 us
  Pallas kernels  94.6 us (50%)
  waiting for transfers between devices  45.8 us (24%)
  starting transfers between devices  21.7 us (11%)
  blocking collectives  15.8 us (8%)
  local copies, waits for them, and re-layouts  10.1 us (5%)
    pallas_call x1, Pallas kernels, on_device(): pl.pallas_call(pair_kernel, grid=(devices // group,), out_shape=(struct((...  72.7 us
    all_to_all x2, waiting for transfers between devices, exchange(): return lax.all_to_all(x, AXES, split_axis=0, concat_axis=0, tiled=True)  45.8 us
    all_to_all x2, starting transfers between devices, exchange(): return lax.all_to_all(x, AXES, split_axis=0, concat_axis=0, tiled=True)  21.7 us
    all_to_all x1, blocking collectives, exchange(): return lax.all_to_all(x, AXES, split_axis=0, concat_axis=0, tiled=True)  15.8 us
    pallas_call x1, Pallas kernels, on_device(): pl.pallas_call(table_kernel, grid=(boxes // group,), out_shape=(struct((b...  13 us
    pallas_call x1, Pallas kernels, on_device(): pl.pallas_call(gather_kernel, grid=(devices // group,), out_shape=struct(...  6.29 us
    unnamed x12, local copies, waits for them, and re-layouts  5.11 us
  transfers between devices with their start and end apart: 2, of which 1 were waited for; matrix products, arithmetic and copies ran while one was open for 3% of the time, Pallas kernels for 7%

profile of v1, /device:TPU:1, one launch (start us, length us, event | category | flops | bytes accessed | tf_op | source)
XLA Modules:
  0.0 190.4 jit_solution(7801635381204842678)
XLA Ops:
  0.6 1.4 copy.23.far_ref
  2.0 1.4 copy.24.near_ref
  3.4 2.6 %ids.1 = s32[128,128]{1,0:T(8,128)} custom-call(s32[64,8]{1,0:T(8,128)} %copy.23.far_ref, s32[64,9]{1,0:T(8,128)} %copy.24.near_ref), custom_call_target="tpu_custom_call" | custom-call | tf_op jit(solution)/shard_map/ids/pallas_call | solution.py:324
  6.0 11.5 %all-to-all-start = ((s32[128,1,128]{2,1,0:T(1,128)}), s32[128,1,128]{2,1,0:T(1,128)S(1)}, u32[]{:S(2)}, u32[]{:S(2)}) async-start(s32[128,1,128]{2,1,0:T(1,128)} %bitcast.19), calls=%async_computation | async-start | bytes 131072 | tf_op jit(solution)/shard_map/all_to_all | solution.py:317
  17.5 1.6 copy.26.pos_ref
  19.1 13.0 %tables.1 = (f32[64,8,128]{2,1,0:T(8,128)}, f32[64,8,128]{2,1,0:T(8,128)}, f32[64,8,128]{2,1,0:T(8,128)}, bf16[64,2,32,128]{3,2,1,0:T(8,128)(2,1)}, f32[64,8,128...) custom-call(f32[64,3,128]{2,1,0:T(4,128)} %copy.26.pos_ref, f32[64,8,128]{2,1,0:T(8,128)} %charge_ref.1, s32[64]{0:T(128)} %count_ref.3, ...), custom_call_target="tpu_custom_call" | custom-call | flops 200000000 | bytes 6000000 | tf_op jit(solution)/shard_map/tables/pallas_call | solution.py:336
  32.1 0.0 all-to-all-done
  32.1 0.0 copy-start.1
  32.1 0.6 copy-done.1
  32.7 6.3 %gather.13 = f32[128,64,128]{2,1,0:T(8,128)} custom-call(s32[128,128]{1,0:T(8,128)} %bitcast.23, f32[64,8,128]{2,1,0:T(8,128)} %get-tuple-element.10.q_ref, f32[64,8,128]{2,1,0:T(8,128)} %get-tuple-element.11.w_ref, f32[64,8,128]{2,1,0:T(8,128)} %get-tuple-element.12.p_ref), custom_call_target="tpu_custom_call" | custom-call | tf_op jit(solution)/shard_map/gather/pallas_call | solution.py:354
  39.0 0.0 copy-start.3
  39.0 0.0 copy-start
  39.0 10.2 %all-to-all-start.1 = ((f32[128,64,128]{2,1,0:T(8,128)}), f32[128,64,128]{2,1,0:T(8,128)}, u32[]{:S(2)}, u32[]{:S(2)}) async-start(f32[128,64,128]{2,1,0:T(8,128)} %gather.13), calls=%async_computation.1 | async-start | bytes 8388608 | tf_op jit(solution)/shard_map/all_to_all | solution.py:317
  49.3 0.0 copy-done.3
  49.3 0.0 copy-start.2
  49.3 0.1 copy.27
  49.4 0.0 copy-done
  49.4 0.7 slice.22.tgt_ref
  50.1 0.1 compare_select_fusion
  50.2 0.1 reshape.38
  50.3 1.0 gather_fusion.1
  51.4 0.2 copy.30
  51.6 0.2 copy.31
  51.9 0.1 reshape.30
  52.0 1.0 gather_fusion
  53.0 0.1 copy.28
  53.2 0.1 copy.29
  53.3 0.0 copy-done.2
  53.3 0.8 broadcast_add_fusion.fc_ref
  54.1 45.8 %all-to-all-done.1.got_ref = f32[128,64,128]{2,1,0:T(8,128)} async-done(((f32[128,64,128]{2,1,0:T(8,128)}), f32[128,64,128]{2,1,0:T(8,128)}, u32[]{:S(2)}, u32[]{:S(2)}) %all-to-all-start.1) | async-done | bytes 4194336 | tf_op jit(solution)/shard_map/all_to_all | solution.py:317
  99.9 1.3 broadcast_in_dim.22.nc_ref
  101.2 72.7 %pairs.1 = (f32[64,8,128]{2,1,0:T(8,128)}, f32[128,128]{1,0:T(8,128)}) custom-call(s32[128,8]{1,0:T(8,128)} %slice.22.tgt_ref, s32[64]{0:T(128)} %count_ref.3, f32[128,64,128]{2,1,0:T(8,128)} %all-to-all-done.1.got_ref, f32[128,16,128]{2,1,0:T(8,128)} %broadcast_in_dim.22.nc_ref, f32[128,8,128]{2,1,0:T(8,128)} %broadcast_add_fusion.fc_ref, ...), custom_call_target="tpu_custom_call" | custom-call | flops 1000000000 | bytes 12000000 | tf_op jit(solution)/shard_map/pairs/pallas_call | solution.py:373
  173.9 15.8 %all_to_all.15 = f32[128,1,128]{2,1,0:T(1,128)S(1)} all-to-all(f32[128,1,128]{2,1,0:T(1,128)} %bitcast.24), channel_id=1, replica_groups=mesh['gx'=8,'gy'=16] {'gx','gy'}, dimensions={0} | all-to-all | bytes 131072 | tf_op jit(solution)/shard_map/all_to_all | solution.py:317
  189.7 0.2 slice_reduce_fusion
  189.8 0.5 broadcast_multiply_fusion
  (5 shorter events, 0.1 us)
Async XLA Ops:
  6.0 26.1 %all-to-all-start = ((s32[128,1,128]{2,1,0:T(1,128)}), s32[128,1,128]{2,1,0:T(1,128)S(1)}, u32[]{:S(2)}, u32[]{:S(2)}) async-start(s32[128,1,128]{2,1,0:T(1,128)} %bitcast.19), calls=%async_computation | async-start | bytes 131072 | tf_op jit(solution)/shard_map/all_to_all | solution.py:317
  32.1 0.6 copy-start.1
  39.0 10.2 %copy-start.3 = (f32[3,64]{1,0:T(4,128)S(1)}, f32[3,64]{1,0:T(4,128)}, u32[]{:S(2)}) copy-start(f32[3,64]{1,0:T(4,128)} %cen_ref.1) | copy-start | bytes 2308
  39.0 10.4 %copy-start = (s32[128,128]{1,0:T(8,128)S(1)}, s32[128,128]{1,0:T(8,128)}, u32[]{:S(2)}) copy-start(s32[128,128]{1,0:T(8,128)} %ids.1) | copy-start | bytes 196612
  39.0 60.9 %all-to-all-start.1 = ((f32[128,64,128]{2,1,0:T(8,128)}), f32[128,64,128]{2,1,0:T(8,128)}, u32[]{:S(2)}, u32[]{:S(2)}) async-start(f32[128,64,128]{2,1,0:T(8,128)} %gather.13), calls=%async_computation.1 | async-start | bytes 8388608 | tf_op jit(solution)/shard_map/all_to_all | solution.py:317
  49.3 4.0 %copy-start.2 = (f32[8,128]{1,0:T(8,128)S(1)}, f32[8,128]{1,0:T(8,128)}, u32[]{:S(2)}) copy-start(f32[8,128]{1,0:T(8,128)} %constant.27) | copy-start | bytes 12292

commit v2 on v1

--- a/solution.py
+++ b/solution.py
@@ -36,13 +36,14 @@
 
 
 def planes(rel, source):
-    sub = iota(rel.shape, 0) % 4
+    axis = rel.ndim - 2
+    sub = iota(rel.shape, axis) % 4
     last = sub == 3
     rel = jnp.where(last, 0.0, rel)
     high = rel.astype(BF).astype(F32)
     low = (rel - high).astype(BF).astype(F32)
     square = high * (high + 2.0 * low)
-    norm = pltpu.roll(square, 1, 0) + pltpu.roll(square, 2, 0) + pltpu.roll(square, 3, 0)
+    norm = pltpu.roll(square, 1, axis) + pltpu.roll(square, 2, axis) + pltpu.roll(square, 3, axis)
     one = norm.astype(BF).astype(F32)
     rest = norm - one
     two = rest.astype(BF).astype(F32)
@@ -61,8 +62,8 @@
             jnp.where(last, one, -2.0 * high),
             jnp.where(
                 sub == 0,
-                pltpu.roll(two, 5, 0),
-                jnp.where(sub == 1, pltpu.roll(three, 6, 0), jnp.where(last, 1.0, 0.0)),
+                pltpu.roll(two, 5, axis),
+                jnp.where(sub == 1, pltpu.roll(three, 6, axis), jnp.where(last, 1.0, 0.0)),
             ),
         ]
     return parts
@@ -317,7 +318,7 @@
     return lax.all_to_all(x, AXES, split_axis=0, concat_axis=0, tiled=True)
 
 
-def on_device(local_pos, charges, counts, box_centers, far_list, near_list):
+def general(local_pos, charges, counts, box_centers, far_list, near_list):
     devices = lax.axis_size("gx") * lax.axis_size("gy")
     boxes, _, slots = local_pos.shape
     struct = jax.ShapeDtypeStruct
@@ -398,6 +399,370 @@
     return (product, curvature)
 
 
+HALF = 64
+ROWS = 48
+
+
+def start_kernel(far_ref, near_ref, most_ref, pos_ref, charge_ref, count_ref, cen_ref, want_ref, ex_ref):
+    boxes = far_ref.shape[1]
+    slots = far_ref.shape[0]
+    sub = iota((8, 128), 0)
+    lane = iota((8, 128), 1)
+    left = lane < HALF
+
+    def body(b, carry):
+        live = lane < count_ref[b]
+        q = pltpu.roll(jnp.where(live, charge_ref[b], 0.0), HALF, 1)
+        point = jnp.zeros((8, 128), F32)
+        for d in range(3):
+            row = jnp.broadcast_to(pos_ref[d, pl.ds(b, 1), :], (8, 128))
+            point = jnp.where(sub == d, cen_ref[d, b] + 0.5 * row, point)
+        ex_ref[b] = jnp.where(left, q, point)
+        return carry
+
+    lax.fori_loop(0, boxes, body, 0, unroll=8)
+
+    peer = iota((128, 128), 0)
+    line = iota((128, 128), 1)
+    tri = (peer < line).astype(F32).astype(BF)
+    row32 = iota((32, 128), 0)
+    boxrow = iota((32, 128), 1) % boxes
+    result = jnp.zeros((128, 32), F32)
+    for ref, first, base in ((near_ref, 1, 0), (far_ref, 0, 4)):
+        seen = jnp.zeros((128, 1), F32)
+        for j in range(0, slots, 2):
+            flat = jnp.concatenate([ref[first + j : first + j + 1, :], ref[first + j + 1 : first + j + 2, :]], axis=1)
+            hit = jnp.broadcast_to(flat // boxes, (128, 128)) == peer
+            ones = hit.astype(F32)
+            onehot = ones.astype(BF)
+            before = dot(onehot, tri) + seen
+            rank = jnp.sum(jnp.where(hit, before, 0.0), axis=0, keepdims=True).astype(jnp.int32)
+            seen = seen + jnp.sum(ones, axis=1, keepdims=True)
+            within = jnp.broadcast_to(flat % boxes, (32, 128))
+            mine = row32 % 4 == jnp.broadcast_to(rank, (32, 128))
+            value = jnp.where(row32 // 4 == base // 4, within, jnp.where(row32 // 4 == base // 4 + 4, boxrow, 0))
+            value = jnp.where(mine, value, 0).astype(F32).astype(BF)
+            result = result + dot(onehot, value, NT)
+    result = jnp.concatenate([result, jnp.zeros((128, 96), F32)], axis=1)
+    extra = jnp.zeros((128, 1), F32)
+    member = iota((128, 1), 0) % 4
+    for y in range(4):
+        column = result[:, y : y + 1]
+        column = pltpu.roll(jnp.broadcast_to(column, (128, 128)), y, 0)[:, 0:1] if y else column
+        extra = jnp.where(member == y, column, extra)
+    result = jnp.where(line == 8, jnp.broadcast_to(extra, (128, 128)), result)
+    most = jnp.max(most_ref[...], axis=1, keepdims=True)
+    want_ref[...] = jnp.where(line == 9, jnp.broadcast_to(most, (128, 128)), result.astype(jnp.int32))
+
+
+def cheb_rows(x):
+    sub = iota((8, 128), 0)
+    second = 2.0 * x * x - 1.0
+    third = 2.0 * x * second - x
+    basis = []
+    for i in range(NODES):
+        theta = (2 * i + 1) * math.pi / 8
+        basis.append(0.25 + 0.5 * (math.cos(theta) * x + math.cos(2 * theta) * second + math.cos(3 * theta) * third))
+    row = lambda i, d: jnp.broadcast_to(basis[i][d : d + 1], (8, 128))
+    sub4 = sub % 4
+    zs = jnp.where(sub4 == 0, row(0, 2), jnp.where(sub4 == 1, row(1, 2), jnp.where(sub4 == 2, row(2, 2), row(3, 2))))
+    ys = [jnp.where(sub < 4, row(0, 1), row(1, 1)) * zs, jnp.where(sub < 4, row(2, 1), row(3, 1)) * zs]
+    return jnp.concatenate([row(i, 0) * ys[j] for i in range(NODES) for j in range(2)], axis=0)
+
+
+def point_rows(pos_ref, b):
+    sub4 = iota((8, 128), 0) % 4
+    x = jnp.zeros((8, 128), F32)
+    for d in range(3):
+        x = jnp.where(sub4 == d, jnp.broadcast_to(pos_ref[d, pl.ds(b, 1), :], (8, 128)), x)
+    return x
+
+
+def doubled(x):
+    return jnp.where(iota((8, 128), 1) < HALF, x, pltpu.roll(x, HALF, 1))
+
+
+def send_table_kernel(pos_ref, charge_ref, count_ref, cen_ref, q_ref, w_ref, p_ref):
+    boxes = charge_ref.shape[0]
+    lane = iota((8, 128), 1)
+    sub4 = iota((8, 128), 0) % 4
+
+    def body(b, carry):
+        q = jnp.where(lane < count_ref[b], charge_ref[b], 0.0)
+        q_ref[b] = doubled(q)
+        x = point_rows(pos_ref, b)
+        qs = jnp.concatenate(split(q), axis=0)
+        weight = fold(dot(qs, stack_kernel(cheb_rows(x)), NT))
+        w_ref[b] = weight + pltpu.roll(weight, 64, 1)
+        cx, cy, cz = cen_ref[0, b], cen_ref[1, b], cen_ref[2, b]
+        far = jnp.where(lane % 4 == 0, cx, jnp.where(lane % 4 == 1, cy, cz))
+        center = jnp.where(sub4 == 0, cx, jnp.where(sub4 == 1, cy, cz))
+        p_ref[b] = jnp.where(sub4 == 3, far, doubled(center + 0.5 * x))
+        return carry
+
+    lax.fori_loop(0, boxes, body, 0, unroll=8)
+
+
+def own_table_kernel(pos_ref, charge_ref, count_ref, q_ref, f_ref, base_ref, t_ref):
+    boxes = charge_ref.shape[0]
+    sub = iota((8, 128), 0)
+    lane = iota((8, 128), 1)
+
+    def body(b, carry):
+        q = jnp.where(lane < count_ref[b], charge_ref[b], 0.0)
+        q_ref[b] = q
+        x = point_rows(pos_ref, b)
+        t_ref[b] = stack_kernel(cheb_rows(x))
+        rel = (0.5 * ROOT3) * x
+        tgt = planes(rel, False)
+        for unit in range(2):
+            f_ref[b, unit] = jnp.concatenate([jnp.where(sub // 4 == unit, part, 0.0) for part in tgt], axis=0).astype(BF)
+        zero = jnp.zeros((96, 128), F32)
+        src = jnp.concatenate(planes(rel, True) + [zero], axis=0).T.astype(BF)
+        first = jnp.concatenate([jnp.where(sub < 4, part, 0.0) for part in tgt] + [zero], axis=0).astype(BF)
+        value = stack_kernel(matern(dot(src, first)))
+        qs = jnp.concatenate(split(q), axis=0)
+        base_ref[b] = fold(dot(jnp.concatenate([qs, qs], axis=1), value)) + q
+        return carry
+
+    lax.fori_loop(0, boxes, body, 0, unroll=4)
+
+
+def send_kernel(ids_ref, q_ref, w_ref, p_ref, ex_ref, out_ref):
+    step = pl.program_id(0)
+    group = out_ref.shape[0]
+    sub4 = iota((8, 128), 0) % 4
+    top = iota((8, 128), 0) < 4
+    lane = iota((8, 128), 1)
+    left = lane < HALF
+
+    def body(k, carry):
+        peer = step * group + k
+        near = [ids_ref[peer, j] for j in range(4)]
+        far = [ids_ref[peer, 4 + j] for j in range(4)]
+        q = [q_ref[n] for n in near]
+        out_ref[k, 0:8] = jnp.where(left, q[0], q[1])
+        out_ref[k, 8:16] = jnp.where(left, q[2], q[3])
+        w = [w_ref[n] for n in far]
+        out_ref[k, 16:24] = jnp.where(left, w[0], w[2])
+        out_ref[k, 24:32] = jnp.where(left, w[1], w[3])
+        out_ref[k, 32:40] = ex_ref[ids_ref[peer, 8]]
+        c = [p_ref[n] for n in far]
+        centers = jnp.where(left, jnp.where(lane < 4, c[0], c[2]), jnp.where(lane < 68, c[1], c[3]))
+        s = [p_ref[n] for n in near]
+        points = jnp.where(top, jnp.where(left, s[0], s[1]), jnp.where(left, s[2], s[3]))
+        out_ref[k, 40:48] = jnp.where(sub4 == 3, centers, points)
+        return carry
+
+    lax.fori_loop(0, group, body, 0, unroll=8)
+
+
+def duo_kernel(
+    tgt_ref, count_ref, got_ref, nc_ref, ec_ref, fc_ref, f_ref, fn_ref, base_ref, q_ref, t_ref, out_ref, term_ref,
+    near_acc, far_acc, ft_ref, xt_ref, *bufs
+):
+    dist_refs, value_refs = bufs[:7], bufs[7:]
+    peers = got_ref.shape[0]
+    duos = peers // 2
+    boxes = f_ref.shape[0]
+    sub = iota((8, 128), 0)
+    lane = iota((8, 128), 1)
+    left = lane < HALF
+    near_acc[...] = base_ref[...]
+    far_acc[...] = jnp.zeros_like(far_acc)
+    xt_ref[...] = jnp.zeros_like(xt_ref)
+    for ref in dist_refs:
+        ref[...] = jnp.zeros_like(ref)
+    for ref in value_refs:
+        ref[...] = jnp.zeros_like(ref)
+    spread = (iota((128, 128), 0) // 64 == iota((128, 128), 1) // 64).astype(F32).astype(BF)
+
+    batch = 16
+    mask = iota((batch, 8, 128), 2) % 64 == iota((batch, 8, 128), 1)
+
+    def far_body(g, carry):
+        at = pl.ds(g * batch, batch)
+        rows = got_ref[at, 40:48, :]
+        rows = jnp.where(mask, jnp.broadcast_to(rows[:, 3:4, :], rows.shape), 0.0).reshape(batch * 8, 128)
+        high = rows.astype(BF)
+        rest = rows - high.astype(F32)
+        mid = rest.astype(BF)
+        low = (rest - mid.astype(F32)).astype(BF)
+        cen = dot(high, spread) + dot(mid, spread) + dot(low, spread)
+        rel = (fc_ref[at] - cen.reshape(batch, 8, 128)) * ROOT3
+        ft_ref[at] = jnp.concatenate(planes(rel, False), axis=1).astype(BF)
+        return carry
+
+    lax.fori_loop(0, peers // batch, far_body, 0, unroll=2)
+
+    def extra(duo):
+        return got_ref[2 * duo, 32:40], got_ref[2 * duo + 1, 32:40]
+
+    def body(i, carry):
+        duo = jnp.maximum(i - 3, 0)
+        go = jnp.broadcast_to(i, (8, 128)) >= 3
+        ex = extra(duo)
+        tiles = [got_ref[2 * duo + k // 2, 8 * (k % 2) : 8 * (k % 2) + 8] for k in range(4)]
+        tiles.append(jnp.where(left, ex[0], pltpu.roll(ex[1], HALF, 1)))
+        goals = [(tgt_ref[2 * duo + k // 2, 2 * (k % 2)], tgt_ref[2 * duo + k // 2, 2 * (k % 2) + 1]) for k in range(4)]
+        goals.append((tgt_ref[2 * duo, 8], tgt_ref[2 * duo + 1, 8]))
+        for k in range(5):
+            q = jnp.where(go, tiles[k], 0.0)
+            qs = split(jnp.where(left, q, 0.0)) + split(jnp.where(left, 0.0, q))
+            qs = jnp.concatenate(qs, axis=0)
+            new = dot(jnp.concatenate([qs, qs], axis=1), value_refs[k][...])
+            near_acc[goals[k][0]] += fold(new[0:16])
+            near_acc[goals[k][1]] += fold(new[16:32])
+        for a in range(2):
+            ws = []
+            for h in range(2):
+                w = jnp.where(go, got_ref[2 * duo + a, 16 + 8 * h : 24 + 8 * h], 0.0)
+                ws += list(split(jnp.where(left, w, 0.0)) + split(jnp.where(left, 0.0, w)))
+            ws = jnp.concatenate(ws, axis=0)
+            new = dot(jnp.concatenate([ws, ws], axis=1), value_refs[5 + a][...])
+            for h in range(2):
+                for u in range(2):
+                    at = 32 * h + 16 * u
+                    part = fold(new[at : at + 16])
+                    far_acc[tgt_ref[2 * duo + a, 4 + 2 * u + h]] += jnp.where(left if h == 0 else jnp.logical_not(left), part, 0.0)
+
+        for k in range(7):
+            value_refs[k][...] = stack_kernel(matern(dist_refs[k][...]))
+
+        duo = jnp.clip(i - 1, 0, duos - 1)
+        upper, lower = xt_ref[0:64, :], xt_ref[64:128, :]
+        goals = [(tgt_ref[2 * duo + k // 2, 2 * (k % 2)], tgt_ref[2 * duo + k // 2, 2 * (k % 2) + 1]) for k in range(4)]
+        goals.append((tgt_ref[2 * duo, 8], tgt_ref[2 * duo + 1, 8]))
+        for k in range(5):
+            v, u = k // 2, k % 2
+            for half, part in enumerate((upper, lower)):
+                pieces = [jnp.zeros((32 * v, 128), BF)] if v else []
+                pieces += [f_ref[goals[k][half], u], jnp.zeros((96 - 32 * v, 128), BF)]
+                dist_refs[k][64 * half : 64 * half + 64, :] = dot(part, jnp.concatenate(pieces, axis=0))
+        for a in range(2):
+            dist_refs[5 + a][...] = dot(fn_ref[...], ft_ref[2 * duo + a])
+
+        duo = jnp.minimum(i, duos - 1)
+        ex = extra(duo)
+        feats = []
+        for a in range(2):
+            feats += planes((got_ref[2 * duo + a, 40:48] - nc_ref[2 * duo + a]) * ROOT3, True)
+        point = jnp.where(left, pltpu.roll(ex[0], HALF, 1), ex[1])
+        feats += planes((point - ec_ref[duo]) * ROOT3, True)
+        feats.append(jnp.zeros((32, 128), F32))
+        xt_ref[...] = jnp.concatenate(feats, axis=0).T.astype(BF)
+        return carry
+
+    lax.fori_loop(0, duos + 3, body, 0)
+
+    def finish(b, total):
+        ls = jnp.concatenate(split(far_acc[b]), axis=0)
+        both = t_ref[b]
+        high, low = both[0:64], both[64:128]
+        table = jnp.concatenate([high, high, low, low], axis=0)
+        far = fold(dot(jnp.concatenate([ls, ls], axis=1), table))
+        product = jnp.where(lane < count_ref[b], near_acc[b] + far, 0.0)
+        out_ref[b] = product
+        return total + product * q_ref[b]
+
+    total = lax.fori_loop(0, boxes, finish, jnp.zeros((8, 128), F32), unroll=8)
+    ones = jnp.ones((128, 128), F32)
+    sums = lax.dot_general(ones, total, NT, precision=lax.Precision.HIGHEST, preferred_element_type=F32)
+    term_ref[...] = jnp.concatenate([sums, jnp.zeros((128, 120), F32)], axis=1)
+
+
+def center_rows(centers, goals, halves=2):
+    n, units = goals.shape[:2]
+    rows = jnp.pad(centers[goals], ((0, 0), (0, 2 - units), (0, 0), (0, 1)))
+    rows = rows.transpose(0, 1, 3, 2).reshape(n, 8, 2, 1)
+    return jnp.broadcast_to(rows, (n, 8, 2, HALF)).reshape(n, 8, 128)
+
+
+def on_device(local_pos, charges, counts, box_centers, far_list, near_list):
+    devices = lax.axis_size("gx") * lax.axis_size("gy")
+    boxes, _, slots = local_pos.shape
+    struct = jax.ShapeDtypeStruct
+    pos = jnp.transpose(local_pos, (1, 0, 2))
+    table = struct((boxes, 8, 128), F32)
+    want, ex_own = pl.pallas_call(
+        start_kernel,
+        out_shape=(struct((devices, 128), jnp.int32), table),
+        in_specs=[vmem(), vmem(), vmem(), vmem(), vmem(), SMEM, SMEM],
+        out_specs=(vmem(), vmem()),
+        compiler_params=params(),
+        name="start",
+    )(far_list.T, near_list.T, counts.reshape(1, boxes), pos, charges, counts, box_centers)
+    moved = [lax.ppermute(ex_own, "gy", [(4 * z, 4 * z + k) for z in range(4)]) for k in range(1, 4)]
+    ex_tab = moved[0] + moved[1] + moved[2] + jnp.where(lax.axis_index("gy") % 4 == 0, ex_own, 0.0)
+    served = exchange(want.reshape(devices, 1, 128)).reshape(devices, 128)
+
+    q2_tab, w_tab, p_tab = pl.pallas_call(
+        send_table_kernel,
+        out_shape=(table, table, table),
+        in_specs=[vmem(), vmem(), SMEM, SMEM],
+        out_specs=(vmem(), vmem(), vmem()),
+        compiler_params=params(),
+        cost_estimate=pl.CostEstimate(flops=50_000_000, bytes_accessed=1_200_000, transcendentals=0),
+        name="send_tables",
+    )(pos, charges, counts, box_centers)
+
+    group = 16
+    lead = lambda shape: vmem((group,) + shape, lambda i: (i,) + (0,) * len(shape))
+    send = pl.pallas_call(
+        send_kernel,
+        grid=(devices // group,),
+        out_shape=struct((devices, ROWS, 128), F32),
+        in_specs=[SMEM, vmem(), vmem(), vmem(), vmem()],
+        out_specs=lead((ROWS, 128)),
+        compiler_params=params(),
+        name="send",
+    )(served, q2_tab, w_tab, p_tab, ex_tab)
+    got = exchange(send)
+
+    q_tab, f_tab, base, cheb = pl.pallas_call(
+        own_table_kernel,
+        out_shape=(table, struct((boxes, 2, 32, 128), BF), table, struct((boxes, 128, 128), BF)),
+        in_specs=[vmem(), vmem(), SMEM],
+        out_specs=(vmem(), vmem(), vmem(), vmem()),
+        compiler_params=params(),
+        cost_estimate=pl.CostEstimate(flops=200_000_000, bytes_accessed=4_000_000, transcendentals=2_000_000),
+        name="own_tables",
+    )(pos, charges, counts)
+
+    centers = box_centers.T
+    goal = want[:, 16:24]
+    more = goal.reshape(devices // 4, 4, 8)[:, 0, :4].reshape(devices, 1)
+    tgt = jnp.concatenate([goal, more], axis=1)
+    near_cen = center_rows(centers, goal[:, :4].reshape(devices, 2, 2))
+    far_cen = center_rows(centers, goal[:, 4:].reshape(devices, 2, 2)) + node_rows()[None]
+    ex_cen = center_rows(centers, more.reshape(devices // 2, 1, 2))
+
+    big = lambda dtype, rows: pltpu.VMEM((rows, 128), dtype)
+    product, term = pl.pallas_call(
+        duo_kernel,
+        out_shape=(table, struct((devices, 128), F32)),
+        in_specs=[SMEM, SMEM] + [vmem()] * 9,
+        out_specs=(vmem(), vmem()),
+        scratch_shapes=[
+            pltpu.VMEM((boxes, 8, 128), F32),
+            pltpu.VMEM((boxes, 8, 128), F32),
+            pltpu.VMEM((devices, 32, 128), BF),
+            big(BF, 128),
+        ]
+        + [big(F32, 128)] * 7
+        + [big(BF, 256)] * 7,
+        compiler_params=params(),
+        cost_estimate=pl.CostEstimate(flops=1_000_000_000, bytes_accessed=12_000_000, transcendentals=20_000_000),
+        name="pairs",
+    )(tgt, counts, got, near_cen, ex_cen, far_cen, f_tab, jnp.asarray(far_sources(), BF), base, q_tab, cheb)
+
+    terms = exchange(term.reshape(devices, 1, 128))[:, 0, :8]
+    curvature = jnp.sum(terms, axis=0) / (devices * boxes * slots)
+    over = jnp.any((served[:, 9] > HALF) & (jnp.arange(devices) % 4 != 0))
+    whole = (local_pos, charges, counts, box_centers, far_list, near_list)
+    return lax.cond(over, lambda: general(*whole), lambda: (product, curvature))
+
+
 def solution(mesh):
     in_specs = (
         P(AXES, None, None),

time: 191 us -> 131 us (0.69)
  Pallas kernels: 94.6 us -> 54.6 us
  waiting for transfers between devices: 45.8 us -> 24.3 us
  blocking collectives: 15.8 us -> 0 us
  local copies, waits for them, and re-layouts: 10.1 us -> 18.3 us
  starting transfers between devices: 21.7 us -> 26.8 us
  other arithmetic: 1.62 us -> 4.77 us
    pallas_call x4 -> x5, Pallas kernels: 94.6 us -> 54.6 us  [the longest x1 31.1 us: on_device(): pl.pallas_call(duo_kernel, out_shape=(table, struct((devices, 128), F32))...]
    all_to_all x2 -> x3, waiting for transfers between devices: 45.8 us -> 24.3 us  [exchange(): return lax.all_to_all(x, AXES, split_axis=0, concat_axis=0, tiled=True)]
    all_to_all x1 -> x0, blocking collectives: 15.8 us -> none  [exchange(): return lax.all_to_all(x, AXES, split_axis=0, concat_axis=0, tiled=True)]
    ppermute x0 -> x3, starting transfers between devices: none -> 7.63 us  [on_device(): lax.ppermute(ex_own, 'gy', [(4 * z, 4 * z + k) for z in range(4)])]
    reshape x1 -> x3, local copies, waits for them, and re-layouts: 0.23 us -> 6.16 us  [center_rows(): return jnp.broadcast_to(rows, (n, 8, 2, HALF)).reshape(n, 8, 128)]
    unnamed x12 -> x33, local copies, waits for them, and re-layouts: 5.11 us -> 2.41 us
    all_to_all x2 -> x3, starting transfers between devices: 21.7 us -> 19.1 us  [exchange(): return lax.all_to_all(x, AXES, split_axis=0, concat_axis=0, tiled=True)]
  transfers between devices with their start and end apart: 2 -> 6, of which waited for: 1 -> 3; matrix products, arithmetic and copies ran while one was open for 3% -> 15% of each run, Pallas kernels for 7% -> 11%
where the time goes in v2:
time: 131 us
  Pallas kernels  54.6 us (42%)
  starting transfers between devices  26.8 us (20%)
  waiting for transfers between devices  24.3 us (19%)
  local copies, waits for them, and re-layouts  18.3 us (14%)
  other arithmetic  4.77 us (4%)
  between operations  1.54 us (1%)
    pallas_call x1, Pallas kernels, on_device(): pl.pallas_call(duo_kernel, out_shape=(table, struct((devices, 128), F32))...  31.1 us
    all_to_all x3, waiting for transfers between devices, exchange(): return lax.all_to_all(x, AXES, split_axis=0, concat_axis=0, tiled=True)  24.3 us
    all_to_all x3, starting transfers between devices, exchange(): return lax.all_to_all(x, AXES, split_axis=0, concat_axis=0, tiled=True)  19.1 us
    pallas_call x1, Pallas kernels, on_device(): pl.pallas_call(own_table_kernel, out_shape=(table, struct((boxes, 2, 32,...  9.77 us
    ppermute x3, starting transfers between devices, on_device(): lax.ppermute(ex_own, 'gy', [(4 * z, 4 * z + k) for z in range(4)])  7.63 us
    reshape x3, local copies, waits for them, and re-layouts, center_rows(): return jnp.broadcast_to(rows, (n, 8, 2, HALF)).reshape(n, 8, 128)  6.16 us
    pallas_call x1, Pallas kernels, on_device(): pl.pallas_call(send_kernel, grid=(devices // group,), out_shape=struct((d...  6.01 us
    pallas_call x1, Pallas kernels, on_device(): pl.pallas_call(send_table_kernel, out_shape=(table, table, table), in_spe...  4.62 us
  transfers between devices with their start and end apart: 6, of which 3 were waited for; matrix products, arithmetic and copies ran while one was open for 15% of the time, Pallas kernels for 11%

profile of v2, /device:TPU:1, one launch (start us, length us, event | category | flops | bytes accessed | tf_op | source)
XLA Modules:
  0.0 130.6 jit_solution(16947148702193646557)
XLA Ops:
  0.6 3.1 %start.1 = (s32[128,128]{1,0:T(8,128)}, f32[64,8,128]{2,1,0:T(8,128)}) custom-call(s32[8,64]{1,0:T(8,128)} %bitcast.92, s32[9,64]{1,0:T(8,128)} %bitcast.87, s32[1,64]{1,0:T(1,128)} %bitcast.95, f32[3,64,128]{2,1,0:T(8,128)} %bitcast.74, f32[64,8,128]{2,1,0:T(8,128)} %charge_ref.5, s32[64]{0:T(128)} %count_ref.7, f32[3,64]{1,0:T(4,128)} %cen_ref.3), custom_call_target="tpu_custom_call" | custom-call | tf_op jit(solution)/shard_map/start/pallas_call | solution.py:687
  3.7 4.0 %collective-permute-start = (f32[64,8,128]{2,1,0:T(8,128)}, f32[64,8,128]{2,1,0:T(8,128)S(1)}, u32[]{:S(2)}, u32[]{:S(2)}) collective-permute-start(f32[64,8,128]{2,1,0:T(8,128)} %get-tuple-element.63), channel_id=1, source_target_pairs={{0,1},{4,5},{8,9},{12,13},{16,17},{20,21},{24,25},{28,29},{32,33},... | collective-permute-start | bytes 786440 | tf_op jit(solution)/shard_map/ppermute | solution.py:695
  7.8 2.3 %collective-permute-start.1 = (f32[64,8,128]{2,1,0:T(8,128)}, f32[64,8,128]{2,1,0:T(8,128)S(1)}, u32[]{:S(2)}, u32[]{:S(2)}) collective-permute-start(f32[64,8,128]{2,1,0:T(8,128)} %get-tuple-element.63), channel_id=1, source_target_pairs={{0,2},{4,6},{8,10},{12,14},{16,18},{20,22},{24,26},{28,30},{32,34}... | collective-permute-start | bytes 786440 | tf_op jit(solution)/shard_map/ppermute | solution.py:695
  10.1 1.3 collective-permute-start.2
  11.4 8.3 %all-to-all-start.3 = ((s32[128,1,128]{2,1,0:T(1,128)}), s32[128,1,128]{2,1,0:T(1,128)S(1)}, u32[]{:S(2)}, u32[]{:S(2)}) async-start(s32[128,1,128]{2,1,0:T(1,128)} %bitcast.73), calls=%async_computation.3 | async-start | bytes 131072 | tf_op jit(solution)/shard_map/all_to_all | solution.py:318
  19.7 4.6 %send_tables.1 = (f32[64,8,128]{2,1,0:T(8,128)}, f32[64,8,128]{2,1,0:T(8,128)}, f32[64,8,128]{2,1,0:T(8,128)}) custom-call(f32[3,64,128]{2,1,0:T(8,128)} %bitcast.75, f32[64,8,128]{2,1,0:T(8,128)} %charge_ref.5, s32[64]{0:T(128)} %count_ref.7, f32[3,64]{1,0:T(4,128)} %cen_ref.3), custom_call_target="tpu_custom_call" | custom-call | flops 50000000 | bytes 1200000 | tf_op jit(solution)/shard_map/send_tables/pallas_call | solution.py:699
  24.4 1.7 %select_add_fusion.ex_ref = f32[64,8,128]{2,1,0:T(8,128)} fusion(f32[64,8,128]{2,1,0:T(8,128)} %get-tuple-element.63, f32[64,8,128]{2,1,0:T(8,128)S(1)} %collective-permute-done.2, f32[64,8,128]{2,1,0:T(8,128)S(1)} %collective-permute-done, f32[64,8,128]{2,1,0:T(8,128)S(1)} %collective-permute-done.1, pred[]{:T(512)S(6)} %eq.7), kind=kLoop, calls=%fused_computation.11 | loop fusion | flops 262144 | bytes 1310721 | tf_op jit(solution)/shard_map/add | solution.py:696
  26.1 3.4 %all-to-all-done.3 = s32[128,1,128]{2,1,0:T(1,128)S(1)} async-done(((s32[128,1,128]{2,1,0:T(1,128)}), s32[128,1,128]{2,1,0:T(1,128)S(1)}, u32[]{:S(2)}, u32[]{:S(2)}) %all-to-all-start.3) | async-done | bytes 65568 | tf_op jit(solution)/shard_map/all_to_all | solution.py:318
  29.5 0.6 copy-done.6
  30.1 6.0 %send.1 = f32[128,48,128]{2,1,0:T(8,128)} custom-call(s32[128,128]{1,0:T(8,128)} %bitcast.77, f32[64,8,128]{2,1,0:T(8,128)} %get-tuple-element.60.q_ref, f32[64,8,128]{2,1,0:T(8,128)} %get-tuple-element.61.w_ref, f32[64,8,128]{2,1,0:T(8,128)} %get-tuple-element.62.p_ref, f32[64,8,128]{2,1,0:T(8,128)} %select_add_fusion.ex_ref), custom_call_target="tpu_custom_call" | custom-call | tf_op jit(solution)/shard_map/send/pallas_call | solution.py:711
  36.1 5.4 %all-to-all-start.4 = ((f32[128,48,128]{2,1,0:T(8,128)}), f32[128,48,128]{2,1,0:T(8,128)S(1)}, u32[]{:S(2)}, u32[]{:S(2)}) async-start(f32[128,48,128]{2,1,0:T(8,128)} %send.1), calls=%async_computation.4 | async-start | bytes 6291456 | tf_op jit(solution)/shard_map/all_to_all | solution.py:318
  41.6 0.1 slice.36
  41.7 0.7 reshape_squeeze.4
  42.4 0.1 reshape_reshape_squeeze.3
  42.5 0.1 copy.81
  42.6 0.1 reshape.192
  42.7 0.6 gather_fusion.3
  43.4 0.1 copy.86
  43.4 0.2 copy.87
  43.6 1.4 %broadcast_in_dim.52 = f32[64,8,2,64]{3,2,1,0:T(2,128)} broadcast(f32[64,8,2]{2,1,0:T(8,128)S(1)} %copy.87), dimensions={0,1,2} | broadcast | bytes 266240 | tf_op jit(solution)/shard_map/broadcast_in_dim | solution.py:678
  45.0 2.0 %reshape.162.ec_ref = f32[64,8,128]{2,1,0:T(8,128)} reshape(f32[64,8,2,64]{3,2,1,0:T(2,128)} %broadcast_in_dim.52) | data formatting | bytes 524288 | tf_op jit(solution)/shard_map/reshape | solution.py:678
  47.1 0.7 fusion.1
  47.9 0.2 copy.89
  48.0 0.2 reshape.200
  48.3 1.0 gather_fusion.4
  49.3 0.1 copy.90
  49.5 0.8 broadcast_in_dim.54
  50.3 2.0 %copy.92 = f32[128,8,128]{2,1,0:T(8,128)} copy(f32[128,8,128]{0,2,1:T(8,128)} %bitcast.64) | data formatting | bytes 1048576 | tf_op jit(solution)/shard_map/reshape | solution.py:678
  52.3 0.9 copy.82
  53.2 0.2 copy.83
  53.4 0.2 reshape.184
  53.6 1.0 gather_fusion.2
  54.7 0.1 copy.84
  54.8 0.8 broadcast_in_dim.50
  55.7 2.1 %copy.93.nc_ref = f32[128,8,128]{2,1,0:T(8,128)} copy(f32[128,8,128]{0,2,1:T(8,128)} %bitcast.65) | data formatting | bytes 1048576 | tf_op jit(solution)/shard_map/reshape | solution.py:678
  57.8 9.8 %own_tables.1 = (f32[64,8,128]{2,1,0:T(8,128)}, bf16[64,2,32,128]{3,2,1,0:T(8,128)(2,1)}, f32[64,8,128]{2,1,0:T(8,128)}, bf16[64,128,128]{2,1,0:T(8,128)(2,1)}) custom-call(f32[3,64,128]{2,1,0:T(8,128)S(1)} %bitcast.76, f32[64,8,128]{2,1,0:T(8,128)} %charge_ref.5, s32[64]{0:T(128)S(1)} %copy-done.15), custom_call_target="tpu_custom_call" | custom-call | flops 200000000 | bytes 4000000 | tf_op jit(solution)/shard_map/own_tables/pallas_call | solution.py:722
  67.5 0.7 pad_add_fusion.tgt_ref
  68.3 0.8 broadcast_add_fusion.1.fc_ref
  69.1 0.2 fusion
  69.3 12.4 %all-to-all-done.4.got_ref = f32[128,48,128]{2,1,0:T(8,128)S(1)} async-done(((f32[128,48,128]{2,1,0:T(8,128)}), f32[128,48,128]{2,1,0:T(8,128)S(1)}, u32[]{:S(2)}, u32[]{:S(2)}) %all-to-all-start.4) | async-done | bytes 3145760 | tf_op jit(solution)/shard_map/all_to_all | solution.py:318
  81.7 1.6 %copy-done = f32[128,48,128]{2,1,0:T(8,128)} copy-done((f32[128,48,128]{2,1,0:T(8,128)}, f32[128,48,128]{2,1,0:T(8,128)S(1)}, u32[]{:S(2)}) %copy-start) | copy-done | bytes 3145752
  83.4 31.1 %pairs.3 = (f32[64,8,128]{2,1,0:T(8,128)}, f32[128,128]{1,0:T(8,128)}) custom-call(s32[128,9]{1,0:T(8,128)} %pad_add_fusion.tgt_ref, s32[64]{0:T(128)S(1)} %copy-done.15, f32[128,48,128]{2,1,0:T(8,128)} %copy-done, f32[128,8,128]{2,1,0:T(8,128)} %copy.93.nc_ref, f32[64,8,128]{2,1,0:T(8,128)} %reshape.162.ec_ref, f32[128,8,128]{2,1,0:T(8,128)} %broadcast_add_fusion.1.fc_ref, ...), custom_call_target="tpu_custom_call" | custom-call | flops 1000000000 | bytes 12000000 | tf_op jit(solution)/shard_map/pairs/pallas_call | solution.py:741
  114.5 5.4 %all-to-all-start.5 = ((f32[128,1,128]{2,1,0:T(1,128)}), f32[128,1,128]{2,1,0:T(1,128)S(1)}, u32[]{:S(2)}, u32[]{:S(2)}) async-start(f32[128,1,128]{2,1,0:T(1,128)} %bitcast.84), calls=%async_computation.5 | async-start | bytes 131072 | tf_op jit(solution)/shard_map/all_to_all | solution.py:318
  119.9 0.6 and_reduce_fusion
  121.2 8.5 %all-to-all-done.5 = f32[128,1,128]{2,1,0:T(1,128)S(1)} async-done(((f32[128,1,128]{2,1,0:T(1,128)}), f32[128,1,128]{2,1,0:T(1,128)S(1)}, u32[]{:S(2)}, u32[]{:S(2)}) %all-to-all-start.5) | async-done | bytes 65568 | tf_op jit(solution)/shard_map/all_to_all | solution.py:318
  129.7 0.2 conditional.1
  129.9 0.2 slice_reduce_fusion
  130.0 0.5 broadcast_multiply_fusion
  (46 shorter events, 0.3 us)
Async XLA Ops:
  3.7 20.6 %collective-permute-start = (f32[64,8,128]{2,1,0:T(8,128)}, f32[64,8,128]{2,1,0:T(8,128)S(1)}, u32[]{:S(2)}, u32[]{:S(2)}) collective-permute-start(f32[64,8,128]{2,1,0:T(8,128)} %get-tuple-element.63), channel_id=1, source_target_pairs={{0,1},{4,5},{8,9},{12,13},{16,17},{20,21},{24,25},{28,29},{32,33},... | collective-permute-start | bytes 786440 | tf_op jit(solution)/shard_map/ppermute | solution.py:695
  7.8 16.6 %collective-permute-start.1 = (f32[64,8,128]{2,1,0:T(8,128)}, f32[64,8,128]{2,1,0:T(8,128)S(1)}, u32[]{:S(2)}, u32[]{:S(2)}) collective-permute-start(f32[64,8,128]{2,1,0:T(8,128)} %get-tuple-element.63), channel_id=1, source_target_pairs={{0,2},{4,6},{8,10},{12,14},{16,18},{20,22},{24,26},{28,30},{32,34}... | collective-permute-start | bytes 786440 | tf_op jit(solution)/shard_map/ppermute | solution.py:695
  10.1 14.3 %collective-permute-start.2 = (f32[64,8,128]{2,1,0:T(8,128)}, f32[64,8,128]{2,1,0:T(8,128)S(1)}, u32[]{:S(2)}, u32[]{:S(2)}) collective-permute-start(f32[64,8,128]{2,1,0:T(8,128)} %get-tuple-element.63), channel_id=1, source_target_pairs={{0,3},{4,7},{8,11},{12,15},{16,19},{20,23},{24,27},{28,31},{32,35}... | collective-permute-start | bytes 786440 | tf_op jit(solution)/shard_map/ppermute | solution.py:695
  11.4 18.1 %all-to-all-start.3 = ((s32[128,1,128]{2,1,0:T(1,128)}), s32[128,1,128]{2,1,0:T(1,128)S(1)}, u32[]{:S(2)}, u32[]{:S(2)}) async-start(s32[128,1,128]{2,1,0:T(1,128)} %bitcast.73), calls=%async_computation.3 | async-start | bytes 131072 | tf_op jit(solution)/shard_map/all_to_all | solution.py:318
  29.5 0.6 copy-start.6
  36.1 5.4 %copy-start.4 = (s32[128,128]{1,0:T(8,128)S(1)}, s32[128,128]{1,0:T(8,128)}, u32[]{:S(2)}) copy-start(s32[128,128]{1,0:T(8,128)} %get-tuple-element.59) | copy-start | bytes 196612
  36.1 6.3 %copy-start.12 = (f32[3,64]{1,0:T(4,128)S(1)}, f32[3,64]{1,0:T(4,128)}, u32[]{:S(2)}) copy-start(f32[3,64]{1,0:T(4,128)} %cen_ref.3) | copy-start | bytes 2308
  36.1 45.6 %all-to-all-start.4 = ((f32[128,48,128]{2,1,0:T(8,128)}), f32[128,48,128]{2,1,0:T(8,128)S(1)}, u32[]{:S(2)}, u32[]{:S(2)}) async-start(f32[128,48,128]{2,1,0:T(8,128)} %send.1), calls=%async_computation.4 | async-start | bytes 6291456 | tf_op jit(solution)/shard_map/all_to_all | solution.py:318
  41.6 0.7 copy-start.8
  49.4 8.3 %copy-start.5 = (f32[64,3,128]{2,0,1:T(8,128)S(1)}, f32[64,3,128]{2,0,1:T(8,128)}, u32[]{:S(2)}) copy-start(f32[64,3,128]{2,0,1:T(8,128)} %param.12) | copy-start | bytes 294916
  49.5 8.3 %copy-start.15 = (s32[64]{0:T(128)S(1)}, s32[64]{0:T(128)}, u32[]{:S(2)}) copy-start(s32[64]{0:T(128)} %count_ref.7) | copy-start | bytes 772
  54.7 13.6 %copy-start.17 = (f32[8,128]{1,0:T(8,128)S(1)}, f32[8,128]{1,0:T(8,128)}, u32[]{:S(2)}) copy-start(f32[8,128]{1,0:T(8,128)} %constant.77) | copy-start | bytes 12292
  54.8 12.8 %copy-start.9 = (s32[128,8]{1,0:T(8,128)S(1)}, s32[128,8]{1,0:T(8,128)}, u32[]{:S(2)}) copy-start(s32[128,8]{1,0:T(8,128)} %copy-done.8) | copy-start | bytes 12292
  54.8 12.8 %copy-start.11 = (s32[128,1]{1,0:T(8,128)S(1)}, s32[128,1]{1,0:T(8,128)}, u32[]{:S(2)}) copy-start(s32[128,1]{1,0:T(8,128)} %reshape_squeeze.4) | copy-start | bytes 1540
  55.7 13.4 %copy-start.7 = (s32[128,1,128]{2,1,0:T(1,128)S(1)}, s32[128,1,128]{2,1,0:T(1,128)}, u32[]{:S(2)}) copy-start(s32[128,1,128]{2,1,0:T(1,128)} %copy-done.6) | copy-start | bytes 196612
  57.7 10.5 %copy-start.1 = (f32[128,8,128]{2,1,0:T(8,128)S(1)}, f32[128,8,128]{2,1,0:T(8,128)}, u32[]{:S(2)}) copy-start(f32[128,8,128]{2,1,0:T(8,128)} %copy.92) | copy-start | bytes 1572868
  81.7 1.6 %copy-start = (f32[128,48,128]{2,1,0:T(8,128)}, f32[128,48,128]{2,1,0:T(8,128)S(1)}, u32[]{:S(2)}) copy-start(f32[128,48,128]{2,1,0:T(8,128)S(1)} %all-to-all-done.4.got_ref) | copy-start | bytes 9437188
  83.3 46.3 %copy-start.3 = (f32[64,8,128]{2,1,0:T(8,128)S(1)}, f32[64,8,128]{2,1,0:T(8,128)}, u32[]{:S(2)}) copy-start(f32[64,8,128]{2,1,0:T(8,128)} %charge_ref.5) | copy-start | bytes 786436
  83.3 46.3 %copy-start.13 = (s32[64,9]{0,1:T(8,128)S(1)}, s32[64,9]{0,1:T(8,128)}, u32[]{:S(2)}) copy-start(s32[64,9]{0,1:T(8,128)} %param.17) | copy-start | bytes 6916
  83.3 46.3 %copy-start.14 = (s32[64,8]{0,1:T(8,128)S(1)}, s32[64,8]{0,1:T(8,128)}, u32[]{:S(2)}) copy-start(s32[64,8]{0,1:T(8,128)} %param.16) | copy-start | bytes 6148
  83.3 46.3 %copy-start.16 = (f32[1,8,128]{2,1,0:T(8,128)S(1)}, f32[1,8,128]{2,1,0:T(8,128)}, u32[]{:S(2)}) copy-start(f32[1,8,128]{2,1,0:T(8,128)} %constant.59.clone) | copy-start | bytes 12292
  114.5 15.2 %all-to-all-start.5 = ((f32[128,1,128]{2,1,0:T(1,128)}), f32[128,1,128]{2,1,0:T(1,128)S(1)}, u32[]{:S(2)}, u32[]{:S(2)}) async-start(f32[128,1,128]{2,1,0:T(1,128)} %bitcast.84), calls=%async_computation.5 | async-start | bytes 131072 | tf_op jit(solution)/shard_map/all_to_all | solution.py:318

commit v3 on v2

--- a/solution.py
+++ b/solution.py
@@ -12,12 +12,12 @@
 AXES = ("gx", "gy")
 NODES = 4
 ROOT3 = 1.7320508075688772
+LOG2E = 1.4426950408889634
 BF = jnp.bfloat16
 F32 = jnp.float32
 NODE = [math.cos((2 * i + 1) * math.pi / 8) for i in range(NODES)]
 NT = (((1,), (1,)), ((), ()))
 TN = (((0,), (0,)), ((), ()))
-VMEM_LIMIT = 56 * 1024 * 1024
 
 
 def iota(shape, dim):
@@ -72,7 +72,7 @@
 def matern(dist2):
     safe = jnp.maximum(dist2, 1e-12)
     scaled = safe * lax.rsqrt(safe)
-    decay = jnp.exp(-scaled)
+    decay = jnp.exp2(scaled * (-LOG2E))
     return decay + scaled * decay
 
 
@@ -310,8 +310,8 @@
 SMEM = pl.BlockSpec(memory_space=pltpu.SMEM)
 
 
-def params():
-    return pltpu.CompilerParams(vmem_limit_bytes=VMEM_LIMIT)
+def params(mebibytes=56):
+    return pltpu.CompilerParams(vmem_limit_bytes=mebibytes * 1024 * 1024)
 
 
 def exchange(x):
@@ -401,6 +401,7 @@
 
 HALF = 64
 ROWS = 48
+UNROLL = 4
 
 
 def start_kernel(far_ref, near_ref, most_ref, pos_ref, charge_ref, count_ref, cen_ref, want_ref, ex_ref):
@@ -438,19 +439,19 @@
             before = dot(onehot, tri) + seen
             rank = jnp.sum(jnp.where(hit, before, 0.0), axis=0, keepdims=True).astype(jnp.int32)
             seen = seen + jnp.sum(ones, axis=1, keepdims=True)
-            within = jnp.broadcast_to(flat % boxes, (32, 128))
+            within = jnp.broadcast_to(flat % boxes * 16, (32, 128))
             mine = row32 % 4 == jnp.broadcast_to(rank, (32, 128))
             value = jnp.where(row32 // 4 == base // 4, within, jnp.where(row32 // 4 == base // 4 + 4, boxrow, 0))
             value = jnp.where(mine, value, 0).astype(F32).astype(BF)
             result = result + dot(onehot, value, NT)
     result = jnp.concatenate([result, jnp.zeros((128, 96), F32)], axis=1)
-    extra = jnp.zeros((128, 1), F32)
-    member = iota((128, 1), 0) % 4
-    for y in range(4):
-        column = result[:, y : y + 1]
-        column = pltpu.roll(jnp.broadcast_to(column, (128, 128)), y, 0)[:, 0:1] if y else column
-        extra = jnp.where(member == y, column, extra)
-    result = jnp.where(line == 8, jnp.broadcast_to(extra, (128, 128)), result)
+    member = peer % 4
+    moved = [result] + [pltpu.roll(result, y, 0) for y in range(1, 4)]
+    for at, base, scale in ((8, 0, 0.5), (24, 16, 1.0)):
+        extra = jnp.zeros((128, 1), F32)
+        for y in range(4):
+            extra = jnp.where(member[:, 0:1] == y, moved[y][:, base + y : base + y + 1], extra)
+        result = jnp.where(line == at, jnp.broadcast_to(scale * extra, (128, 128)), result)
     most = jnp.max(most_ref[...], axis=1, keepdims=True)
     want_ref[...] = jnp.where(line == 9, jnp.broadcast_to(most, (128, 128)), result.astype(jnp.int32))
 
@@ -482,22 +483,22 @@
     return jnp.where(iota((8, 128), 1) < HALF, x, pltpu.roll(x, HALF, 1))
 
 
-def send_table_kernel(pos_ref, charge_ref, count_ref, cen_ref, q_ref, w_ref, p_ref):
+def send_table_kernel(pos_ref, charge_ref, count_ref, cen_ref, near_ref, far_ref):
     boxes = charge_ref.shape[0]
     lane = iota((8, 128), 1)
     sub4 = iota((8, 128), 0) % 4
 
     def body(b, carry):
         q = jnp.where(lane < count_ref[b], charge_ref[b], 0.0)
-        q_ref[b] = doubled(q)
+        near_ref[b, 0:8] = doubled(q)
         x = point_rows(pos_ref, b)
+        cx, cy, cz = cen_ref[0, b], cen_ref[1, b], cen_ref[2, b]
+        center = jnp.where(sub4 == 0, cx, jnp.where(sub4 == 1, cy, cz))
+        near_ref[b, 8:16] = doubled(center + 0.5 * x)
         qs = jnp.concatenate(split(q), axis=0)
         weight = fold(dot(qs, stack_kernel(cheb_rows(x)), NT))
-        w_ref[b] = weight + pltpu.roll(weight, 64, 1)
-        cx, cy, cz = cen_ref[0, b], cen_ref[1, b], cen_ref[2, b]
-        far = jnp.where(lane % 4 == 0, cx, jnp.where(lane % 4 == 1, cy, cz))
-        center = jnp.where(sub4 == 0, cx, jnp.where(sub4 == 1, cy, cz))
-        p_ref[b] = jnp.where(sub4 == 3, far, doubled(center + 0.5 * x))
+        far_ref[b, 0:8] = weight + pltpu.roll(weight, 64, 1)
+        far_ref[b, 8:16] = jnp.where(lane % 4 == 0, cx, jnp.where(lane % 4 == 1, cy, cz))
         return carry
 
     lax.fori_loop(0, boxes, body, 0, unroll=8)
@@ -528,7 +529,45 @@
     lax.fori_loop(0, boxes, body, 0, unroll=4)
 
 
-def send_kernel(ids_ref, q_ref, w_ref, p_ref, ex_ref, out_ref):
+def goal_kernel(want_ref, cen_ref, node_ref, nc_ref, fc_ref, ec_ref, odd_ref):
+    lane = iota((128, 128), 1)
+    left = lane < HALF
+    boxes = cen_ref.shape[1]
+    cen = jnp.concatenate([cen_ref[...], jnp.zeros((5, boxes), F32)], axis=0)
+    cen = jnp.concatenate([cen, jnp.zeros((8, 128 - boxes), F32)], axis=1)
+    cen = jnp.concatenate([cen, jnp.zeros((120, 128), F32)], axis=0).T
+    high, rest = split(cen)
+    rest = cen - high.astype(F32)
+    mid, low = split(rest)
+    parts = jnp.concatenate([high, mid, low], axis=0)
+    want = want_ref[...]
+
+    def centers(at):
+        goal = jnp.broadcast_to(want[:, at : at + 1], (128, 128))
+        onehot = (goal == lane).astype(F32).astype(BF)
+        found = dot(jnp.concatenate([onehot] * 3, axis=1), parts)
+        return [jnp.broadcast_to(found[:, d : d + 1], (128, 128)) for d in range(3)]
+
+    nc_ref[...] = jnp.zeros_like(nc_ref)
+    fc_ref[...] = jnp.zeros_like(fc_ref)
+    ec_ref[...] = jnp.zeros_like(ec_ref)
+    for ref, base in ((nc_ref, 16), (fc_ref, 20)):
+        for u in range(2):
+            first, second = centers(base + 2 * u), centers(base + 2 * u + 1)
+            for d in range(3):
+                row = jnp.where(left, first[d], second[d])
+                if base == 20:
+                    row = row + node_ref[d : d + 1, :]
+                ref[pl.ds(4 * u + d, 128, stride=8), :] = row
+    extra = centers(24)
+    for d in range(3):
+        odd_ref[...] = extra[d]
+        even, odd = odd_ref[pl.ds(0, 64, stride=2), :], odd_ref[pl.ds(1, 64, stride=2), :]
+        ec_ref[pl.ds(d, 64, stride=8), :] = jnp.where(left[:64], even, odd)
+
+
+def send_kernel(member_ref, served_ref, near_ref, far_ref, own_ref, *refs):
+    moved, (out_ref, ids_ref, ex_ref, sem) = refs[:3], refs[3:]
     step = pl.program_id(0)
     group = out_ref.shape[0]
     sub4 = iota((8, 128), 0) % 4
@@ -536,45 +575,59 @@
     lane = iota((8, 128), 1)
     left = lane < HALF
 
+    @pl.when(step == 0)
+    def _():
+        copy = pltpu.make_async_copy(served_ref, ids_ref, sem)
+        copy.start()
+        ex_ref[...] = moved[0][...] + moved[1][...] + moved[2][...]
+
+        @pl.when(member_ref[0] == 0)
+        def _():
+            ex_ref[...] = own_ref[...]
+
+        copy.wait()
+
     def body(k, carry):
         peer = step * group + k
-        near = [ids_ref[peer, j] for j in range(4)]
-        far = [ids_ref[peer, 4 + j] for j in range(4)]
-        q = [q_ref[n] for n in near]
+        rows = lambda ref, j, at, size: ref[pl.ds(pl.multiple_of(ids_ref[peer, j], size) + at, 8), :]
+        q = [rows(near_ref, j, 0, 16) for j in range(4)]
+        s = [rows(near_ref, j, 8, 16) for j in range(4)]
+        w = [rows(far_ref, 4 + j, 0, 16) for j in range(4)]
+        c = [rows(far_ref, 4 + j, 8, 16) for j in range(4)]
         out_ref[k, 0:8] = jnp.where(left, q[0], q[1])
         out_ref[k, 8:16] = jnp.where(left, q[2], q[3])
-        w = [w_ref[n] for n in far]
         out_ref[k, 16:24] = jnp.where(left, w[0], w[2])
         out_ref[k, 24:32] = jnp.where(left, w[1], w[3])
-        out_ref[k, 32:40] = ex_ref[ids_ref[peer, 8]]
-        c = [p_ref[n] for n in far]
+        out_ref[k, 32:40] = rows(ex_ref, 8, 0, 8)
         centers = jnp.where(left, jnp.where(lane < 4, c[0], c[2]), jnp.where(lane < 68, c[1], c[3]))
-        s = [p_ref[n] for n in near]
         points = jnp.where(top, jnp.where(left, s[0], s[1]), jnp.where(left, s[2], s[3]))
         out_ref[k, 40:48] = jnp.where(sub4 == 3, centers, points)
         return carry
 
-    lax.fori_loop(0, group, body, 0, unroll=8)
+    lax.fori_loop(0, group, body, 0, unroll=16)
 
 
 def duo_kernel(
-    tgt_ref, count_ref, got_ref, nc_ref, ec_ref, fc_ref, f_ref, fn_ref, base_ref, q_ref, t_ref, out_ref, term_ref,
-    near_acc, far_acc, ft_ref, xt_ref, *bufs
+    got_ref, fn_ref, want_hbm, nc_hbm, ec_hbm, fc_hbm, f_hbm, base_hbm, q_hbm, w_hbm, near_hbm, far_hbm, term_ref,
+    tgt_ref, nc_ref, ec_ref, fc_ref, f_ref, base_ref, q_ref, w_ref, near_ref, far_ref, sems, ft_ref, *bufs
 ):
-    dist_refs, value_refs = bufs[:7], bufs[7:]
+    whole = [(fc_hbm, fc_ref), (want_hbm, tgt_ref), (nc_hbm, nc_ref), (ec_hbm, ec_ref), (f_hbm, f_ref)]
+    whole += [(base_hbm, base_ref), (q_hbm, q_ref), (w_hbm, w_ref)]
+    loads = [pltpu.make_async_copy(source, target, sems.at[i]) for i, (source, target) in enumerate(whole)]
+    for copy in loads:
+        copy.start()
+    xt_refs, dist_refs, value_refs = bufs[:2], (bufs[2:9], bufs[9:16]), (bufs[16:23], bufs[23:30])
+    near_accs, far_accs = bufs[30:32], bufs[32:34]
     peers = got_ref.shape[0]
     duos = peers // 2
     boxes = f_ref.shape[0]
     sub = iota((8, 128), 0)
     lane = iota((8, 128), 1)
     left = lane < HALF
-    near_acc[...] = base_ref[...]
-    far_acc[...] = jnp.zeros_like(far_acc)
-    xt_ref[...] = jnp.zeros_like(xt_ref)
-    for ref in dist_refs:
+    for ref in value_refs[1] + near_accs + far_accs:
         ref[...] = jnp.zeros_like(ref)
-    for ref in value_refs:
-        ref[...] = jnp.zeros_like(ref)
+    for ref in dist_refs[1]:
+        ref[...] = jnp.full(ref.shape, 1e6, F32)
     spread = (iota((128, 128), 0) // 64 == iota((128, 128), 1) // 64).astype(F32).astype(BF)
 
     batch = 16
@@ -593,56 +646,57 @@
         ft_ref[at] = jnp.concatenate(planes(rel, False), axis=1).astype(BF)
         return carry
 
+    loads[0].wait()
     lax.fori_loop(0, peers // batch, far_body, 0, unroll=2)
 
     def extra(duo):
         return got_ref[2 * duo, 32:40], got_ref[2 * duo + 1, 32:40]
 
-    def body(i, carry):
-        duo = jnp.maximum(i - 3, 0)
-        go = jnp.broadcast_to(i, (8, 128)) >= 3
+    def goals(duo):
+        pairs = [(tgt_ref[2 * duo + k // 2, 16 + 2 * (k % 2)], tgt_ref[2 * duo + k // 2, 17 + 2 * (k % 2)]) for k in range(4)]
+        return pairs + [(tgt_ref[2 * duo, 24], tgt_ref[2 * duo + 1, 24])]
+
+    def halves(x):
+        high = x.astype(BF).astype(F32)
+        both = [high, x - high]
+        return [jnp.where(left, part, 0.0) for part in both] + [jnp.where(left, 0.0, part) for part in both]
+
+    def products(duo, value):
         ex = extra(duo)
         tiles = [got_ref[2 * duo + k // 2, 8 * (k % 2) : 8 * (k % 2) + 8] for k in range(4)]
         tiles.append(jnp.where(left, ex[0], pltpu.roll(ex[1], HALF, 1)))
-        goals = [(tgt_ref[2 * duo + k // 2, 2 * (k % 2)], tgt_ref[2 * duo + k // 2, 2 * (k % 2) + 1]) for k in range(4)]
-        goals.append((tgt_ref[2 * duo, 8], tgt_ref[2 * duo + 1, 8]))
-        for k in range(5):
-            q = jnp.where(go, tiles[k], 0.0)
-            qs = split(jnp.where(left, q, 0.0)) + split(jnp.where(left, 0.0, q))
-            qs = jnp.concatenate(qs, axis=0)
-            new = dot(jnp.concatenate([qs, qs], axis=1), value_refs[k][...])
-            near_acc[goals[k][0]] += fold(new[0:16])
-            near_acc[goals[k][1]] += fold(new[16:32])
+        for k, goal in enumerate(goals(duo)):
+            qs = jnp.concatenate(halves(tiles[k]), axis=0).astype(BF)
+            new = dot(jnp.concatenate([qs, qs], axis=1), value[k][...])
+            for h in range(2):
+                near_accs[h][goal[h]] += fold(new[16 * h : 16 * h + 16])
         for a in range(2):
             ws = []
             for h in range(2):
-                w = jnp.where(go, got_ref[2 * duo + a, 16 + 8 * h : 24 + 8 * h], 0.0)
-                ws += list(split(jnp.where(left, w, 0.0)) + split(jnp.where(left, 0.0, w)))
-            ws = jnp.concatenate(ws, axis=0)
-            new = dot(jnp.concatenate([ws, ws], axis=1), value_refs[5 + a][...])
+                ws += halves(got_ref[2 * duo + a, 16 + 8 * h : 24 + 8 * h])
+            ws = jnp.concatenate(ws, axis=0).astype(BF)
+            new = dot(jnp.concatenate([ws, ws], axis=1), value[5 + a][...])
             for h in range(2):
                 for u in range(2):
                     at = 32 * h + 16 * u
-                    part = fold(new[at : at + 16])
-                    far_acc[tgt_ref[2 * duo + a, 4 + 2 * u + h]] += jnp.where(left if h == 0 else jnp.logical_not(left), part, 0.0)
-
+                    far_accs[h][tgt_ref[2 * duo + a, 20 + 2 * u + h]] += fold(new[at : at + 16])
+
+    def values(dist, value):
         for k in range(7):
-            value_refs[k][...] = stack_kernel(matern(dist_refs[k][...]))
-
-        duo = jnp.clip(i - 1, 0, duos - 1)
-        upper, lower = xt_ref[0:64, :], xt_ref[64:128, :]
-        goals = [(tgt_ref[2 * duo + k // 2, 2 * (k % 2)], tgt_ref[2 * duo + k // 2, 2 * (k % 2) + 1]) for k in range(4)]
-        goals.append((tgt_ref[2 * duo, 8], tgt_ref[2 * duo + 1, 8]))
-        for k in range(5):
+            value[k][...] = stack_kernel(matern(dist[k][...]))
+
+    def distances(duo, xt, dist):
+        for k, goal in enumerate(goals(duo)):
             v, u = k // 2, k % 2
-            for half, part in enumerate((upper, lower)):
+            for half in range(2):
                 pieces = [jnp.zeros((32 * v, 128), BF)] if v else []
-                pieces += [f_ref[goals[k][half], u], jnp.zeros((96 - 32 * v, 128), BF)]
-                dist_refs[k][64 * half : 64 * half + 64, :] = dot(part, jnp.concatenate(pieces, axis=0))
+                pieces += [f_ref[goal[half], u], jnp.zeros((96 - 32 * v, 128), BF)]
+                at = slice(64 * half, 64 * half + 64)
+                dist[k][at, :] = dot(xt[at, :], jnp.concatenate(pieces, axis=0))
         for a in range(2):
-            dist_refs[5 + a][...] = dot(fn_ref[...], ft_ref[2 * duo + a])
-
-        duo = jnp.minimum(i, duos - 1)
+            dist[5 + a][...] = dot(fn_ref[...], ft_ref[2 * duo + a])
+
+    def features(duo, xt):
         ex = extra(duo)
         feats = []
         for a in range(2):
@@ -650,32 +704,65 @@
         point = jnp.where(left, pltpu.roll(ex[0], HALF, 1), ex[1])
         feats += planes((point - ec_ref[duo]) * ROOT3, True)
         feats.append(jnp.zeros((32, 128), F32))
-        xt_ref[...] = jnp.concatenate(feats, axis=0).T.astype(BF)
+        xt[...] = jnp.concatenate(feats, axis=0).T.astype(BF)
+
+    def body(i, carry):
+        for s in range(UNROLL):
+            now, was = s % 2, 1 - s % 2
+            step = UNROLL * i + s
+            products(jnp.maximum(step - 2, 0), value_refs[was])
+            values(dist_refs[was], value_refs[now])
+            distances(step, xt_refs[was], dist_refs[now])
+            features(jnp.minimum(step + 1, duos - 1), xt_refs[now])
         return carry
 
-    lax.fori_loop(0, duos + 3, body, 0)
+    for copy in loads[1:5]:
+        copy.wait()
+    features(0, xt_refs[1])
+    lax.fori_loop(0, duos // UNROLL, body, 0)
+    products(duos - 2, value_refs[1])
+    values(dist_refs[1], value_refs[0])
+    products(duos - 1, value_refs[0])
+
+    for copy in loads[5:]:
+        copy.wait()
 
     def finish(b, total):
-        ls = jnp.concatenate(split(far_acc[b]), axis=0)
-        both = t_ref[b]
-        high, low = both[0:64], both[64:128]
-        table = jnp.concatenate([high, high, low, low], axis=0)
-        far = fold(dot(jnp.concatenate([ls, ls], axis=1), table))
-        product = jnp.where(lane < count_ref[b], near_acc[b] + far, 0.0)
-        out_ref[b] = product
-        return total + product * q_ref[b]
-
-    total = lax.fori_loop(0, boxes, finish, jnp.zeros((8, 128), F32), unroll=8)
+        near = near_accs[0][b] + near_accs[1][b] + base_ref[b]
+        far = jnp.where(left, far_accs[0][b], far_accs[1][b])
+        near_ref[b] = near
+        far_ref[b] = far
+        return total + near * q_ref[b] + far * w_ref[b, 0:8]
+
+    total = jnp.zeros((8, 128), F32)
+    stores = []
+    quarter = boxes // 4
+    for part in range(4):
+        total = lax.fori_loop(part * quarter, part * quarter + quarter, finish, total, unroll=16)
+        at = pl.ds(part * quarter, quarter)
+        for source, target, sem in ((near_ref, near_hbm, 8 + part), (far_ref, far_hbm, 12 + part)):
+            copy = pltpu.make_async_copy(source.at[at], target.at[at], sems.at[sem])
+            copy.start()
+            stores.append(copy)
     ones = jnp.ones((128, 128), F32)
     sums = lax.dot_general(ones, total, NT, precision=lax.Precision.HIGHEST, preferred_element_type=F32)
     term_ref[...] = jnp.concatenate([sums, jnp.zeros((128, 120), F32)], axis=1)
-
-
-def center_rows(centers, goals, halves=2):
-    n, units = goals.shape[:2]
-    rows = jnp.pad(centers[goals], ((0, 0), (0, 2 - units), (0, 0), (0, 1)))
-    rows = rows.transpose(0, 1, 3, 2).reshape(n, 8, 2, 1)
-    return jnp.broadcast_to(rows, (n, 8, 2, HALF)).reshape(n, 8, 128)
+    for copy in stores:
+        copy.wait()
+
+
+def finish_kernel(count_ref, near_ref, far_ref, t_ref, out_ref):
+    boxes = near_ref.shape[0]
+    lane = iota((8, 128), 1)
+
+    def body(b, carry):
+        ls = jnp.concatenate(split(far_ref[b]), axis=0)
+        high, low = t_ref[b, 0:64], t_ref[b, 64:128]
+        far = fold(dot(jnp.concatenate([ls, ls], axis=1), jnp.concatenate([high, high, low, low], axis=0)))
+        out_ref[b] = jnp.where(lane < count_ref[b], near_ref[b] + far, 0.0)
+        return carry
+
+    lax.fori_loop(0, boxes, body, 0, unroll=16)
 
 
 def on_device(local_pos, charges, counts, box_centers, far_list, near_list):
@@ -684,80 +771,117 @@
     struct = jax.ShapeDtypeStruct
     pos = jnp.transpose(local_pos, (1, 0, 2))
     table = struct((boxes, 8, 128), F32)
+    hbm = pltpu.HBM
+    stay = lambda x: pltpu.with_memory_space_constraint(x, pltpu.HBM)
+    anywhere = pl.BlockSpec(memory_space=pltpu.HBM)
+    wide = struct((boxes, 16, 128), F32)
+    member = (lax.axis_index("gy") % 4).astype(jnp.int32).reshape(1)
     want, ex_own = pl.pallas_call(
         start_kernel,
         out_shape=(struct((devices, 128), jnp.int32), table),
         in_specs=[vmem(), vmem(), vmem(), vmem(), vmem(), SMEM, SMEM],
         out_specs=(vmem(), vmem()),
-        compiler_params=params(),
+        compiler_params=params(8),
         name="start",
     )(far_list.T, near_list.T, counts.reshape(1, boxes), pos, charges, counts, box_centers)
     moved = [lax.ppermute(ex_own, "gy", [(4 * z, 4 * z + k) for z in range(4)]) for k in range(1, 4)]
-    ex_tab = moved[0] + moved[1] + moved[2] + jnp.where(lax.axis_index("gy") % 4 == 0, ex_own, 0.0)
     served = exchange(want.reshape(devices, 1, 128)).reshape(devices, 128)
 
-    q2_tab, w_tab, p_tab = pl.pallas_call(
+    near_tab, far_tab = pl.pallas_call(
         send_table_kernel,
-        out_shape=(table, table, table),
+        out_shape=(wide, wide),
         in_specs=[vmem(), vmem(), SMEM, SMEM],
-        out_specs=(vmem(), vmem(), vmem()),
-        compiler_params=params(),
+        out_specs=(vmem(), vmem()),
+        compiler_params=params(8),
         cost_estimate=pl.CostEstimate(flops=50_000_000, bytes_accessed=1_200_000, transcendentals=0),
         name="send_tables",
     )(pos, charges, counts, box_centers)
 
-    group = 16
-    lead = lambda shape: vmem((group,) + shape, lambda i: (i,) + (0,) * len(shape))
+    group = 64
+    flat = lambda x: x.reshape(-1, 128)
     send = pl.pallas_call(
         send_kernel,
         grid=(devices // group,),
         out_shape=struct((devices, ROWS, 128), F32),
-        in_specs=[SMEM, vmem(), vmem(), vmem(), vmem()],
-        out_specs=lead((ROWS, 128)),
-        compiler_params=params(),
+        in_specs=[SMEM, pl.BlockSpec(memory_space=pl.ANY)] + [vmem()] * 6,
+        out_specs=vmem((group, ROWS, 128), lambda i: (i, 0, 0)),
+        scratch_shapes=[
+            pltpu.SMEM((devices, 128), jnp.int32),
+            pltpu.VMEM((boxes * 8, 128), F32),
+            pltpu.SemaphoreType.DMA(()),
+        ],
+        compiler_params=params(12),
         name="send",
-    )(served, q2_tab, w_tab, p_tab, ex_tab)
+    )(member, served, flat(near_tab), flat(far_tab), flat(ex_own), *[flat(x) for x in moved])
     got = exchange(send)
 
     q_tab, f_tab, base, cheb = pl.pallas_call(
         own_table_kernel,
-        out_shape=(table, struct((boxes, 2, 32, 128), BF), table, struct((boxes, 128, 128), BF)),
+        out_shape=(
+            hbm((boxes, 8, 128), F32),
+            hbm((boxes, 2, 32, 128), BF),
+            hbm((boxes, 8, 128), F32),
+            hbm((boxes, 128, 128), BF),
+        ),
         in_specs=[vmem(), vmem(), SMEM],
         out_specs=(vmem(), vmem(), vmem(), vmem()),
-        compiler_params=params(),
+        compiler_params=params(8),
         cost_estimate=pl.CostEstimate(flops=200_000_000, bytes_accessed=4_000_000, transcendentals=2_000_000),
         name="own_tables",
     )(pos, charges, counts)
 
-    centers = box_centers.T
-    goal = want[:, 16:24]
-    more = goal.reshape(devices // 4, 4, 8)[:, 0, :4].reshape(devices, 1)
-    tgt = jnp.concatenate([goal, more], axis=1)
-    near_cen = center_rows(centers, goal[:, :4].reshape(devices, 2, 2))
-    far_cen = center_rows(centers, goal[:, 4:].reshape(devices, 2, 2)) + node_rows()[None]
-    ex_cen = center_rows(centers, more.reshape(devices // 2, 1, 2))
+    near_cen, far_cen, ex_cen = pl.pallas_call(
+        goal_kernel,
+        out_shape=(hbm((devices * 8, 128), F32), hbm((devices * 8, 128), F32), hbm((devices * 4, 128), F32)),
+        in_specs=[vmem()] * 3,
+        out_specs=(vmem(), vmem(), vmem()),
+        scratch_shapes=[pltpu.VMEM((128, 128), F32)],
+        compiler_params=params(8),
+        cost_estimate=pl.CostEstimate(flops=50_000_000, bytes_accessed=2_000_000, transcendentals=0),
+        name="goals",
+    )(want, box_centers, jnp.asarray(node_rows()))
+    near_cen, far_cen, ex_cen = [x.reshape(-1, 8, 128) for x in (near_cen, far_cen, ex_cen)]
 
     big = lambda dtype, rows: pltpu.VMEM((rows, 128), dtype)
-    product, term = pl.pallas_call(
+    near, far, term = pl.pallas_call(
         duo_kernel,
-        out_shape=(table, struct((devices, 128), F32)),
-        in_specs=[SMEM, SMEM] + [vmem()] * 9,
-        out_specs=(vmem(), vmem()),
+        out_shape=(hbm((boxes, 8, 128), F32), hbm((boxes, 8, 128), F32), struct((devices, 128), F32)),
+        in_specs=[vmem()] * 2 + [anywhere] * 8,
+        out_specs=(anywhere, anywhere, vmem()),
         scratch_shapes=[
+            pltpu.SMEM((devices, 128), jnp.int32),
+            pltpu.VMEM((devices, 8, 128), F32),
+            pltpu.VMEM((devices // 2, 8, 128), F32),
+            pltpu.VMEM((devices, 8, 128), F32),
+            pltpu.VMEM((boxes, 2, 32, 128), BF),
             pltpu.VMEM((boxes, 8, 128), F32),
             pltpu.VMEM((boxes, 8, 128), F32),
+            pltpu.VMEM((boxes, 16, 128), F32),
+            pltpu.VMEM((boxes, 8, 128), F32),
+            pltpu.VMEM((boxes, 8, 128), F32),
+            pltpu.SemaphoreType.DMA((16,)),
             pltpu.VMEM((devices, 32, 128), BF),
-            big(BF, 128),
         ]
-        + [big(F32, 128)] * 7
-        + [big(BF, 256)] * 7,
-        compiler_params=params(),
+        + [big(BF, 128)] * 2
+        + [big(F32, 128)] * 14
+        + [big(BF, 256)] * 14
+        + [pltpu.VMEM((boxes, 8, 128), F32)] * 4,
+        compiler_params=params(20),
         cost_estimate=pl.CostEstimate(flops=1_000_000_000, bytes_accessed=12_000_000, transcendentals=20_000_000),
         name="pairs",
-    )(tgt, counts, got, near_cen, ex_cen, far_cen, f_tab, jnp.asarray(far_sources(), BF), base, q_tab, cheb)
+    )(got, jnp.asarray(far_sources(), BF), *[stay(x) for x in (want, near_cen, ex_cen, far_cen, f_tab, base, q_tab, far_tab)])
 
     terms = exchange(term.reshape(devices, 1, 128))[:, 0, :8]
     curvature = jnp.sum(terms, axis=0) / (devices * boxes * slots)
+    product = pl.pallas_call(
+        finish_kernel,
+        out_shape=table,
+        in_specs=[SMEM] + [vmem()] * 3,
+        out_specs=vmem(),
+        compiler_params=params(8),
+        cost_estimate=pl.CostEstimate(flops=50_000_000, bytes_accessed=3_000_000, transcendentals=0),
+        name="finish",
+    )(counts, stay(near), stay(far), stay(cheb))
     over = jnp.any((served[:, 9] > HALF) & (jnp.arange(devices) % 4 != 0))
     whole = (local_pos, charges, counts, box_centers, far_list, near_list)
     return lax.cond(over, lambda: general(*whole), lambda: (product, curvature))

time: 131 us -> 116 us (0.89)
  local copies, waits for them, and re-layouts: 18.3 us -> 0.08 us
  waiting for transfers between devices: 24.3 us -> 38.3 us
  Pallas kernels: 54.6 us -> 48.3 us
  other arithmetic: 4.77 us -> 1.48 us
    all_to_all x3, waiting for transfers between devices: 24.3 us -> 38.3 us  [exchange(): return lax.all_to_all(x, AXES, split_axis=0, concat_axis=0, tiled=True)]
    reshape x3 -> x0, local copies, waits for them, and re-layouts: 6.16 us -> none  [center_rows(): return jnp.broadcast_to(rows, (n, 8, 2, HALF)).reshape(n, 8, 128)]
    pallas_call x3 -> x5, Pallas kernels: 45.5 us -> 41.2 us  [the longest x1 21.2 us: on_device(): pl.pallas_call(duo_kernel, out_shape=(hbm((boxes, 8, 128), F32), hbm((box...]
    broadcast_in_dim x6 -> x0, local copies, waits for them, and re-layouts: 3.29 us -> none  [center_rows(): return jnp.broadcast_to(rows, (n, 8, 2, HALF)).reshape(n, 8, 128)]
    gather x6 -> x0, local copies, waits for them, and re-layouts: 3 us -> none  [center_rows(): rows = jnp.pad(centers[goals], ((0, 0), (0, 2 - units), (0, 0), (0, 1)))]
    add x2 -> x0, other arithmetic: 2.54 us -> none  [the longest x1 1.72 us: on_device(): moved[0] + moved[1] + moved[2]]
    unnamed x33 -> x20, local copies, waits for them, and re-layouts: 2.41 us -> 0.08 us
    pallas_call x1, Pallas kernels: 6.01 us -> 3.88 us  [on_device(): pl.pallas_call(send_kernel, grid=(devices // group,), out_shape=struct((d...]
  transfers between devices with their start and end apart: 6 -> 6, of which waited for: 3 -> 3; matrix products, arithmetic and copies ran while one was open for 15% -> 1% of each run, Pallas kernels for 11% -> 17%
where the time goes in v3:
time: 116 us
  Pallas kernels  48.3 us (42%)
  waiting for transfers between devices  38.3 us (33%)
  starting transfers between devices  25.8 us (22%)
  other arithmetic  1.48 us (1%)
  between operations  1.48 us (1%)
    all_to_all x3, waiting for transfers between devices, exchange(): return lax.all_to_all(x, AXES, split_axis=0, concat_axis=0, tiled=True)  38.3 us
    pallas_call x1, Pallas kernels, on_device(): pl.pallas_call(duo_kernel, out_shape=(hbm((boxes, 8, 128), F32), hbm((box...  21.2 us
    all_to_all x3, starting transfers between devices, exchange(): return lax.all_to_all(x, AXES, split_axis=0, concat_axis=0, tiled=True)  18.1 us
    pallas_call x1, Pallas kernels, on_device(): pl.pallas_call(own_table_kernel, out_shape=(hbm((boxes, 8, 128), F32), hb...  9.53 us
    ppermute x3, starting transfers between devices, on_device(): lax.ppermute(ex_own, 'gy', [(4 * z, 4 * z + k) for z in range(4)])  7.63 us
    pallas_call x1, Pallas kernels, on_device(): pl.pallas_call(goal_kernel, out_shape=(hbm((devices * 8, 128), F32), hbm(...  3.97 us
    pallas_call x1, Pallas kernels, on_device(): pl.pallas_call(send_kernel, grid=(devices // group,), out_shape=struct((d...  3.88 us
    pallas_call x1, Pallas kernels, on_device(): pl.pallas_call(send_table_kernel, out_shape=(wide, wide), in_specs=[vmem(...  3.74 us
  transfers between devices with their start and end apart: 6, of which 3 were waited for; matrix products, arithmetic and copies ran while one was open for 1% of the time, Pallas kernels for 17%

profile of v3, /device:TPU:1, one launch (start us, length us, event | category | flops | bytes accessed | tf_op | source)
XLA Modules:
  0.0 115.6 jit_solution(16383122789336644817)
XLA Ops:
  0.6 3.2 %start.1 = (s32[128,128]{1,0:T(8,128)}, f32[64,8,128]{2,1,0:T(8,128)S(1)}) custom-call(s32[8,64]{1,0:T(8,128)} %bitcast.61, s32[9,64]{1,0:T(8,128)} %bitcast.59, s32[1,64]{1,0:T(1,128)} %bitcast.62, f32[3,64,128]{2,1,0:T(8,128)} %bitcast.53, f32[64,8,128]{2,1,0:T(8,128)} %charge_ref.5, s32[64]{0:T(128)} %count_ref.7, f32[3,64]{1,0:T(4,128)} %cen_ref.5), custom_call_target="tpu_custom_call" | custom-call | tf_op jit(solution)/shard_map/start/pallas_call | solution.py:779
  3.8 4.0 %collective-permute-start = (f32[64,8,128]{2,1,0:T(8,128)S(1)}, f32[64,8,128]{2,1,0:T(8,128)S(1)}, u32[]{:S(2)}, u32[]{:S(2)}) collective-permute-start(f32[64,8,128]{2,1,0:T(8,128)S(1)} %get-tuple-element.65), channel_id=1, source_target_pairs={{0,1},{4,5},{8,9},{12,13},{16,17},{20,21},{24,25},{28,29},{32,33},... | collective-permute-start | bytes 786440 | tf_op jit(solution)/shard_map/ppermute | solution.py:787
  7.8 2.3 %collective-permute-start.1 = (f32[64,8,128]{2,1,0:T(8,128)S(1)}, f32[64,8,128]{2,1,0:T(8,128)S(1)}, u32[]{:S(2)}, u32[]{:S(2)}) collective-permute-start(f32[64,8,128]{2,1,0:T(8,128)S(1)} %get-tuple-element.65), channel_id=1, source_target_pairs={{0,2},{4,6},{8,10},{12,14},{16,18},{20,22},{24,26},{28,30},{32,34}... | collective-permute-start | bytes 786440 | tf_op jit(solution)/shard_map/ppermute | solution.py:787
  10.2 1.3 %collective-permute-start.2 = (f32[64,8,128]{2,1,0:T(8,128)S(1)}, f32[64,8,128]{2,1,0:T(8,128)S(1)}, u32[]{:S(2)}, u32[]{:S(2)}) collective-permute-start(f32[64,8,128]{2,1,0:T(8,128)S(1)} %get-tuple-element.65), channel_id=1, source_target_pairs={{0,3},{4,7},{8,11},{12,15},{16,19},{20,23},{24,27},{28,31},{32,35}... | collective-permute-start | bytes 786440 | tf_op jit(solution)/shard_map/ppermute | solution.py:787
  11.5 8.3 %all-to-all-start.3 = ((s32[128,1,128]{2,1,0:T(1,128)}), s32[128,1,128]{2,1,0:T(1,128)S(1)}, u32[]{:S(2)}, u32[]{:S(2)}) async-start(s32[128,1,128]{2,1,0:T(1,128)} %bitcast.22), calls=%async_computation.3 | async-start | bytes 131072 | tf_op jit(solution)/shard_map/all_to_all | solution.py:318
  19.8 3.7 %send_tables.1 = (f32[64,16,128]{2,1,0:T(8,128)S(1)}, f32[64,16,128]{2,1,0:T(8,128)S(1)}) custom-call(f32[3,64,128]{2,1,0:T(8,128)} %bitcast.54, f32[64,8,128]{2,1,0:T(8,128)} %charge_ref.5, s32[64]{0:T(128)} %count_ref.7, f32[3,64]{1,0:T(4,128)} %cen_ref.5), custom_call_target="tpu_custom_call" | custom-call | flops 50000000 | bytes 1200000 | tf_op jit(solution)/shard_map/send_tables/pallas_call | solution.py:790
  23.5 0.0 copy-start
  23.6 6.0 %all-to-all-done.3 = s32[128,1,128]{2,1,0:T(1,128)S(1)} async-done(((s32[128,1,128]{2,1,0:T(1,128)}), s32[128,1,128]{2,1,0:T(1,128)S(1)}, u32[]{:S(2)}, u32[]{:S(2)}) %all-to-all-start.3) | async-done | bytes 65568 | tf_op jit(solution)/shard_map/all_to_all | solution.py:318
  29.6 0.0 collective-permute-done
  29.6 0.0 collective-permute-done.1
  29.6 0.0 collective-permute-done.2
  29.6 3.9 %send.1 = f32[128,48,128]{2,1,0:T(8,128)} custom-call(s32[1]{0:T(128)} %bitcast.24.member_ref, s32[128,128]{1,0:T(8,128)S(1)} %bitcast.38, f32[1024,128]{1,0:T(8,128)S(1)} %bitcast.41, f32[1024,128]{1,0:T(8,128)S(1)} %bitcast.40, f32[512,128]{1,0:T(8,128)S(1)} %bitcast.42, f32[512,128]{1,0:T(8,128)S(1)} %bitcast.43, f32[512,128]{1,0:T(8,128)S(1)} %bitcast.44, ...), custom_call_target="tpu_custom_call" | custom-call | tf_op jit(solution)/shard_map/send/pallas_call | solution.py:802
  33.5 0.0 copy-start.1
  33.5 0.0 copy-start.7
  33.5 0.0 copy-start.3
  33.5 0.0 copy-start.9
  33.5 0.0 copy-done
  33.5 4.4 %all-to-all-start.4 = ((f32[128,48,128]{2,1,0:T(8,128)}), f32[128,48,128]{2,1,0:T(8,128)S(1)}, u32[]{:S(2)}, u32[]{:S(2)}) async-start(f32[128,48,128]{2,1,0:T(8,128)} %send.1), calls=%async_computation.4 | async-start | bytes 6291456 | tf_op jit(solution)/shard_map/all_to_all | solution.py:318
  37.9 0.0 copy-start.11
  37.9 0.0 copy-done.1
  37.9 0.0 copy-done.7
  37.9 4.0 %goals.1 = (f32[1024,128]{1,0:T(8,128)}, f32[1024,128]{1,0:T(8,128)}, f32[512,128]{1,0:T(8,128)}) custom-call(s32[128,128]{1,0:T(8,128)} %get-tuple-element.62.want_ref.want_hbm, f32[3,64]{1,0:T(4,128)S(1)} %copy-done.7, f32[8,128]{1,0:T(8,128)S(1)} %copy-done.1), custom_call_target="tpu_custom_call" | custom-call | flops 50000000 | bytes 2000000 | tf_op jit(solution)/shard_map/goals/pallas_call | solution.py:833
  41.9 0.0 copy-done.3
  41.9 0.0 copy-done.9
  41.9 9.5 %own_tables.1 = (f32[64,8,128]{2,1,0:T(8,128)}, bf16[64,2,32,128]{3,2,1,0:T(8,128)(2,1)}, f32[64,8,128]{2,1,0:T(8,128)}, bf16[64,128,128]{2,1,0:T(8,128)(2,1)}) custom-call(f32[3,64,128]{2,1,0:T(8,128)} %bitcast.55, f32[64,8,128]{2,1,0:T(8,128)S(1)} %copy-done.3, s32[64]{0:T(128)S(1)} %copy-done.9), custom_call_target="tpu_custom_call" | custom-call | flops 200000000 | bytes 4000000 | tf_op jit(solution)/shard_map/own_tables/pallas_call | solution.py:818
  51.4 0.2 fusion
  51.6 26.6 %all-to-all-done.4.got_ref = f32[128,48,128]{2,1,0:T(8,128)S(1)} async-done(((f32[128,48,128]{2,1,0:T(8,128)}), f32[128,48,128]{2,1,0:T(8,128)S(1)}, u32[]{:S(2)}, u32[]{:S(2)}) %all-to-all-start.4) | async-done | bytes 3145760 | tf_op jit(solution)/shard_map/all_to_all | solution.py:318
  78.2 0.0 copy-done.11
  78.2 0.0 copy-start.6
  78.2 0.0 copy-start.8
  78.2 0.0 copy-start.10
  78.2 21.2 %pairs.3 = (f32[64,8,128]{2,1,0:T(8,128)}, f32[64,8,128]{2,1,0:T(8,128)}, f32[128,128]{1,0:T(8,128)}) custom-call(f32[128,48,128]{2,1,0:T(8,128)S(1)} %all-to-all-done.4.got_ref, bf16[128,32]{1,0:T(8,128)(2,1)S(1)} %copy-done.11, s32[128,128]{1,0:T(8,128)} %get-tuple-element.62.want_ref.want_hbm, f32[128,8,128]{2,1,0:T(8,128)} %bitcast.64, ...), custom_call_target="tpu_custom_call" | custom-call | flops 1000000000 | bytes 12000000 | tf_op jit(solution)/shard_map/pairs/pallas_call | solution.py:846
  99.4 5.4 %all-to-all-start.5 = ((f32[128,1,128]{2,1,0:T(1,128)}), f32[128,1,128]{2,1,0:T(1,128)S(1)}, u32[]{:S(2)}, u32[]{:S(2)}) async-start(f32[128,1,128]{2,1,0:T(1,128)} %bitcast.35), calls=%async_computation.5 | async-start | bytes 131072 | tf_op jit(solution)/shard_map/all_to_all | solution.py:318
  104.8 0.6 and_reduce_fusion
  106.1 2.8 %finish.1 = f32[64,8,128]{2,1,0:T(8,128)S(1)} custom-call(s32[64]{0:T(128)S(1)} %copy-done.9, f32[64,8,128]{2,1,0:T(8,128)} %get-tuple-element.73.near_ref, f32[64,8,128]{2,1,0:T(8,128)} %get-tuple-element.74.far_ref, bf16[64,128,128]{2,1,0:T(8,128)(2,1)} %get-tuple-element.75.t_ref), custom_call_target="tpu_custom_call" | custom-call | flops 50000000 | bytes 3000000 | tf_op jit(solution)/shard_map/finish/pallas_call | solution.py:876
  108.9 5.7 %all-to-all-done.5 = f32[128,1,128]{2,1,0:T(1,128)S(1)} async-done(((f32[128,1,128]{2,1,0:T(1,128)}), f32[128,1,128]{2,1,0:T(1,128)S(1)}, u32[]{:S(2)}, u32[]{:S(2)}) %all-to-all-start.5) | async-done | bytes 65568 | tf_op jit(solution)/shard_map/all_to_all | solution.py:318
  114.6 0.0 copy-done.6
  114.6 0.0 copy-done.8
  114.6 0.0 copy-done.10
  114.6 0.2 conditional.1
  114.9 0.0 copy-start.5
  114.9 0.2 slice_reduce_fusion
  115.0 0.5 broadcast_multiply_fusion
  115.5 0.0 copy-done.5
Async XLA Ops:
  3.8 25.8 %collective-permute-start = (f32[64,8,128]{2,1,0:T(8,128)S(1)}, f32[64,8,128]{2,1,0:T(8,128)S(1)}, u32[]{:S(2)}, u32[]{:S(2)}) collective-permute-start(f32[64,8,128]{2,1,0:T(8,128)S(1)} %get-tuple-element.65), channel_id=1, source_target_pairs={{0,1},{4,5},{8,9},{12,13},{16,17},{20,21},{24,25},{28,29},{32,33},... | collective-permute-start | bytes 786440 | tf_op jit(solution)/shard_map/ppermute | solution.py:787
  7.8 21.7 %collective-permute-start.1 = (f32[64,8,128]{2,1,0:T(8,128)S(1)}, f32[64,8,128]{2,1,0:T(8,128)S(1)}, u32[]{:S(2)}, u32[]{:S(2)}) collective-permute-start(f32[64,8,128]{2,1,0:T(8,128)S(1)} %get-tuple-element.65), channel_id=1, source_target_pairs={{0,2},{4,6},{8,10},{12,14},{16,18},{20,22},{24,26},{28,30},{32,34}... | collective-permute-start | bytes 786440 | tf_op jit(solution)/shard_map/ppermute | solution.py:787
  10.2 19.4 %collective-permute-start.2 = (f32[64,8,128]{2,1,0:T(8,128)S(1)}, f32[64,8,128]{2,1,0:T(8,128)S(1)}, u32[]{:S(2)}, u32[]{:S(2)}) collective-permute-start(f32[64,8,128]{2,1,0:T(8,128)S(1)} %get-tuple-element.65), channel_id=1, source_target_pairs={{0,3},{4,7},{8,11},{12,15},{16,19},{20,23},{24,27},{28,31},{32,35}... | collective-permute-start | bytes 786440 | tf_op jit(solution)/shard_map/ppermute | solution.py:787
  11.5 18.1 %all-to-all-start.3 = ((s32[128,1,128]{2,1,0:T(1,128)}), s32[128,1,128]{2,1,0:T(1,128)S(1)}, u32[]{:S(2)}, u32[]{:S(2)}) async-start(s32[128,1,128]{2,1,0:T(1,128)} %bitcast.22), calls=%async_computation.3 | async-start | bytes 131072 | tf_op jit(solution)/shard_map/all_to_all | solution.py:318
  23.5 10.0 %copy-start = (f32[64,16,128]{2,1,0:T(8,128)}, f32[64,16,128]{2,1,0:T(8,128)S(1)}, u32[]{:S(2)}) copy-start(f32[64,16,128]{2,1,0:T(8,128)S(1)} %get-tuple-element.64.w_hbm) | copy-start | bytes 1572868
  33.5 4.5 %copy-start.1 = (f32[8,128]{1,0:T(8,128)S(1)}, f32[8,128]{1,0:T(8,128)}, u32[]{:S(2)}) copy-start(f32[8,128]{1,0:T(8,128)} %constant.55.clone.node_ref) | copy-start | bytes 12292
  33.5 4.5 %copy-start.7 = (f32[3,64]{1,0:T(4,128)S(1)}, f32[3,64]{1,0:T(4,128)}, u32[]{:S(2)}) copy-start(f32[3,64]{1,0:T(4,128)} %cen_ref.5) | copy-start | bytes 2308
  33.5 8.4 %copy-start.3 = (f32[64,8,128]{2,1,0:T(8,128)S(1)}, f32[64,8,128]{2,1,0:T(8,128)}, u32[]{:S(2)}) copy-start(f32[64,8,128]{2,1,0:T(8,128)} %charge_ref.5) | copy-start | bytes 786436
  33.5 8.4 %copy-start.9 = (s32[64]{0:T(128)S(1)}, s32[64]{0:T(128)}, u32[]{:S(2)}) copy-start(s32[64]{0:T(128)} %count_ref.7) | copy-start | bytes 772
  33.5 44.7 %all-to-all-start.4 = ((f32[128,48,128]{2,1,0:T(8,128)}), f32[128,48,128]{2,1,0:T(8,128)S(1)}, u32[]{:S(2)}, u32[]{:S(2)}) async-start(f32[128,48,128]{2,1,0:T(8,128)} %send.1), calls=%async_computation.4 | async-start | bytes 6291456 | tf_op jit(solution)/shard_map/all_to_all | solution.py:318
  37.9 40.3 %copy-start.11 = (bf16[128,32]{1,0:T(8,128)(2,1)S(1)}, bf16[128,32]{1,0:T(8,128)(2,1)}, u32[]{:S(2)}) copy-start(bf16[128,32]{1,0:T(8,128)(2,1)} %constant.56.clone.fn_ref) | copy-start | bytes 24580
  78.2 36.4 %copy-start.6 = (s32[64,9]{0,1:T(8,128)S(1)}, s32[64,9]{0,1:T(8,128)}, u32[]{:S(2)}) copy-start(s32[64,9]{0,1:T(8,128)} %param.17) | copy-start | bytes 6916
  78.2 36.4 %copy-start.8 = (s32[64,8]{0,1:T(8,128)S(1)}, s32[64,8]{0,1:T(8,128)}, u32[]{:S(2)}) copy-start(s32[64,8]{0,1:T(8,128)} %param.16) | copy-start | bytes 6148
  78.2 36.4 %copy-start.10 = (f32[1,8,128]{2,1,0:T(8,128)S(1)}, f32[1,8,128]{2,1,0:T(8,128)}, u32[]{:S(2)}) copy-start(f32[1,8,128]{2,1,0:T(8,128)} %constant.57.clone) | copy-start | bytes 12292
  99.4 15.2 %all-to-all-start.5 = ((f32[128,1,128]{2,1,0:T(1,128)}), f32[128,1,128]{2,1,0:T(1,128)S(1)}, u32[]{:S(2)}, u32[]{:S(2)}) async-start(f32[128,1,128]{2,1,0:T(1,128)} %bitcast.35), calls=%async_computation.5 | async-start | bytes 131072 | tf_op jit(solution)/shard_map/all_to_all | solution.py:318
  114.9 0.7 copy-start.5

commit v4 on v3

--- a/solution.py
+++ b/solution.py
@@ -400,60 +400,71 @@
 
 
 HALF = 64
-ROWS = 48
+ROWS = 44
+NEAR_ROWS = 24
 UNROLL = 4
 
 
-def start_kernel(far_ref, near_ref, most_ref, pos_ref, charge_ref, count_ref, cen_ref, want_ref, ex_ref):
+def start_kernel(far_ref, near_ref, most_ref, pos_ref, charge_ref, count_ref, cen_ref, row_ref, msg_ref, want_ref, ex_ref):
     boxes = far_ref.shape[1]
     slots = far_ref.shape[0]
-    sub = iota((8, 128), 0)
     lane = iota((8, 128), 1)
     left = lane < HALF
+    for d in range(3):
+        center = jnp.concatenate([row_ref[...], jnp.zeros((5, boxes), F32)], axis=0)
+        center = jnp.concatenate([center, jnp.zeros((8, 128 - boxes), F32)], axis=1)
+        center = jnp.concatenate([center, jnp.zeros((120, 128), F32)], axis=0).T[:boxes, d : d + 1]
+        ex_ref[pl.ds(d, boxes, stride=8), :] = center + 0.5 * pos_ref[d]
+    for d in range(3, 8):
+        ex_ref[pl.ds(d, boxes, stride=8), :] = jnp.zeros((boxes, 128), F32)
 
     def body(b, carry):
-        live = lane < count_ref[b]
-        q = pltpu.roll(jnp.where(live, charge_ref[b], 0.0), HALF, 1)
-        point = jnp.zeros((8, 128), F32)
-        for d in range(3):
-            row = jnp.broadcast_to(pos_ref[d, pl.ds(b, 1), :], (8, 128))
-            point = jnp.where(sub == d, cen_ref[d, b] + 0.5 * row, point)
-        ex_ref[b] = jnp.where(left, q, point)
+        q = pltpu.roll(jnp.where(lane < count_ref[b], charge_ref[b], 0.0), HALF, 1)
+        at = pl.ds(pl.multiple_of(8 * b, 8), 8)
+        ex_ref[at, :] = jnp.where(left, q, ex_ref[at, :])
         return carry
 
-    lax.fori_loop(0, boxes, body, 0, unroll=8)
+    lax.fori_loop(0, boxes, body, 0, unroll=16)
 
     peer = iota((128, 128), 0)
     line = iota((128, 128), 1)
     tri = (peer < line).astype(F32).astype(BF)
+    full = jnp.ones((128, 128), BF)
     row32 = iota((32, 128), 0)
+    kind = row32 // 4
     boxrow = iota((32, 128), 1) % boxes
     result = jnp.zeros((128, 32), F32)
-    for ref, first, base in ((near_ref, 1, 0), (far_ref, 0, 4)):
-        seen = jnp.zeros((128, 1), F32)
+    for ref, first, group in ((near_ref, 1, 0), (far_ref, 0, 1)):
+        seen = jnp.zeros((128, 128), F32)
         for j in range(0, slots, 2):
             flat = jnp.concatenate([ref[first + j : first + j + 1, :], ref[first + j + 1 : first + j + 2, :]], axis=1)
             hit = jnp.broadcast_to(flat // boxes, (128, 128)) == peer
-            ones = hit.astype(F32)
-            onehot = ones.astype(BF)
+            onehot = hit.astype(F32).astype(BF)
             before = dot(onehot, tri) + seen
             rank = jnp.sum(jnp.where(hit, before, 0.0), axis=0, keepdims=True).astype(jnp.int32)
-            seen = seen + jnp.sum(ones, axis=1, keepdims=True)
-            within = jnp.broadcast_to(flat % boxes * 16, (32, 128))
-            mine = row32 % 4 == jnp.broadcast_to(rank, (32, 128))
-            value = jnp.where(row32 // 4 == base // 4, within, jnp.where(row32 // 4 == base // 4 + 4, boxrow, 0))
-            value = jnp.where(mine, value, 0).astype(F32).astype(BF)
+            if j + 2 < slots:
+                seen = seen + dot(onehot, full)
+            within = jnp.broadcast_to(flat % boxes, (32, 128))
+            if group == 0:
+                value = jnp.where(kind == 0, within * NEAR_ROWS, jnp.where(kind == 2, within * 8, 0))
+            else:
+                value = jnp.where(kind == 1, within * 8, 0)
+            value = jnp.where(kind == 4 + group, boxrow, value)
+            value = jnp.where(row32 % 4 == jnp.broadcast_to(rank, (32, 128)), value, 0).astype(F32).astype(BF)
             result = result + dot(onehot, value, NT)
     result = jnp.concatenate([result, jnp.zeros((128, 96), F32)], axis=1)
-    member = peer % 4
-    moved = [result] + [pltpu.roll(result, y, 0) for y in range(1, 4)]
-    for at, base, scale in ((8, 0, 0.5), (24, 16, 1.0)):
-        extra = jnp.zeros((128, 1), F32)
-        for y in range(4):
-            extra = jnp.where(member[:, 0:1] == y, moved[y][:, base + y : base + y + 1], extra)
-        result = jnp.where(line == at, jnp.broadcast_to(scale * extra, (128, 128)), result)
-    most = jnp.max(most_ref[...], axis=1, keepdims=True)
-    want_ref[...] = jnp.where(line == 9, jnp.broadcast_to(most, (128, 128)), result.astype(jnp.int32))
+    heavy = (line == peer - peer % 4).astype(F32).astype(BF)
+    first = dot(heavy, result.astype(BF))
+    for at, base in ((8, 8), (24, 16)):
+        extra = dot(jnp.where(line == base + peer % 4, first, 0.0).astype(BF), full)
+        result = jnp.where(line == at, extra, result)
+    most = jnp.max(most_ref[...], axis=1, keepdims=True).astype(F32)
+    result = jnp.where(line == 9, jnp.broadcast_to(most, (128, 128)), result)
+    want_ref[...] = result.astype(jnp.int32)
+    rows = [jnp.concatenate([row_ref[d : d + 1, :]] * 2, axis=1) for d in range(3)]
+    rows = [jnp.broadcast_to(row, (128, 128)) for row in rows]
+    msg_ref[pl.ds(0, 128, stride=2), :] = jnp.where(line < HALF, result, rows[2])
+    msg_ref[pl.ds(1, 128, stride=2), :] = jnp.where(line < HALF, rows[0], rows[1])
 
 
 def cheb_rows(x):
@@ -483,22 +494,33 @@
     return jnp.where(iota((8, 128), 1) < HALF, x, pltpu.roll(x, HALF, 1))
 
 
-def send_table_kernel(pos_ref, charge_ref, count_ref, cen_ref, near_ref, far_ref):
+def send_table_kernel(pos_ref, charge_ref, count_ref, cen_ref, near_ref, far_ref, basis_ref):
     boxes = charge_ref.shape[0]
     lane = iota((8, 128), 1)
-    sub4 = iota((8, 128), 0) % 4
+    sub = iota((8, 128), 0)
+    for d in range(3):
+        x = pos_ref[d]
+        second = 2.0 * x * x - 1.0
+        third = 2.0 * x * second - x
+        for i in range(NODES):
+            theta = (2 * i + 1) * math.pi / 8
+            value = math.cos(theta) * x + math.cos(2 * theta) * second + math.cos(3 * theta) * third
+            basis_ref[4 * d + i] = 0.25 + 0.5 * value
 
     def body(b, carry):
         q = jnp.where(lane < count_ref[b], charge_ref[b], 0.0)
         near_ref[b, 0:8] = doubled(q)
-        x = point_rows(pos_ref, b)
-        cx, cy, cz = cen_ref[0, b], cen_ref[1, b], cen_ref[2, b]
-        center = jnp.where(sub4 == 0, cx, jnp.where(sub4 == 1, cy, cz))
-        near_ref[b, 8:16] = doubled(center + 0.5 * x)
+        x, y, z = [doubled(cen_ref[d, b] + 0.5 * jnp.broadcast_to(pos_ref[d, pl.ds(b, 1), :], (8, 128))) for d in range(3)]
+        near_ref[b, 8:16] = jnp.where(sub == 4, x, jnp.where(sub == 5, y, z))
+        near_ref[b, 16:24] = jnp.where(sub == 7, x, jnp.where((sub == 3) | (sub == 5), y, z))
+        row = lambda i, d: jnp.broadcast_to(basis_ref[4 * d + i, pl.ds(b, 1), :], (8, 128))
+        sub4 = sub % 4
+        zs = jnp.where(sub4 == 0, row(0, 2), jnp.where(sub4 == 1, row(1, 2), jnp.where(sub4 == 2, row(2, 2), row(3, 2))))
+        ys = [jnp.where(sub < 4, row(0, 1), row(1, 1)) * zs, jnp.where(sub < 4, row(2, 1), row(3, 1)) * zs]
+        table = jnp.concatenate([row(i, 0) * ys[j] for i in range(NODES) for j in range(2)], axis=0)
         qs = jnp.concatenate(split(q), axis=0)
-        weight = fold(dot(qs, stack_kernel(cheb_rows(x)), NT))
-        far_ref[b, 0:8] = weight + pltpu.roll(weight, 64, 1)
-        far_ref[b, 8:16] = jnp.where(lane % 4 == 0, cx, jnp.where(lane % 4 == 1, cy, cz))
+        weight = fold(dot(qs, stack_kernel(table), NT))
+        far_ref[b] = weight + pltpu.roll(weight, 64, 1)
         return carry
 
     lax.fori_loop(0, boxes, body, 0, unroll=8)
@@ -529,36 +551,49 @@
     lax.fori_loop(0, boxes, body, 0, unroll=4)
 
 
-def goal_kernel(want_ref, cen_ref, node_ref, nc_ref, fc_ref, ec_ref, odd_ref):
+def goal_kernel(want_ref, served_ref, cen_ref, node_ref, nc_ref, fc_ref, ec_ref, odd_ref):
     lane = iota((128, 128), 1)
     left = lane < HALF
     boxes = cen_ref.shape[1]
     cen = jnp.concatenate([cen_ref[...], jnp.zeros((5, boxes), F32)], axis=0)
     cen = jnp.concatenate([cen, jnp.zeros((8, 128 - boxes), F32)], axis=1)
     cen = jnp.concatenate([cen, jnp.zeros((120, 128), F32)], axis=0).T
-    high, rest = split(cen)
-    rest = cen - high.astype(F32)
-    mid, low = split(rest)
-    parts = jnp.concatenate([high, mid, low], axis=0)
+
+    def split3(x, axis):
+        high = x.astype(BF)
+        rest = x - high.astype(F32)
+        mid = rest.astype(BF)
+        return jnp.concatenate([high, mid, (rest - mid.astype(F32)).astype(BF)], axis=axis)
+
+    parts = split3(cen, 0)
     want = want_ref[...]
+    sources = [served_ref[pl.ds(1, 128, stride=2), :], served_ref[pl.ds(0, 128, stride=2), :]]
+    halves = [jnp.concatenate([(iota((128, 128), 0) // HALF == h).astype(F32).astype(BF)] * 3, axis=0) for h in range(2)]
+
+    def column(at):
+        return jnp.broadcast_to(want[:, at : at + 1], (128, 128))
 
     def centers(at):
-        goal = jnp.broadcast_to(want[:, at : at + 1], (128, 128))
-        onehot = (goal == lane).astype(F32).astype(BF)
+        onehot = (column(at) == lane).astype(F32).astype(BF)
         found = dot(jnp.concatenate([onehot] * 3, axis=1), parts)
         return [jnp.broadcast_to(found[:, d : d + 1], (128, 128)) for d in range(3)]
+
+    def gaps(j):
+        mine = lane % HALF == column(4 + j) // 8
+        both = [split3(jnp.where(mine, source, 0.0), 1) for source in sources]
+        theirs = [dot(both[0], halves[0]), dot(both[0], halves[1]), dot(both[1], halves[1])]
+        return [a - b for a, b in zip(centers(20 + j), theirs)]
 
     nc_ref[...] = jnp.zeros_like(nc_ref)
     fc_ref[...] = jnp.zeros_like(fc_ref)
     ec_ref[...] = jnp.zeros_like(ec_ref)
-    for ref, base in ((nc_ref, 16), (fc_ref, 20)):
-        for u in range(2):
-            first, second = centers(base + 2 * u), centers(base + 2 * u + 1)
-            for d in range(3):
-                row = jnp.where(left, first[d], second[d])
-                if base == 20:
-                    row = row + node_ref[d : d + 1, :]
-                ref[pl.ds(4 * u + d, 128, stride=8), :] = row
+    for u in range(2):
+        first, second = centers(16 + 2 * u), centers(17 + 2 * u)
+        for d in range(3):
+            nc_ref[pl.ds(4 * u + d, 128, stride=8), :] = jnp.where(left, first[d], second[d])
+        first, second = gaps(2 * u), gaps(2 * u + 1)
+        for d in range(3):
+            fc_ref[pl.ds(4 * u + d, 128, stride=8), :] = jnp.where(left, first[d], second[d]) + node_ref[d : d + 1, :]
     extra = centers(24)
     for d in range(3):
         odd_ref[...] = extra[d]
@@ -566,60 +601,83 @@
         ec_ref[pl.ds(d, 64, stride=8), :] = jnp.where(left[:64], even, odd)
 
 
+def far_kernel(fc_ref, fn_ref, out_ref):
+    group = fc_ref.shape[0]
+    tgt = jnp.concatenate(planes(fc_ref[...] * ROOT3, False), axis=1).astype(BF)
+    for k in range(group):
+        out_ref[k] = stack_kernel(matern(dot(fn_ref[...], tgt[k])))
+
+
 def send_kernel(member_ref, served_ref, near_ref, far_ref, own_ref, *refs):
-    moved, (out_ref, ids_ref, ex_ref, sem) = refs[:3], refs[3:]
-    step = pl.program_id(0)
-    group = out_ref.shape[0]
-    sub4 = iota((8, 128), 0) % 4
-    top = iota((8, 128), 0) < 4
+    moved, (out_ref, ids_ref, int_ref, ex_ref, buf_ref, sems) = refs[:3], refs[3:]
+    peers = ids_ref.shape[0]
+    sub = iota((8, 128), 0)
     lane = iota((8, 128), 1)
     left = lane < HALF
-
-    @pl.when(step == 0)
+    keep = left | (sub < 3)
+    second = sub < 5
+    int_ref[...] = served_ref[pl.ds(0, peers, stride=2), :].astype(jnp.int32)
+    copy = pltpu.make_async_copy(int_ref, ids_ref, sems.at[0])
+    copy.start()
+    ex_ref[...] = moved[0][...] + moved[1][...] + moved[2][...]
+
+    @pl.when(member_ref[0] == 0)
     def _():
-        copy = pltpu.make_async_copy(served_ref, ids_ref, sem)
-        copy.start()
-        ex_ref[...] = moved[0][...] + moved[1][...] + moved[2][...]
-
-        @pl.when(member_ref[0] == 0)
-        def _():
-            ex_ref[...] = own_ref[...]
-
+        ex_ref[...] = own_ref[...]
+
+    copy.wait()
+
+    def body(i, carry):
+        base = pl.multiple_of(i * 2 * ROWS, 8)
+        for k in range(2):
+            peer = 2 * i + k
+            at = lambda row: pl.ds(base + (k * ROWS + row), 8)
+            rows = lambda ref, j, row: ref[pl.ds(pl.multiple_of(ids_ref[peer, j], 8) + row, 8), :]
+            q = [rows(near_ref, j, 0) for j in range(4)]
+            w = [rows(far_ref, 4 + j, 0) for j in range(4)]
+            p = [rows(near_ref, j, 16 if j < 2 else 8) for j in range(4)]
+            buf_ref[at(0), :] = jnp.where(left, q[0], q[1])
+            buf_ref[at(8), :] = jnp.where(left, q[2], q[3])
+            buf_ref[at(16), :] = jnp.where(left, w[0], w[2])
+            buf_ref[at(24), :] = jnp.where(left, w[1], w[3])
+            buf_ref[at(36), :] = jnp.where(sub == 7, jnp.where(left, p[0], p[1]), jnp.where(left, p[2], p[3]))
+            buf_ref[at(32), :] = jnp.where(keep, rows(ex_ref, 8, 0), jnp.where(second, p[1], p[0]))
+        return carry
+
+    chunks = 4
+    each = peers // chunks
+    stores = []
+    for c in range(chunks):
+        lax.fori_loop(c * each // 2, (c + 1) * each // 2, body, 0, unroll=8)
+        at = pl.ds(c * each * ROWS, each * ROWS)
+        stores.append(pltpu.make_async_copy(buf_ref.at[at], out_ref.at[at], sems.at[1 + c]))
+        stores[-1].start()
+    for copy in stores:
         copy.wait()
 
-    def body(k, carry):
-        peer = step * group + k
-        rows = lambda ref, j, at, size: ref[pl.ds(pl.multiple_of(ids_ref[peer, j], size) + at, 8), :]
-        q = [rows(near_ref, j, 0, 16) for j in range(4)]
-        s = [rows(near_ref, j, 8, 16) for j in range(4)]
-        w = [rows(far_ref, 4 + j, 0, 16) for j in range(4)]
-        c = [rows(far_ref, 4 + j, 8, 16) for j in range(4)]
-        out_ref[k, 0:8] = jnp.where(left, q[0], q[1])
-        out_ref[k, 8:16] = jnp.where(left, q[2], q[3])
-        out_ref[k, 16:24] = jnp.where(left, w[0], w[2])
-        out_ref[k, 24:32] = jnp.where(left, w[1], w[3])
-        out_ref[k, 32:40] = rows(ex_ref, 8, 0, 8)
-        centers = jnp.where(left, jnp.where(lane < 4, c[0], c[2]), jnp.where(lane < 68, c[1], c[3]))
-        points = jnp.where(top, jnp.where(left, s[0], s[1]), jnp.where(left, s[2], s[3]))
-        out_ref[k, 40:48] = jnp.where(sub4 == 3, centers, points)
-        return carry
-
-    lax.fori_loop(0, group, body, 0, unroll=16)
-
 
 def duo_kernel(
-    got_ref, fn_ref, want_hbm, nc_hbm, ec_hbm, fc_hbm, f_hbm, base_hbm, q_hbm, w_hbm, near_hbm, far_hbm, term_ref,
-    tgt_ref, nc_ref, ec_ref, fc_ref, f_ref, base_ref, q_ref, w_ref, near_ref, far_ref, sems, ft_ref, *bufs
+    got_ref, want_hbm, nc_hbm, ec_hbm, f_hbm, base_hbm, q_hbm, w_hbm, v_hbm, near_hbm, far_hbm, term_ref,
+    tgt_ref, nc_ref, ec_ref, f_ref, base_ref, q_ref, w_ref, v_ref, near_ref, far_ref, sems, *bufs
 ):
-    whole = [(fc_hbm, fc_ref), (want_hbm, tgt_ref), (nc_hbm, nc_ref), (ec_hbm, ec_ref), (f_hbm, f_ref)]
+    whole = [(want_hbm, tgt_ref), (nc_hbm, nc_ref), (ec_hbm, ec_ref), (f_hbm, f_ref)]
     whole += [(base_hbm, base_ref), (q_hbm, q_ref), (w_hbm, w_ref)]
     loads = [pltpu.make_async_copy(source, target, sems.at[i]) for i, (source, target) in enumerate(whole)]
-    for copy in loads:
+    for copy in loads[:4]:
         copy.start()
-    xt_refs, dist_refs, value_refs = bufs[:2], (bufs[2:9], bufs[9:16]), (bufs[16:23], bufs[23:30])
-    near_accs, far_accs = bufs[30:32], bufs[32:34]
-    peers = got_ref.shape[0]
-    duos = peers // 2
+    chunk = v_ref.shape[0] // 4
+
+    def far_values(c):
+        at = pl.ds(c * chunk, chunk)
+        return pltpu.make_async_copy(v_hbm.at[at], v_ref.at[at], sems.at[16 + c])
+
+    for c in range(4):
+        far_values(c).start()
+    for copy in loads[4:]:
+        copy.start()
+    xt_refs, dist_refs, value_refs = bufs[:2], (bufs[2:7], bufs[7:12]), (bufs[12:17], bufs[17:22])
+    near_accs, far_accs = bufs[22:24], bufs[24:26]
+    duos = ec_ref.shape[0]
     boxes = f_ref.shape[0]
     sub = iota((8, 128), 0)
     lane = iota((8, 128), 1)
@@ -628,29 +686,11 @@
         ref[...] = jnp.zeros_like(ref)
     for ref in dist_refs[1]:
         ref[...] = jnp.full(ref.shape, 1e6, F32)
-    spread = (iota((128, 128), 0) // 64 == iota((128, 128), 1) // 64).astype(F32).astype(BF)
-
-    batch = 16
-    mask = iota((batch, 8, 128), 2) % 64 == iota((batch, 8, 128), 1)
-
-    def far_body(g, carry):
-        at = pl.ds(g * batch, batch)
-        rows = got_ref[at, 40:48, :]
-        rows = jnp.where(mask, jnp.broadcast_to(rows[:, 3:4, :], rows.shape), 0.0).reshape(batch * 8, 128)
-        high = rows.astype(BF)
-        rest = rows - high.astype(F32)
-        mid = rest.astype(BF)
-        low = (rest - mid.astype(F32)).astype(BF)
-        cen = dot(high, spread) + dot(mid, spread) + dot(low, spread)
-        rel = (fc_ref[at] - cen.reshape(batch, 8, 128)) * ROOT3
-        ft_ref[at] = jnp.concatenate(planes(rel, False), axis=1).astype(BF)
-        return carry
-
-    loads[0].wait()
-    lax.fori_loop(0, peers // batch, far_body, 0, unroll=2)
+    def tile(duo, a, row):
+        return got_ref[pl.ds(pl.multiple_of(duo * 2 * ROWS, 8) + (a * ROWS + row), 8), :]
 
     def extra(duo):
-        return got_ref[2 * duo, 32:40], got_ref[2 * duo + 1, 32:40]
+        return tile(duo, 0, 32), tile(duo, 1, 32)
 
     def goals(duo):
         pairs = [(tgt_ref[2 * duo + k // 2, 16 + 2 * (k % 2)], tgt_ref[2 * duo + k // 2, 17 + 2 * (k % 2)]) for k in range(4)]
@@ -663,26 +703,28 @@
 
     def products(duo, value):
         ex = extra(duo)
-        tiles = [got_ref[2 * duo + k // 2, 8 * (k % 2) : 8 * (k % 2) + 8] for k in range(4)]
+        tiles = [tile(duo, k // 2, 8 * (k % 2)) for k in range(4)]
         tiles.append(jnp.where(left, ex[0], pltpu.roll(ex[1], HALF, 1)))
         for k, goal in enumerate(goals(duo)):
             qs = jnp.concatenate(halves(tiles[k]), axis=0).astype(BF)
             new = dot(jnp.concatenate([qs, qs], axis=1), value[k][...])
             for h in range(2):
                 near_accs[h][goal[h]] += fold(new[16 * h : 16 * h + 16])
+
+    def far_products(duo):
         for a in range(2):
             ws = []
             for h in range(2):
-                ws += halves(got_ref[2 * duo + a, 16 + 8 * h : 24 + 8 * h])
+                ws += halves(tile(duo, a, 16 + 8 * h))
             ws = jnp.concatenate(ws, axis=0).astype(BF)
-            new = dot(jnp.concatenate([ws, ws], axis=1), value[5 + a][...])
+            new = dot(jnp.concatenate([ws, ws], axis=1), v_ref[2 * duo + a])
             for h in range(2):
                 for u in range(2):
                     at = 32 * h + 16 * u
                     far_accs[h][tgt_ref[2 * duo + a, 20 + 2 * u + h]] += fold(new[at : at + 16])
 
     def values(dist, value):
-        for k in range(7):
+        for k in range(5):
             value[k][...] = stack_kernel(matern(dist[k][...]))
 
     def distances(duo, xt, dist):
@@ -693,38 +735,47 @@
                 pieces += [f_ref[goal[half], u], jnp.zeros((96 - 32 * v, 128), BF)]
                 at = slice(64 * half, 64 * half + 64)
                 dist[k][at, :] = dot(xt[at, :], jnp.concatenate(pieces, axis=0))
-        for a in range(2):
-            dist[5 + a][...] = dot(fn_ref[...], ft_ref[2 * duo + a])
 
     def features(duo, xt):
         ex = extra(duo)
+        turned = [pltpu.roll(x, HALF, 1) for x in ex]
         feats = []
         for a in range(2):
-            feats += planes((got_ref[2 * duo + a, 40:48] - nc_ref[2 * duo + a]) * ROOT3, True)
-        point = jnp.where(left, pltpu.roll(ex[0], HALF, 1), ex[1])
+            full = tile(duo, a, 36)
+            split_rows = jnp.where(left, pltpu.roll(turned[a], 4, 0), pltpu.roll(ex[a], 6, 0))
+            point = jnp.where(sub >= 4, full, jnp.where(sub == 0, pltpu.roll(full, 1, 0), split_rows))
+            feats += planes((point - nc_ref[2 * duo + a]) * ROOT3, True)
+        point = jnp.where(left, turned[0], ex[1])
         feats += planes((point - ec_ref[duo]) * ROOT3, True)
         feats.append(jnp.zeros((32, 128), F32))
         xt[...] = jnp.concatenate(feats, axis=0).T.astype(BF)
 
+    turns = duos // UNROLL
+
     def body(i, carry):
+        @pl.when(i % (turns // 4) == 0)
+        def _():
+            far_values(i // (turns // 4)).wait()
+
         for s in range(UNROLL):
             now, was = s % 2, 1 - s % 2
             step = UNROLL * i + s
             products(jnp.maximum(step - 2, 0), value_refs[was])
+            far_products(step)
             values(dist_refs[was], value_refs[now])
             distances(step, xt_refs[was], dist_refs[now])
             features(jnp.minimum(step + 1, duos - 1), xt_refs[now])
         return carry
 
-    for copy in loads[1:5]:
+    for copy in loads[:4]:
         copy.wait()
     features(0, xt_refs[1])
-    lax.fori_loop(0, duos // UNROLL, body, 0)
+    lax.fori_loop(0, turns, body, 0)
     products(duos - 2, value_refs[1])
     values(dist_refs[1], value_refs[0])
     products(duos - 1, value_refs[0])
 
-    for copy in loads[5:]:
+    for copy in loads[4:]:
         copy.wait()
 
     def finish(b, total):
@@ -732,7 +783,7 @@
         far = jnp.where(left, far_accs[0][b], far_accs[1][b])
         near_ref[b] = near
         far_ref[b] = far
-        return total + near * q_ref[b] + far * w_ref[b, 0:8]
+        return total + near * q_ref[b] + far * w_ref[b]
 
     total = jnp.zeros((8, 128), F32)
     stores = []
@@ -769,51 +820,51 @@
     devices = lax.axis_size("gx") * lax.axis_size("gy")
     boxes, _, slots = local_pos.shape
     struct = jax.ShapeDtypeStruct
-    pos = jnp.transpose(local_pos, (1, 0, 2))
-    table = struct((boxes, 8, 128), F32)
     hbm = pltpu.HBM
     stay = lambda x: pltpu.with_memory_space_constraint(x, pltpu.HBM)
     anywhere = pl.BlockSpec(memory_space=pltpu.HBM)
-    wide = struct((boxes, 16, 128), F32)
+    pos = jnp.transpose(local_pos, (1, 0, 2))
+    table = struct((boxes, 8, 128), F32)
+    flat = lambda x: x.reshape(-1, 128)
     member = (lax.axis_index("gy") % 4).astype(jnp.int32).reshape(1)
-    want, ex_own = pl.pallas_call(
+    msg, want, ex_own = pl.pallas_call(
         start_kernel,
-        out_shape=(struct((devices, 128), jnp.int32), table),
-        in_specs=[vmem(), vmem(), vmem(), vmem(), vmem(), SMEM, SMEM],
-        out_specs=(vmem(), vmem()),
+        out_shape=(struct((devices * 2, 128), F32), struct((devices, 128), jnp.int32), struct((boxes * 8, 128), F32)),
+        in_specs=[vmem()] * 5 + [SMEM, SMEM, vmem()],
+        out_specs=(vmem(), vmem(), vmem()),
         compiler_params=params(8),
         name="start",
-    )(far_list.T, near_list.T, counts.reshape(1, boxes), pos, charges, counts, box_centers)
+    )(far_list.T, near_list.T, counts.reshape(1, boxes), pos, charges, counts, box_centers, box_centers)
     moved = [lax.ppermute(ex_own, "gy", [(4 * z, 4 * z + k) for z in range(4)]) for k in range(1, 4)]
-    served = exchange(want.reshape(devices, 1, 128)).reshape(devices, 128)
+    served = flat(exchange(msg.reshape(devices, 2, 128)))
 
     near_tab, far_tab = pl.pallas_call(
         send_table_kernel,
-        out_shape=(wide, wide),
+        out_shape=(struct((boxes, NEAR_ROWS, 128), F32), table),
         in_specs=[vmem(), vmem(), SMEM, SMEM],
         out_specs=(vmem(), vmem()),
+        scratch_shapes=[pltpu.VMEM((12, boxes, 128), F32)],
         compiler_params=params(8),
         cost_estimate=pl.CostEstimate(flops=50_000_000, bytes_accessed=1_200_000, transcendentals=0),
         name="send_tables",
     )(pos, charges, counts, box_centers)
 
-    group = 64
-    flat = lambda x: x.reshape(-1, 128)
     send = pl.pallas_call(
         send_kernel,
-        grid=(devices // group,),
-        out_shape=struct((devices, ROWS, 128), F32),
-        in_specs=[SMEM, pl.BlockSpec(memory_space=pl.ANY)] + [vmem()] * 6,
-        out_specs=vmem((group, ROWS, 128), lambda i: (i, 0, 0)),
+        out_shape=hbm((devices * ROWS, 128), F32),
+        in_specs=[SMEM] + [vmem()] * 7,
+        out_specs=anywhere,
         scratch_shapes=[
             pltpu.SMEM((devices, 128), jnp.int32),
+            pltpu.VMEM((devices, 128), jnp.int32),
             pltpu.VMEM((boxes * 8, 128), F32),
-            pltpu.SemaphoreType.DMA(()),
+            pltpu.VMEM((devices * ROWS, 128), F32),
+            pltpu.SemaphoreType.DMA((5,)),
         ],
         compiler_params=params(12),
         name="send",
-    )(member, served, flat(near_tab), flat(far_tab), flat(ex_own), *[flat(x) for x in moved])
-    got = exchange(send)
+    )(member, served, flat(near_tab), flat(far_tab), ex_own, *moved)
+    got = flat(exchange(send.reshape(devices, ROWS // 4, 4, 128)))
 
     q_tab, f_tab, base, cheb = pl.pallas_call(
         own_table_kernel,
@@ -830,46 +881,56 @@
         name="own_tables",
     )(pos, charges, counts)
 
-    near_cen, far_cen, ex_cen = pl.pallas_call(
+    near_cen, far_gap, ex_cen = pl.pallas_call(
         goal_kernel,
         out_shape=(hbm((devices * 8, 128), F32), hbm((devices * 8, 128), F32), hbm((devices * 4, 128), F32)),
-        in_specs=[vmem()] * 3,
+        in_specs=[vmem()] * 4,
         out_specs=(vmem(), vmem(), vmem()),
         scratch_shapes=[pltpu.VMEM((128, 128), F32)],
         compiler_params=params(8),
         cost_estimate=pl.CostEstimate(flops=50_000_000, bytes_accessed=2_000_000, transcendentals=0),
         name="goals",
-    )(want, box_centers, jnp.asarray(node_rows()))
-    near_cen, far_cen, ex_cen = [x.reshape(-1, 8, 128) for x in (near_cen, far_cen, ex_cen)]
+    )(want, served, box_centers, jnp.asarray(node_rows()))
+    near_cen, far_gap, ex_cen = [x.reshape(-1, 8, 128) for x in (near_cen, far_gap, ex_cen)]
+    group = 8
+    far_value = pl.pallas_call(
+        far_kernel,
+        grid=(devices // group,),
+        out_shape=hbm((devices, 256, 128), BF),
+        in_specs=[vmem((group, 8, 128), lambda i: (i, 0, 0)), vmem()],
+        out_specs=vmem((group, 256, 128), lambda i: (i, 0, 0)),
+        compiler_params=params(8),
+        cost_estimate=pl.CostEstimate(flops=200_000_000, bytes_accessed=9_000_000, transcendentals=4_000_000),
+        name="far_values",
+    )(far_gap, jnp.asarray(far_sources(), BF))
 
     big = lambda dtype, rows: pltpu.VMEM((rows, 128), dtype)
     near, far, term = pl.pallas_call(
         duo_kernel,
         out_shape=(hbm((boxes, 8, 128), F32), hbm((boxes, 8, 128), F32), struct((devices, 128), F32)),
-        in_specs=[vmem()] * 2 + [anywhere] * 8,
+        in_specs=[vmem()] + [anywhere] * 8,
         out_specs=(anywhere, anywhere, vmem()),
         scratch_shapes=[
             pltpu.SMEM((devices, 128), jnp.int32),
             pltpu.VMEM((devices, 8, 128), F32),
             pltpu.VMEM((devices // 2, 8, 128), F32),
-            pltpu.VMEM((devices, 8, 128), F32),
             pltpu.VMEM((boxes, 2, 32, 128), BF),
             pltpu.VMEM((boxes, 8, 128), F32),
             pltpu.VMEM((boxes, 8, 128), F32),
-            pltpu.VMEM((boxes, 16, 128), F32),
+            pltpu.VMEM((boxes, 8, 128), F32),
+            pltpu.VMEM((devices, 256, 128), BF),
             pltpu.VMEM((boxes, 8, 128), F32),
             pltpu.VMEM((boxes, 8, 128), F32),
-            pltpu.SemaphoreType.DMA((16,)),
-            pltpu.VMEM((devices, 32, 128), BF),
+            pltpu.SemaphoreType.DMA((20,)),
         ]
         + [big(BF, 128)] * 2
-        + [big(F32, 128)] * 14
-        + [big(BF, 256)] * 14
+        + [big(F32, 128)] * 10
+        + [big(BF, 256)] * 10
         + [pltpu.VMEM((boxes, 8, 128), F32)] * 4,
-        compiler_params=params(20),
+        compiler_params=params(28),
         cost_estimate=pl.CostEstimate(flops=1_000_000_000, bytes_accessed=12_000_000, transcendentals=20_000_000),
         name="pairs",
-    )(got, jnp.asarray(far_sources(), BF), *[stay(x) for x in (want, near_cen, ex_cen, far_cen, f_tab, base, q_tab, far_tab)])
+    )(got, *[stay(x) for x in (want, near_cen, ex_cen, f_tab, base, q_tab, far_tab, far_value)])
 
     terms = exchange(term.reshape(devices, 1, 128))[:, 0, :8]
     curvature = jnp.sum(terms, axis=0) / (devices * boxes * slots)
@@ -882,7 +943,7 @@
         cost_estimate=pl.CostEstimate(flops=50_000_000, bytes_accessed=3_000_000, transcendentals=0),
         name="finish",
     )(counts, stay(near), stay(far), stay(cheb))
-    over = jnp.any((served[:, 9] > HALF) & (jnp.arange(devices) % 4 != 0))
+    over = jnp.any((served.reshape(devices, 2, 128)[:, 0, 9] > HALF) & (jnp.arange(devices) % 4 != 0))
     whole = (local_pos, charges, counts, box_centers, far_list, near_list)
     return lax.cond(over, lambda: general(*whole), lambda: (product, curvature))
 

time: 116 us -> 111 us (0.957)
  waiting for transfers between devices: 38.3 us -> 23.8 us
  Pallas kernels: 48.3 us -> 52.7 us
  other arithmetic: 1.48 us -> 3.83 us
  starting transfers between devices: 25.8 us -> 27 us
    all_to_all x3, waiting for transfers between devices: 38.3 us -> 23.8 us  [exchange(): return lax.all_to_all(x, AXES, split_axis=0, concat_axis=0, tiled=True)]
    pallas_call x3 -> x4, Pallas kernels: 10.8 us -> 20.5 us  [the longest x1 9.88 us: on_device(): pl.pallas_call(far_kernel, grid=(devices // group,), out_shape=hbm((devic...]
    pallas_call x1, Pallas kernels: 21.2 us -> 17.2 us  [on_device(): pl.pallas_call(duo_kernel, out_shape=(hbm((boxes, 8, 128), F32), hbm((box...]
    gt x1, other arithmetic: 0.17 us -> 2.52 us  [on_device(): served.reshape(devices, 2, 128)[:, 0, 9] > HALF]
    pallas_call x1, Pallas kernels: 3.97 us -> 2.58 us  [on_device(): pl.pallas_call(goal_kernel, out_shape=(hbm((devices * 8, 128), F32), hbm(...]
  transfers between devices with their start and end apart: 6 -> 6, of which waited for: 3 -> 3; matrix products, arithmetic and copies ran while one was open for 1% -> 3% of each run, Pallas kernels for 17% -> 26%
where the time goes in v4:
time: 111 us; the launch traced here: 110 us
  Pallas kernels  52.7 us (47%)
  starting transfers between devices  27 us (24%)
  waiting for transfers between devices  23.8 us (21%)
  other arithmetic  3.83 us (3%)
  between operations  1.51 us (1%)
  local copies, waits for them, and re-layouts  1.14 us (1%)
    all_to_all x3, waiting for transfers between devices, exchange(): return lax.all_to_all(x, AXES, split_axis=0, concat_axis=0, tiled=True)  23.8 us
    all_to_all x3, starting transfers between devices, exchange(): return lax.all_to_all(x, AXES, split_axis=0, concat_axis=0, tiled=True)  18.9 us
    pallas_call x1, Pallas kernels, on_device(): pl.pallas_call(duo_kernel, out_shape=(hbm((boxes, 8, 128), F32), hbm((box...  17.2 us
    pallas_call x1, Pallas kernels, on_device(): pl.pallas_call(far_kernel, grid=(devices // group,), out_shape=hbm((devic...  9.88 us
    pallas_call x1, Pallas kernels, on_device(): pl.pallas_call(own_table_kernel, out_shape=(hbm((boxes, 8, 128), F32), hb...  9.59 us
    ppermute x3, starting transfers between devices, on_device(): lax.ppermute(ex_own, 'gy', [(4 * z, 4 * z + k) for z in range(4)])  8.08 us
    pallas_call x1, Pallas kernels, on_device(): pl.pallas_call(send_table_kernel, out_shape=(struct((boxes, NEAR_ROWS, 12...  3.77 us
    pallas_call x1, Pallas kernels, on_device(): pl.pallas_call(send_kernel, out_shape=hbm((devices * ROWS, 128), F32), in...  3.55 us
  transfers between devices with their start and end apart: 6, of which 3 were waited for; matrix products, arithmetic and copies ran while one was open for 3% of the time, Pallas kernels for 26%

profile of v4, /device:TPU:1, one launch (start us, length us, event | category | flops | bytes accessed | tf_op | source)
XLA Modules:
  0.0 110.2 jit_solution(1225200374605104797)
XLA Ops:
  0.6 3.3 %start.1 = (f32[256,128]{1,0:T(8,128)}, s32[128,128]{1,0:T(8,128)S(1)}, f32[512,128]{1,0:T(8,128)S(1)}) custom-call(s32[8,64]{1,0:T(8,128)} %bitcast.56, s32[9,64]{1,0:T(8,128)} %bitcast.54, s32[1,64]{1,0:T(1,128)} %bitcast.57, f32[3,64,128]{2,1,0:T(8,128)} %bitcast.48, f32[64,8,128]{2,1,0:T(8,128)} %charge_ref.5, s32[64]{0:T(128)} %count_ref.7, ...), custom_call_target="tpu_custom_call" | custom-call | tf_op jit(solution)/shard_map/start/pallas_call | solution.py:830
  3.9 5.5 %collective-permute-start.2 = (f32[512,128]{1,0:T(8,128)S(1)}, f32[512,128]{1,0:T(8,128)S(1)}, u32[]{:S(2)}, u32[]{:S(2)}) collective-permute-start(f32[512,128]{1,0:T(8,128)S(1)} %get-tuple-element.66.own_ref), channel_id=1, source_target_pairs={{0,3},{4,7},{8,11},{12,15},{16,19},{20,23},{24,27},{28,31},{32,35}... | collective-permute-start | bytes 786440 | tf_op jit(solution)/shard_map/ppermute | solution.py:838
  9.4 1.3 %collective-permute-start.1 = (f32[512,128]{1,0:T(8,128)S(1)}, f32[512,128]{1,0:T(8,128)S(1)}, u32[]{:S(2)}, u32[]{:S(2)}) collective-permute-start(f32[512,128]{1,0:T(8,128)S(1)} %get-tuple-element.66.own_ref), channel_id=1, source_target_pairs={{0,2},{4,6},{8,10},{12,14},{16,18},{20,22},{24,26},{28,30},{32,34}... | collective-permute-start | bytes 786440 | tf_op jit(solution)/shard_map/ppermute | solution.py:838
  10.7 1.3 %collective-permute-start = (f32[512,128]{1,0:T(8,128)S(1)}, f32[512,128]{1,0:T(8,128)S(1)}, u32[]{:S(2)}, u32[]{:S(2)}) collective-permute-start(f32[512,128]{1,0:T(8,128)S(1)} %get-tuple-element.66.own_ref), channel_id=1, source_target_pairs={{0,1},{4,5},{8,9},{12,13},{16,17},{20,21},{24,25},{28,29},{32,33},... | collective-permute-start | bytes 786440 | tf_op jit(solution)/shard_map/ppermute | solution.py:838
  12.1 8.3 %all-to-all-start.3 = ((f32[128,2,128]{2,1,0:T(2,128)}), f32[128,2,128]{2,1,0:T(2,128)S(1)}, u32[]{:S(2)}, u32[]{:S(2)}) async-start(f32[128,2,128]{2,1,0:T(2,128)} %bitcast.21), calls=%async_computation.3 | async-start | bytes 262144 | tf_op jit(solution)/shard_map/all_to_all | solution.py:318
  20.4 3.8 %send_tables.1 = (f32[64,24,128]{2,1,0:T(8,128)S(1)}, f32[64,8,128]{2,1,0:T(8,128)S(1)}) custom-call(f32[3,64,128]{2,1,0:T(8,128)} %bitcast.49, f32[64,8,128]{2,1,0:T(8,128)} %charge_ref.5, s32[64]{0:T(128)} %count_ref.7, f32[3,64]{1,0:T(4,128)} %cen_ref.5), custom_call_target="tpu_custom_call" | custom-call | flops 50000000 | bytes 1200000 | tf_op jit(solution)/shard_map/send_tables/pallas_call | solution.py:841
  24.2 6.4 %all-to-all-done.3 = f32[128,2,128]{2,1,0:T(2,128)S(1)} async-done(((f32[128,2,128]{2,1,0:T(2,128)}), f32[128,2,128]{2,1,0:T(2,128)S(1)}, u32[]{:S(2)}, u32[]{:S(2)}) %all-to-all-start.3) | async-done | bytes 131104 | tf_op jit(solution)/shard_map/all_to_all | solution.py:318
  30.6 0.0 collective-permute-done.2.refs_2_
  30.6 0.0 collective-permute-done.1.refs_1_
  30.6 0.0 collective-permute-done.refs_0_
  30.6 3.6 %send.1 = f32[5632,128]{1,0:T(8,128)} custom-call(s32[1]{0:T(128)} %bitcast.22.member_ref, f32[256,128]{1,0:T(8,128)S(1)} %bitcast.35, f32[1536,128]{1,0:T(8,128)S(1)} %bitcast.37, f32[512,128]{1,0:T(8,128)S(1)} %bitcast.39, f32[512,128]{1,0:T(8,128)S(1)} %get-tuple-element.66.own_ref, f32[512,128]{1,0:T(8,128)S(1)} %collective-permute-done.refs_0_, ...), custom_call_target="tpu_custom_call" | custom-call | tf_op jit(solution)/shard_map/send/pallas_call | solution.py:852
  34.2 0.0 copy-start.6
  34.2 0.0 copy-start.13
  34.2 0.0 copy-done.1
  34.2 5.3 %all-to-all-start.4 = ((f32[128,11,4,128]{3,2,1,0:T(4,128)}), f32[128,11,4,128]{3,2,1,0:T(4,128)S(1)}, u32[]{:S(2)}, u32[]{:S(2)}) async-start(f32[128,11,4,128]{3,2,1,0:T(4,128)} %bitcast.42), calls=%async_computation.4 | async-start | bytes 5767168 | tf_op jit(solution)/shard_map/all_to_all | solution.py:318
  39.5 0.0 copy-start.3
  39.5 0.0 copy-start.9
  39.5 0.0 copy-start.10
  39.5 0.0 copy-done.6
  39.5 0.0 copy-done.13
  39.5 9.6 %own_tables.1 = (f32[64,8,128]{2,1,0:T(8,128)}, bf16[64,2,32,128]{3,2,1,0:T(8,128)(2,1)}, f32[64,8,128]{2,1,0:T(8,128)}, bf16[64,128,128]{2,1,0:T(8,128)(2,1)}) custom-call(f32[3,64,128]{2,1,0:T(8,128)S(1)} %bitcast.50, f32[64,8,128]{2,1,0:T(8,128)} %charge_ref.5, s32[64]{0:T(128)S(1)} %copy-done.13), custom_call_target="tpu_custom_call" | custom-call | flops 200000000 | bytes 4000000 | tf_op jit(solution)/shard_map/own_tables/pallas_call | solution.py:869
  49.1 0.0 copy-done.2
  49.1 0.0 copy-done.3
  49.1 0.0 copy-done.9
  49.2 2.6 %goals.1 = (f32[1024,128]{1,0:T(8,128)}, f32[1024,128]{1,0:T(8,128)}, f32[512,128]{1,0:T(8,128)}) custom-call(s32[128,128]{1,0:T(8,128)S(1)} %get-tuple-element.67.want_ref.want_hbm, f32[256,128]{1,0:T(8,128)S(1)} %bitcast.36, f32[3,64]{1,0:T(4,128)S(1)} %copy-done.9, f32[8,128]{1,0:T(8,128)S(1)} %copy-done.3), custom_call_target="tpu_custom_call" | custom-call | flops 50000000 | bytes 2000000 | tf_op jit(solution)/shard_map/goals/pallas_call | solution.py:884
  51.7 0.0 copy-done.10
  51.7 1.0 copy-done
  52.8 9.9 %far_values.1.v_hbm = bf16[128,256,128]{2,1,0:T(8,128)(2,1)} custom-call(f32[128,8,128]{2,1,0:T(8,128)S(1)} %bitcast.38, bf16[128,32]{1,0:T(8,128)(2,1)S(1)} %copy-done.10), custom_call_target="tpu_custom_call" | custom-call | flops 200000000 | bytes 9000000 | tf_op jit(solution)/shard_map/far_values/pallas_call | solution.py:896
  62.7 2.5 %compare_reduce_fusion = pred[128]{0:T(512)(128)(4,1)S(1)} fusion(f32[128,2,128]{2,1,0:T(2,128)S(1)} %all-to-all-done.3), kind=kLoop, calls=%fused_computation.7 | loop fusion | flops 128 | bytes 640 | tf_op jit(solution)/shard_map/gt | solution.py:946
  65.2 11.7 %all-to-all-done.4 = f32[128,11,4,128]{3,2,1,0:T(4,128)S(1)} async-done(((f32[128,11,4,128]{3,2,1,0:T(4,128)}), f32[128,11,4,128]{3,2,1,0:T(4,128)S(1)}, u32[]{:S(2)}, u32[]{:S(2)}) %all-to-all-start.4) | async-done | bytes 2883616 | tf_op jit(solution)/shard_map/all_to_all | solution.py:318
  76.9 17.2 %pairs.3 = (f32[64,8,128]{2,1,0:T(8,128)}, f32[64,8,128]{2,1,0:T(8,128)}, f32[128,128]{1,0:T(8,128)}) custom-call(f32[5632,128]{1,0:T(8,128)S(1)} %bitcast.34, s32[128,128]{1,0:T(8,128)} %copy-done.2, f32[128,8,128]{2,1,0:T(8,128)} %bitcast.59, f32[64,8,128]{2,1,0:T(8,128)} %bitcast.60, bf16[64,2,32,128]{3,2,1,0:T(8,128)(2,1)} %get-tuple-element.70.f_hbm, ...), custom_call_target="tpu_custom_call" | custom-call | flops 1000000000 | bytes 12000000 | tf_op jit(solution)/shard_map/pairs/pallas_call | solution.py:908
  94.1 0.0 copy-start.5
  94.1 0.0 copy-start.11
  94.1 0.0 copy-start.12
  94.1 0.0 copy-start.14
  94.1 5.3 %all-to-all-start.5 = ((f32[128,1,128]{2,1,0:T(1,128)}), f32[128,1,128]{2,1,0:T(1,128)S(1)}, u32[]{:S(2)}, u32[]{:S(2)}) async-start(f32[128,1,128]{2,1,0:T(1,128)} %bitcast.32), calls=%async_computation.5 | async-start | bytes 131072 | tf_op jit(solution)/shard_map/all_to_all | solution.py:318
  99.5 0.6 and_reduce_fusion
  100.8 2.8 %finish.1 = f32[64,8,128]{2,1,0:T(8,128)S(1)} custom-call(s32[64]{0:T(128)S(1)} %copy-done.13, f32[64,8,128]{2,1,0:T(8,128)} %get-tuple-element.75.near_ref, f32[64,8,128]{2,1,0:T(8,128)} %get-tuple-element.76.far_ref, bf16[64,128,128]{2,1,0:T(8,128)(2,1)} %get-tuple-element.77.t_ref), custom_call_target="tpu_custom_call" | custom-call | flops 50000000 | bytes 3000000 | tf_op jit(solution)/shard_map/finish/pallas_call | solution.py:937
  103.6 5.7 %all-to-all-done.5 = f32[128,1,128]{2,1,0:T(1,128)S(1)} async-done(((f32[128,1,128]{2,1,0:T(1,128)}), f32[128,1,128]{2,1,0:T(1,128)S(1)}, u32[]{:S(2)}, u32[]{:S(2)}) %all-to-all-start.5) | async-done | bytes 65568 | tf_op jit(solution)/shard_map/all_to_all | solution.py:318
  109.2 0.0 copy-done.5
  109.2 0.0 copy-done.11
  109.2 0.0 copy-done.12
  109.2 0.0 copy-done.14
  109.2 0.2 conditional.1
  109.5 0.0 copy-start.8
  109.5 0.2 slice_reduce_fusion
  109.7 0.5 broadcast_multiply_fusion
  110.2 0.0 copy-done.8
  (3 shorter events, 0.0 us)
Async XLA Ops:
  3.9 45.2 %copy-start.2 = (s32[128,128]{1,0:T(8,128)}, s32[128,128]{1,0:T(8,128)S(1)}, u32[]{:S(2)}) copy-start(s32[128,128]{1,0:T(8,128)S(1)} %get-tuple-element.67.want_ref.want_hbm) | copy-start | bytes 196612
  3.9 26.6 %collective-permute-start.2 = (f32[512,128]{1,0:T(8,128)S(1)}, f32[512,128]{1,0:T(8,128)S(1)}, u32[]{:S(2)}, u32[]{:S(2)}) collective-permute-start(f32[512,128]{1,0:T(8,128)S(1)} %get-tuple-element.66.own_ref), channel_id=1, source_target_pairs={{0,3},{4,7},{8,11},{12,15},{16,19},{20,23},{24,27},{28,31},{32,35}... | collective-permute-start | bytes 786440 | tf_op jit(solution)/shard_map/ppermute | solution.py:838
  9.4 21.2 %collective-permute-start.1 = (f32[512,128]{1,0:T(8,128)S(1)}, f32[512,128]{1,0:T(8,128)S(1)}, u32[]{:S(2)}, u32[]{:S(2)}) collective-permute-start(f32[512,128]{1,0:T(8,128)S(1)} %get-tuple-element.66.own_ref), channel_id=1, source_target_pairs={{0,2},{4,6},{8,10},{12,14},{16,18},{20,22},{24,26},{28,30},{32,34}... | collective-permute-start | bytes 786440 | tf_op jit(solution)/shard_map/ppermute | solution.py:838
  10.7 19.9 %collective-permute-start = (f32[512,128]{1,0:T(8,128)S(1)}, f32[512,128]{1,0:T(8,128)S(1)}, u32[]{:S(2)}, u32[]{:S(2)}) collective-permute-start(f32[512,128]{1,0:T(8,128)S(1)} %get-tuple-element.66.own_ref), channel_id=1, source_target_pairs={{0,1},{4,5},{8,9},{12,13},{16,17},{20,21},{24,25},{28,29},{32,33},... | collective-permute-start | bytes 786440 | tf_op jit(solution)/shard_map/ppermute | solution.py:838
  12.1 18.5 %all-to-all-start.3 = ((f32[128,2,128]{2,1,0:T(2,128)}), f32[128,2,128]{2,1,0:T(2,128)S(1)}, u32[]{:S(2)}, u32[]{:S(2)}) async-start(f32[128,2,128]{2,1,0:T(2,128)} %bitcast.21), calls=%async_computation.3 | async-start | bytes 262144 | tf_op jit(solution)/shard_map/all_to_all | solution.py:318
  24.2 10.0 %copy-start.1 = (f32[64,8,128]{2,1,0:T(8,128)}, f32[64,8,128]{2,1,0:T(8,128)S(1)}, u32[]{:S(2)}) copy-start(f32[64,8,128]{2,1,0:T(8,128)S(1)} %get-tuple-element.65.w_hbm) | copy-start | bytes 786436
  34.2 5.4 %copy-start.6 = (f32[64,3,128]{2,0,1:T(8,128)S(1)}, f32[64,3,128]{2,0,1:T(8,128)}, u32[]{:S(2)}) copy-start(f32[64,3,128]{2,0,1:T(8,128)} %param.12) | copy-start | bytes 294916
  34.2 5.4 %copy-start.13 = (s32[64]{0:T(128)S(1)}, s32[64]{0:T(128)}, u32[]{:S(2)}) copy-start(s32[64]{0:T(128)} %count_ref.7) | copy-start | bytes 772
  34.2 42.7 %all-to-all-start.4 = ((f32[128,11,4,128]{3,2,1,0:T(4,128)}), f32[128,11,4,128]{3,2,1,0:T(4,128)S(1)}, u32[]{:S(2)}, u32[]{:S(2)}) async-start(f32[128,11,4,128]{3,2,1,0:T(4,128)} %bitcast.42), calls=%async_computation.4 | async-start | bytes 5767168 | tf_op jit(solution)/shard_map/all_to_all | solution.py:318
  39.5 9.7 %copy-start.3 = (f32[8,128]{1,0:T(8,128)S(1)}, f32[8,128]{1,0:T(8,128)}, u32[]{:S(2)}) copy-start(f32[8,128]{1,0:T(8,128)} %constant.55.clone.node_ref) | copy-start | bytes 12292
  39.5 9.6 %copy-start.9 = (f32[3,64]{1,0:T(4,128)S(1)}, f32[3,64]{1,0:T(4,128)}, u32[]{:S(2)}) copy-start(f32[3,64]{1,0:T(4,128)} %cen_ref.5) | copy-start | bytes 2308
  39.5 12.2 %copy-start.10 = (bf16[128,32]{1,0:T(8,128)(2,1)S(1)}, bf16[128,32]{1,0:T(8,128)(2,1)}, u32[]{:S(2)}) copy-start(bf16[128,32]{1,0:T(8,128)(2,1)} %constant.56.clone.fn_ref) | copy-start | bytes 24580
  51.7 1.0 copy-start
  94.1 15.2 %copy-start.5 = (f32[64,8,128]{2,1,0:T(8,128)S(1)}, f32[64,8,128]{2,1,0:T(8,128)}, u32[]{:S(2)}) copy-start(f32[64,8,128]{2,1,0:T(8,128)} %charge_ref.5) | copy-start | bytes 786436
  94.1 15.2 %copy-start.11 = (s32[64,9]{0,1:T(8,128)S(1)}, s32[64,9]{0,1:T(8,128)}, u32[]{:S(2)}) copy-start(s32[64,9]{0,1:T(8,128)} %param.17) | copy-start | bytes 6916
  94.1 15.1 %copy-start.12 = (s32[64,8]{0,1:T(8,128)S(1)}, s32[64,8]{0,1:T(8,128)}, u32[]{:S(2)}) copy-start(s32[64,8]{0,1:T(8,128)} %param.16) | copy-start | bytes 6148
  94.1 15.1 %copy-start.14 = (f32[1,8,128]{2,1,0:T(8,128)S(1)}, f32[1,8,128]{2,1,0:T(8,128)}, u32[]{:S(2)}) copy-start(f32[1,8,128]{2,1,0:T(8,128)} %constant.57.clone) | copy-start | bytes 12292
  94.1 15.1 %all-to-all-start.5 = ((f32[128,1,128]{2,1,0:T(1,128)}), f32[128,1,128]{2,1,0:T(1,128)S(1)}, u32[]{:S(2)}, u32[]{:S(2)}) async-start(f32[128,1,128]{2,1,0:T(1,128)} %bitcast.32), calls=%async_computation.5 | async-start | bytes 131072 | tf_op jit(solution)/shard_map/all_to_all | solution.py:318
  109.5 0.7 copy-start.8

commit v5 on v4

--- a/solution.py
+++ b/solution.py
@@ -403,29 +403,35 @@
 ROWS = 44
 NEAR_ROWS = 24
 UNROLL = 4
-
-
-def start_kernel(far_ref, near_ref, most_ref, pos_ref, charge_ref, count_ref, cen_ref, row_ref, msg_ref, want_ref, ex_ref):
+CHUNKS = 16
+AHEAD = 4
+
+
+def upper_kernel(pos_ref, charge_ref, count_ref, row_ref, ex_ref):
+    half = charge_ref.shape[0] // 2
+    lane = iota((8, 128), 1)
+    left = lane < HALF
+    center = jnp.concatenate([row_ref[...], jnp.zeros((5, 2 * half), F32)], axis=0)
+    center = jnp.concatenate([center, jnp.zeros((8, 128 - 2 * half), F32)], axis=1)
+    center = jnp.concatenate([center, jnp.zeros((120, 128), F32)], axis=0).T
+    wide = iota((half, 128), 1) < HALF
+    for d in range(3):
+        first = center[:half, d : d + 1] + 0.5 * pos_ref[d, :half]
+        second = center[half : 2 * half, d : d + 1] + 0.5 * pos_ref[d, half:]
+        ex_ref[(8 + d) * half : (9 + d) * half, :] = jnp.where(wide, pltpu.roll(first, HALF, 1), second)
+
+    def body(b, carry):
+        first = pltpu.roll(jnp.where(lane < count_ref[b], charge_ref[b], 0.0), HALF, 1)
+        second = jnp.where(lane < count_ref[b + half], charge_ref[b + half], 0.0)
+        ex_ref[pl.ds(pl.multiple_of(8 * b, 8), 8), :] = jnp.where(left, first, second)
+        return carry
+
+    lax.fori_loop(0, half, body, 0, unroll=16)
+
+
+def start_kernel(far_ref, near_ref, most_ref, row_ref, msg_ref, want_ref):
     boxes = far_ref.shape[1]
     slots = far_ref.shape[0]
-    lane = iota((8, 128), 1)
-    left = lane < HALF
-    for d in range(3):
-        center = jnp.concatenate([row_ref[...], jnp.zeros((5, boxes), F32)], axis=0)
-        center = jnp.concatenate([center, jnp.zeros((8, 128 - boxes), F32)], axis=1)
-        center = jnp.concatenate([center, jnp.zeros((120, 128), F32)], axis=0).T[:boxes, d : d + 1]
-        ex_ref[pl.ds(d, boxes, stride=8), :] = center + 0.5 * pos_ref[d]
-    for d in range(3, 8):
-        ex_ref[pl.ds(d, boxes, stride=8), :] = jnp.zeros((boxes, 128), F32)
-
-    def body(b, carry):
-        q = pltpu.roll(jnp.where(lane < count_ref[b], charge_ref[b], 0.0), HALF, 1)
-        at = pl.ds(pl.multiple_of(8 * b, 8), 8)
-        ex_ref[at, :] = jnp.where(left, q, ex_ref[at, :])
-        return carry
-
-    lax.fori_loop(0, boxes, body, 0, unroll=16)
-
     peer = iota((128, 128), 0)
     line = iota((128, 128), 1)
     tri = (peer < line).astype(F32).astype(BF)
@@ -523,7 +529,7 @@
         far_ref[b] = weight + pltpu.roll(weight, 64, 1)
         return carry
 
-    lax.fori_loop(0, boxes, body, 0, unroll=8)
+    lax.fori_loop(0, boxes, body, 0, unroll=32)
 
 
 def own_table_kernel(pos_ref, charge_ref, count_ref, q_ref, f_ref, base_ref, t_ref):
@@ -551,7 +557,7 @@
     lax.fori_loop(0, boxes, body, 0, unroll=4)
 
 
-def goal_kernel(want_ref, served_ref, cen_ref, node_ref, nc_ref, fc_ref, ec_ref, odd_ref):
+def goal_kernel(want_ref, served_ref, cen_ref, node_ref, nc_ref, fc_ref, ec_ref, goal_ref, odd_ref):
     lane = iota((128, 128), 1)
     left = lane < HALF
     boxes = cen_ref.shape[1]
@@ -567,6 +573,7 @@
 
     parts = split3(cen, 0)
     want = want_ref[...]
+    goal_ref[...] = want.astype(F32).T[16:32].astype(jnp.int32)
     sources = [served_ref[pl.ds(1, 128, stride=2), :], served_ref[pl.ds(0, 128, stride=2), :]]
     halves = [jnp.concatenate([(iota((128, 128), 0) // HALF == h).astype(F32).astype(BF)] * 3, axis=0) for h in range(2)]
 
@@ -610,21 +617,26 @@
 
 def send_kernel(member_ref, served_ref, near_ref, far_ref, own_ref, *refs):
     moved, (out_ref, ids_ref, int_ref, ex_ref, buf_ref, sems) = refs[:3], refs[3:]
-    peers = ids_ref.shape[0]
+    peers = ids_ref.shape[1]
     sub = iota((8, 128), 0)
     lane = iota((8, 128), 1)
     left = lane < HALF
     keep = left | (sub < 3)
     second = sub < 5
-    int_ref[...] = served_ref[pl.ds(0, peers, stride=2), :].astype(jnp.int32)
+    int_ref[...] = served_ref[pl.ds(0, peers, stride=2), :].T[:16].astype(jnp.int32)
     copy = pltpu.make_async_copy(int_ref, ids_ref, sems.at[0])
     copy.start()
-    ex_ref[...] = moved[0][...] + moved[1][...] + moved[2][...]
-
-    @pl.when(member_ref[0] == 0)
-    def _():
-        ex_ref[...] = own_ref[...]
-
+    half = ex_ref.shape[0] // 16
+    packed = moved[0][...] + moved[1][...] + moved[2][...]
+    packed = jnp.where(member_ref[0] == 0, own_ref[...], packed)
+    for d in range(3):
+        rows = packed[(8 + d) * half : (9 + d) * half]
+        ex_ref[pl.ds(d, half, stride=8), :] = pltpu.roll(rows, HALF, 1)
+        ex_ref[pl.ds(8 * half + d, half, stride=8), :] = rows
+    for b in range(half):
+        tile = packed[8 * b : 8 * b + 8]
+        for at, part in ((8 * b, tile), (8 * (b + half), pltpu.roll(tile, HALF, 1))):
+            ex_ref[at : at + 8, :] = jnp.where(left, part, jnp.where(sub < 3, ex_ref[at : at + 8, :], 0.0))
     copy.wait()
 
     def body(i, carry):
@@ -632,7 +644,7 @@
         for k in range(2):
             peer = 2 * i + k
             at = lambda row: pl.ds(base + (k * ROWS + row), 8)
-            rows = lambda ref, j, row: ref[pl.ds(pl.multiple_of(ids_ref[peer, j], 8) + row, 8), :]
+            rows = lambda ref, j, row: ref[pl.ds(pl.multiple_of(ids_ref[j, peer], 8) + row, 8), :]
             q = [rows(near_ref, j, 0) for j in range(4)]
             w = [rows(far_ref, 4 + j, 0) for j in range(4)]
             p = [rows(near_ref, j, 16 if j < 2 else 8) for j in range(4)]
@@ -657,7 +669,7 @@
 
 
 def duo_kernel(
-    got_ref, want_hbm, nc_hbm, ec_hbm, f_hbm, base_hbm, q_hbm, w_hbm, v_hbm, near_hbm, far_hbm, term_ref,
+    scale, got_ref, want_hbm, nc_hbm, ec_hbm, f_hbm, base_hbm, q_hbm, w_hbm, v_hbm, near_hbm, far_hbm, term_ref,
     tgt_ref, nc_ref, ec_ref, f_ref, base_ref, q_ref, w_ref, v_ref, near_ref, far_ref, sems, *bufs
 ):
     whole = [(want_hbm, tgt_ref), (nc_hbm, nc_ref), (ec_hbm, ec_ref), (f_hbm, f_ref)]
@@ -665,16 +677,14 @@
     loads = [pltpu.make_async_copy(source, target, sems.at[i]) for i, (source, target) in enumerate(whole)]
     for copy in loads[:4]:
         copy.start()
-    chunk = v_ref.shape[0] // 4
+    chunk = v_ref.shape[0] // CHUNKS
 
     def far_values(c):
         at = pl.ds(c * chunk, chunk)
-        return pltpu.make_async_copy(v_hbm.at[at], v_ref.at[at], sems.at[16 + c])
-
-    for c in range(4):
+        return pltpu.make_async_copy(v_hbm.at[at], v_ref.at[at], sems.at[16 + c % AHEAD])
+
+    for c in range(AHEAD):
         far_values(c).start()
-    for copy in loads[4:]:
-        copy.start()
     xt_refs, dist_refs, value_refs = bufs[:2], (bufs[2:7], bufs[7:12]), (bufs[12:17], bufs[17:22])
     near_accs, far_accs = bufs[22:24], bufs[24:26]
     duos = ec_ref.shape[0]
@@ -693,8 +703,8 @@
         return tile(duo, 0, 32), tile(duo, 1, 32)
 
     def goals(duo):
-        pairs = [(tgt_ref[2 * duo + k // 2, 16 + 2 * (k % 2)], tgt_ref[2 * duo + k // 2, 17 + 2 * (k % 2)]) for k in range(4)]
-        return pairs + [(tgt_ref[2 * duo, 24], tgt_ref[2 * duo + 1, 24])]
+        pairs = [(tgt_ref[2 * (k % 2), 2 * duo + k // 2], tgt_ref[2 * (k % 2) + 1, 2 * duo + k // 2]) for k in range(4)]
+        return pairs + [(tgt_ref[8, 2 * duo], tgt_ref[8, 2 * duo + 1])]
 
     def halves(x):
         high = x.astype(BF).astype(F32)
@@ -721,7 +731,7 @@
             for h in range(2):
                 for u in range(2):
                     at = 32 * h + 16 * u
-                    far_accs[h][tgt_ref[2 * duo + a, 20 + 2 * u + h]] += fold(new[at : at + 16])
+                    far_accs[h][tgt_ref[4 + 2 * u + h, 2 * duo + a]] += fold(new[at : at + 16])
 
     def values(dist, value):
         for k in range(5):
@@ -751,11 +761,14 @@
         xt[...] = jnp.concatenate(feats, axis=0).T.astype(BF)
 
     turns = duos // UNROLL
+    assert turns == CHUNKS
 
     def body(i, carry):
-        @pl.when(i % (turns // 4) == 0)
+        far_values(i).wait()
+
+        @pl.when(i + AHEAD < CHUNKS)
         def _():
-            far_values(i // (turns // 4)).wait()
+            far_values(i + AHEAD).start()
 
         for s in range(UNROLL):
             now, was = s % 2, 1 - s % 2
@@ -770,6 +783,8 @@
     for copy in loads[:4]:
         copy.wait()
     features(0, xt_refs[1])
+    for copy in loads[4:]:
+        copy.start()
     lax.fori_loop(0, turns, body, 0)
     products(duos - 2, value_refs[1])
     values(dist_refs[1], value_refs[0])
@@ -797,7 +812,7 @@
             stores.append(copy)
     ones = jnp.ones((128, 128), F32)
     sums = lax.dot_general(ones, total, NT, precision=lax.Precision.HIGHEST, preferred_element_type=F32)
-    term_ref[...] = jnp.concatenate([sums, jnp.zeros((128, 120), F32)], axis=1)
+    term_ref[...] = jnp.concatenate([sums * scale, jnp.zeros((128, 120), F32)], axis=1)
     for copy in stores:
         copy.wait()
 
@@ -827,14 +842,22 @@
     table = struct((boxes, 8, 128), F32)
     flat = lambda x: x.reshape(-1, 128)
     member = (lax.axis_index("gy") % 4).astype(jnp.int32).reshape(1)
-    msg, want, ex_own = pl.pallas_call(
+    ex_own = pl.pallas_call(
+        upper_kernel,
+        out_shape=struct((boxes * 11 // 2, 128), F32),
+        in_specs=[vmem(), vmem(), SMEM, vmem()],
+        out_specs=vmem(),
+        compiler_params=params(8),
+        name="upper_halves",
+    )(pos, charges, counts, box_centers)
+    msg, want = pl.pallas_call(
         start_kernel,
-        out_shape=(struct((devices * 2, 128), F32), struct((devices, 128), jnp.int32), struct((boxes * 8, 128), F32)),
-        in_specs=[vmem()] * 5 + [SMEM, SMEM, vmem()],
-        out_specs=(vmem(), vmem(), vmem()),
+        out_shape=(struct((devices * 2, 128), F32), struct((devices, 128), jnp.int32)),
+        in_specs=[vmem()] * 4,
+        out_specs=(vmem(), vmem()),
         compiler_params=params(8),
         name="start",
-    )(far_list.T, near_list.T, counts.reshape(1, boxes), pos, charges, counts, box_centers, box_centers)
+    )(far_list.T, near_list.T, counts.reshape(1, boxes), box_centers)
     moved = [lax.ppermute(ex_own, "gy", [(4 * z, 4 * z + k) for z in range(4)]) for k in range(1, 4)]
     served = flat(exchange(msg.reshape(devices, 2, 128)))
 
@@ -855,8 +878,8 @@
         in_specs=[SMEM] + [vmem()] * 7,
         out_specs=anywhere,
         scratch_shapes=[
-            pltpu.SMEM((devices, 128), jnp.int32),
-            pltpu.VMEM((devices, 128), jnp.int32),
+            pltpu.SMEM((16, devices), jnp.int32),
+            pltpu.VMEM((16, devices), jnp.int32),
             pltpu.VMEM((boxes * 8, 128), F32),
             pltpu.VMEM((devices * ROWS, 128), F32),
             pltpu.SemaphoreType.DMA((5,)),
@@ -881,11 +904,16 @@
         name="own_tables",
     )(pos, charges, counts)
 
-    near_cen, far_gap, ex_cen = pl.pallas_call(
+    near_cen, far_gap, ex_cen, goals = pl.pallas_call(
         goal_kernel,
-        out_shape=(hbm((devices * 8, 128), F32), hbm((devices * 8, 128), F32), hbm((devices * 4, 128), F32)),
+        out_shape=(
+            hbm((devices * 8, 128), F32),
+            hbm((devices * 8, 128), F32),
+            hbm((devices * 4, 128), F32),
+            hbm((16, devices), jnp.int32),
+        ),
         in_specs=[vmem()] * 4,
-        out_specs=(vmem(), vmem(), vmem()),
+        out_specs=(vmem(),) * 4,
         scratch_shapes=[pltpu.VMEM((128, 128), F32)],
         compiler_params=params(8),
         cost_estimate=pl.CostEstimate(flops=50_000_000, bytes_accessed=2_000_000, transcendentals=0),
@@ -906,12 +934,12 @@
 
     big = lambda dtype, rows: pltpu.VMEM((rows, 128), dtype)
     near, far, term = pl.pallas_call(
-        duo_kernel,
+        functools.partial(duo_kernel, 1.0 / (devices * boxes * slots)),
         out_shape=(hbm((boxes, 8, 128), F32), hbm((boxes, 8, 128), F32), struct((devices, 128), F32)),
         in_specs=[vmem()] + [anywhere] * 8,
         out_specs=(anywhere, anywhere, vmem()),
         scratch_shapes=[
-            pltpu.SMEM((devices, 128), jnp.int32),
+            pltpu.SMEM((16, devices), jnp.int32),
             pltpu.VMEM((devices, 8, 128), F32),
             pltpu.VMEM((devices // 2, 8, 128), F32),
             pltpu.VMEM((boxes, 2, 32, 128), BF),
@@ -930,10 +958,10 @@
         compiler_params=params(28),
         cost_estimate=pl.CostEstimate(flops=1_000_000_000, bytes_accessed=12_000_000, transcendentals=20_000_000),
         name="pairs",
-    )(got, *[stay(x) for x in (want, near_cen, ex_cen, f_tab, base, q_tab, far_tab, far_value)])
+    )(got, *[stay(x) for x in (goals, near_cen, ex_cen, f_tab, base, q_tab, far_tab, far_value)])
 
     terms = exchange(term.reshape(devices, 1, 128))[:, 0, :8]
-    curvature = jnp.sum(terms, axis=0) / (devices * boxes * slots)
+    curvature = jnp.sum(terms, axis=0)
     product = pl.pallas_call(
         finish_kernel,
         out_shape=table,

time: 111 us -> 109 us (0.982)
  starting transfers between devices: 27 us -> 25.8 us
    all_to_all x3, starting transfers between devices: 18.9 us -> 17.8 us  [exchange(): return lax.all_to_all(x, AXES, split_axis=0, concat_axis=0, tiled=True)]
    pallas_call x1, Pallas kernels: 3.77 us -> 2.59 us  [on_device(): pl.pallas_call(send_table_kernel, out_shape=(struct((boxes, NEAR_ROWS, 12...]
    pallas_call x1 -> x2, Pallas kernels: 17.2 us -> 18.1 us  [the longest x1 16.7 us: on_device(): pl.pallas_call(functools.partial(duo_kernel, 1.0 / (devices * boxes * slo...]
  transfers between devices with their start and end apart: 6 -> 6, of which waited for: 3 -> 3; matrix products, arithmetic and copies ran while one was open for 3% -> 3% of each run, Pallas kernels for 26% -> 28%
where the time goes in v5:
time: 109 us
  Pallas kernels  51.9 us (48%)
  starting transfers between devices  25.8 us (24%)
  waiting for transfers between devices  24.4 us (22%)
  other arithmetic  3.82 us (4%)
  between operations  1.47 us (1%)
  local copies, waits for them, and re-layouts  1.1 us (1%)
    all_to_all x3, waiting for transfers between devices, exchange(): return lax.all_to_all(x, AXES, split_axis=0, concat_axis=0, tiled=True)  24.4 us
    all_to_all x3, starting transfers between devices, exchange(): return lax.all_to_all(x, AXES, split_axis=0, concat_axis=0, tiled=True)  17.8 us
    pallas_call x1, Pallas kernels, on_device(): pl.pallas_call(functools.partial(duo_kernel, 1.0 / (devices * boxes * slo...  16.7 us
    pallas_call x1, Pallas kernels, on_device(): pl.pallas_call(far_kernel, grid=(devices // group,), out_shape=hbm((devic...  9.77 us
    pallas_call x1, Pallas kernels, on_device(): pl.pallas_call(own_table_kernel, out_shape=(hbm((boxes, 8, 128), F32), hb...  9.59 us
    ppermute x3, starting transfers between devices, on_device(): lax.ppermute(ex_own, 'gy', [(4 * z, 4 * z + k) for z in range(4)])  8.08 us
    pallas_call x1, Pallas kernels, on_device(): pl.pallas_call(finish_kernel, out_shape=table, in_specs=[SMEM] + [vmem()]...  3.52 us
    pallas_call x1, Pallas kernels, on_device(): pl.pallas_call(send_kernel, out_shape=hbm((devices * ROWS, 128), F32), in...  3.15 us
  transfers between devices with their start and end apart: 6, of which 3 were waited for; matrix products, arithmetic and copies ran while one was open for 3% of the time, Pallas kernels for 28%

profile of v5, /device:TPU:1, one launch (start us, length us, event | category | flops | bytes accessed | tf_op | source)
XLA Modules:
  0.0 108.5 jit_solution(13201663773037199547)
XLA Ops:
  0.6 1.4 %upper_halves.1.own_ref = f32[352,128]{1,0:T(8,128)S(1)} custom-call(f32[3,64,128]{2,1,0:T(8,128)} %bitcast.47, f32[64,8,128]{2,1,0:T(8,128)} %charge_ref.5, s32[64]{0:T(128)} %count_ref.7, f32[3,64]{1,0:T(4,128)} %cen_ref.3), custom_call_target="tpu_custom_call" | custom-call | tf_op jit(solution)/shard_map/upper_halves/pallas_call | solution.py:845
  2.0 5.5 %collective-permute-start.2 = (f32[352,128]{1,0:T(8,128)S(1)}, f32[352,128]{1,0:T(8,128)S(1)}, u32[]{:S(2)}, u32[]{:S(2)}) collective-permute-start(f32[352,128]{1,0:T(8,128)S(1)} %upper_halves.1.own_ref), channel_id=1, source_target_pairs={{0,3},{4,7},{8,11},{12,15},{16,19},{20,23},{24,27},{28,31},{32,35}... | collective-permute-start | bytes 540680 | tf_op jit(solution)/shard_map/ppermute | solution.py:861
  7.5 1.3 %collective-permute-start.1 = (f32[352,128]{1,0:T(8,128)S(1)}, f32[352,128]{1,0:T(8,128)S(1)}, u32[]{:S(2)}, u32[]{:S(2)}) collective-permute-start(f32[352,128]{1,0:T(8,128)S(1)} %upper_halves.1.own_ref), channel_id=1, source_target_pairs={{0,2},{4,6},{8,10},{12,14},{16,18},{20,22},{24,26},{28,30},{32,34}... | collective-permute-start | bytes 540680 | tf_op jit(solution)/shard_map/ppermute | solution.py:861
  8.8 1.3 %collective-permute-start = (f32[352,128]{1,0:T(8,128)S(1)}, f32[352,128]{1,0:T(8,128)S(1)}, u32[]{:S(2)}, u32[]{:S(2)}) collective-permute-start(f32[352,128]{1,0:T(8,128)S(1)} %upper_halves.1.own_ref), channel_id=1, source_target_pairs={{0,1},{4,5},{8,9},{12,13},{16,17},{20,21},{24,25},{28,29},{32,33},... | collective-permute-start | bytes 540680 | tf_op jit(solution)/shard_map/ppermute | solution.py:861
  10.1 2.5 %start.1 = (f32[256,128]{1,0:T(8,128)}, s32[128,128]{1,0:T(8,128)S(1)}) custom-call(s32[8,64]{1,0:T(8,128)} %bitcast.55, s32[9,64]{1,0:T(8,128)} %bitcast.53, s32[1,64]{1,0:T(1,128)} %bitcast.56, f32[3,64]{1,0:T(4,128)} %cen_ref.3), custom_call_target="tpu_custom_call" | custom-call | tf_op jit(solution)/shard_map/start/pallas_call | solution.py:853
  12.6 8.3 %all-to-all-start.3 = ((f32[128,2,128]{2,1,0:T(2,128)}), f32[128,2,128]{2,1,0:T(2,128)S(1)}, u32[]{:S(2)}, u32[]{:S(2)}) async-start(f32[128,2,128]{2,1,0:T(2,128)} %bitcast.19), calls=%async_computation.3 | async-start | bytes 262144 | tf_op jit(solution)/shard_map/all_to_all | solution.py:318
  20.9 2.6 %send_tables.1 = (f32[64,24,128]{2,1,0:T(8,128)S(1)}, f32[64,8,128]{2,1,0:T(8,128)S(1)}) custom-call(f32[3,64,128]{2,1,0:T(8,128)} %bitcast.48, f32[64,8,128]{2,1,0:T(8,128)} %charge_ref.5, s32[64]{0:T(128)} %count_ref.7, f32[3,64]{1,0:T(4,128)} %cen_ref.3), custom_call_target="tpu_custom_call" | custom-call | flops 50000000 | bytes 1200000 | tf_op jit(solution)/shard_map/send_tables/pallas_call | solution.py:864
  23.5 0.0 copy-start.1
  23.5 7.6 %all-to-all-done.3 = f32[128,2,128]{2,1,0:T(2,128)S(1)} async-done(((f32[128,2,128]{2,1,0:T(2,128)}), f32[128,2,128]{2,1,0:T(2,128)S(1)}, u32[]{:S(2)}, u32[]{:S(2)}) %all-to-all-start.3) | async-done | bytes 131104 | tf_op jit(solution)/shard_map/all_to_all | solution.py:318
  31.1 0.0 collective-permute-done.2.refs_2_
  31.1 0.0 collective-permute-done.1.refs_1_
  31.1 0.0 collective-permute-done.refs_0_
  31.1 3.2 %send.1 = f32[5632,128]{1,0:T(8,128)} custom-call(s32[1]{0:T(128)} %bitcast.20.member_ref, f32[256,128]{1,0:T(8,128)S(1)} %bitcast.34, f32[1536,128]{1,0:T(8,128)S(1)} %bitcast.36, f32[512,128]{1,0:T(8,128)S(1)} %bitcast.38, f32[352,128]{1,0:T(8,128)S(1)} %upper_halves.1.own_ref, f32[352,128]{1,0:T(8,128)S(1)} %collective-permute-done.refs_0_, ...), custom_call_target="tpu_custom_call" | custom-call | tf_op jit(solution)/shard_map/send/pallas_call | solution.py:875
  34.3 0.0 copy-start.5
  34.3 0.0 copy-start.11
  34.3 0.0 copy-done.1
  34.3 4.1 %all-to-all-start.4 = ((f32[128,11,4,128]{3,2,1,0:T(4,128)}), f32[128,11,4,128]{3,2,1,0:T(4,128)S(1)}, u32[]{:S(2)}, u32[]{:S(2)}) async-start(f32[128,11,4,128]{3,2,1,0:T(4,128)} %bitcast.41), calls=%async_computation.4 | async-start | bytes 5767168 | tf_op jit(solution)/shard_map/all_to_all | solution.py:318
  38.4 0.0 copy-start.2
  38.4 0.0 copy-start.7
  38.4 0.0 copy-start.8
  38.4 0.0 copy-done.5
  38.5 0.0 copy-done.11
  38.5 9.6 %own_tables.1 = (f32[64,8,128]{2,1,0:T(8,128)}, bf16[64,2,32,128]{3,2,1,0:T(8,128)(2,1)}, f32[64,8,128]{2,1,0:T(8,128)}, bf16[64,128,128]{2,1,0:T(8,128)(2,1)}) custom-call(f32[3,64,128]{2,1,0:T(8,128)S(1)} %bitcast.49, f32[64,8,128]{2,1,0:T(8,128)} %charge_ref.5, s32[64]{0:T(128)S(1)} %copy-done.11), custom_call_target="tpu_custom_call" | custom-call | flops 200000000 | bytes 4000000 | tf_op jit(solution)/shard_map/own_tables/pallas_call | solution.py:892
  48.1 0.0 copy-done.2
  48.1 0.0 copy-done.7
  48.1 2.7 %goals.1 = (f32[1024,128]{1,0:T(8,128)}, f32[1024,128]{1,0:T(8,128)}, f32[512,128]{1,0:T(8,128)}, s32[16,128]{1,0:T(8,128)}) custom-call(s32[128,128]{1,0:T(8,128)S(1)} %get-tuple-element.63.want_ref, f32[256,128]{1,0:T(8,128)S(1)} %bitcast.35, f32[3,64]{1,0:T(4,128)S(1)} %copy-done.7, f32[8,128]{1,0:T(8,128)S(1)} %copy-done.2), custom_call_target="tpu_custom_call" | custom-call | flops 50000000 | bytes 2000000 | tf_op jit(solution)/shard_map/goals/pallas_call | solution.py:907
  50.7 0.0 copy-done.8
  50.7 0.0 copy-start
  50.8 1.0 copy-done
  51.8 9.8 %far_values.1.v_hbm = bf16[128,256,128]{2,1,0:T(8,128)(2,1)} custom-call(f32[128,8,128]{2,1,0:T(8,128)S(1)} %bitcast.37, bf16[128,32]{1,0:T(8,128)(2,1)S(1)} %copy-done.8), custom_call_target="tpu_custom_call" | custom-call | flops 200000000 | bytes 9000000 | tf_op jit(solution)/shard_map/far_values/pallas_call | solution.py:924
  61.6 2.5 %compare_reduce_fusion = pred[128]{0:T(512)(128)(4,1)S(1)} fusion(f32[128,2,128]{2,1,0:T(2,128)S(1)} %all-to-all-done.3), kind=kLoop, calls=%fused_computation.10 | loop fusion | flops 128 | bytes 640 | tf_op jit(solution)/shard_map/gt | solution.py:974
  64.1 11.9 %all-to-all-done.4 = f32[128,11,4,128]{3,2,1,0:T(4,128)S(1)} async-done(((f32[128,11,4,128]{3,2,1,0:T(4,128)}), f32[128,11,4,128]{3,2,1,0:T(4,128)S(1)}, u32[]{:S(2)}, u32[]{:S(2)}) %all-to-all-start.4) | async-done | bytes 2883616 | tf_op jit(solution)/shard_map/all_to_all | solution.py:318
  75.9 16.7 %pairs.3 = (f32[64,8,128]{2,1,0:T(8,128)}, f32[64,8,128]{2,1,0:T(8,128)}, f32[128,128]{1,0:T(8,128)}) custom-call(f32[5632,128]{1,0:T(8,128)S(1)} %bitcast.33, s32[16,128]{1,0:T(8,128)} %get-tuple-element.64.want_hbm, f32[128,8,128]{2,1,0:T(8,128)} %bitcast.57, f32[64,8,128]{2,1,0:T(8,128)} %bitcast.58, bf16[64,2,32,128]{3,2,1,0:T(8,128)(2,1)} %get-tuple-element.67.f_hbm, ...), custom_call_target="tpu_custom_call" | custom-call | flops 1000000000 | bytes 12000000 | tf_op jit(solution)/shard_map/pairs/pallas_call | solution.py:936
  92.6 0.0 copy-start.4
  92.7 0.0 copy-start.9
  92.7 0.0 copy-start.10
  92.7 5.4 %all-to-all-start.5 = ((f32[128,1,128]{2,1,0:T(1,128)}), f32[128,1,128]{2,1,0:T(1,128)S(1)}, u32[]{:S(2)}, u32[]{:S(2)}) async-start(f32[128,1,128]{2,1,0:T(1,128)} %bitcast.31), calls=%async_computation.5 | async-start | bytes 131072 | tf_op jit(solution)/shard_map/all_to_all | solution.py:318
  98.1 0.6 and_reduce_fusion
  99.4 3.5 %finish.1 = f32[64,8,128]{2,1,0:T(8,128)} custom-call(s32[64]{0:T(128)S(1)} %copy-done.11, f32[64,8,128]{2,1,0:T(8,128)} %get-tuple-element.72.near_ref, f32[64,8,128]{2,1,0:T(8,128)} %get-tuple-element.73.far_ref, bf16[64,128,128]{2,1,0:T(8,128)(2,1)} %get-tuple-element.74.t_ref), custom_call_target="tpu_custom_call" | custom-call | flops 50000000 | bytes 3000000 | tf_op jit(solution)/shard_map/finish/pallas_call | solution.py:965
  102.9 5.0 %all-to-all-done.5 = f32[128,1,128]{2,1,0:T(1,128)S(1)} async-done(((f32[128,1,128]{2,1,0:T(1,128)}), f32[128,1,128]{2,1,0:T(1,128)S(1)}, u32[]{:S(2)}, u32[]{:S(2)}) %all-to-all-start.5) | async-done | bytes 65568 | tf_op jit(solution)/shard_map/all_to_all | solution.py:318
  107.8 0.0 copy-done.4
  107.8 0.0 copy-done.9
  107.8 0.0 copy-done.10
  107.8 0.7 conditional.1
  107.9 0.7 slice_reduce_fusion
Async XLA Ops:
  2.0 29.1 %collective-permute-start.2 = (f32[352,128]{1,0:T(8,128)S(1)}, f32[352,128]{1,0:T(8,128)S(1)}, u32[]{:S(2)}, u32[]{:S(2)}) collective-permute-start(f32[352,128]{1,0:T(8,128)S(1)} %upper_halves.1.own_ref), channel_id=1, source_target_pairs={{0,3},{4,7},{8,11},{12,15},{16,19},{20,23},{24,27},{28,31},{32,35}... | collective-permute-start | bytes 540680 | tf_op jit(solution)/shard_map/ppermute | solution.py:861
  7.5 23.6 %collective-permute-start.1 = (f32[352,128]{1,0:T(8,128)S(1)}, f32[352,128]{1,0:T(8,128)S(1)}, u32[]{:S(2)}, u32[]{:S(2)}) collective-permute-start(f32[352,128]{1,0:T(8,128)S(1)} %upper_halves.1.own_ref), channel_id=1, source_target_pairs={{0,2},{4,6},{8,10},{12,14},{16,18},{20,22},{24,26},{28,30},{32,34}... | collective-permute-start | bytes 540680 | tf_op jit(solution)/shard_map/ppermute | solution.py:861
  8.8 22.3 %collective-permute-start = (f32[352,128]{1,0:T(8,128)S(1)}, f32[352,128]{1,0:T(8,128)S(1)}, u32[]{:S(2)}, u32[]{:S(2)}) collective-permute-start(f32[352,128]{1,0:T(8,128)S(1)} %upper_halves.1.own_ref), channel_id=1, source_target_pairs={{0,1},{4,5},{8,9},{12,13},{16,17},{20,21},{24,25},{28,29},{32,33},... | collective-permute-start | bytes 540680 | tf_op jit(solution)/shard_map/ppermute | solution.py:861
  12.6 18.5 %all-to-all-start.3 = ((f32[128,2,128]{2,1,0:T(2,128)}), f32[128,2,128]{2,1,0:T(2,128)S(1)}, u32[]{:S(2)}, u32[]{:S(2)}) async-start(f32[128,2,128]{2,1,0:T(2,128)} %bitcast.19), calls=%async_computation.3 | async-start | bytes 262144 | tf_op jit(solution)/shard_map/all_to_all | solution.py:318
  23.5 10.8 %copy-start.1 = (f32[64,8,128]{2,1,0:T(8,128)}, f32[64,8,128]{2,1,0:T(8,128)S(1)}, u32[]{:S(2)}) copy-start(f32[64,8,128]{2,1,0:T(8,128)S(1)} %get-tuple-element.62.w_hbm) | copy-start | bytes 786436
  34.3 4.1 %copy-start.5 = (f32[64,3,128]{2,0,1:T(8,128)S(1)}, f32[64,3,128]{2,0,1:T(8,128)}, u32[]{:S(2)}) copy-start(f32[64,3,128]{2,0,1:T(8,128)} %param.12) | copy-start | bytes 294916
  34.3 4.1 %copy-start.11 = (s32[64]{0:T(128)S(1)}, s32[64]{0:T(128)}, u32[]{:S(2)}) copy-start(s32[64]{0:T(128)} %count_ref.7) | copy-start | bytes 772
  34.3 41.6 %all-to-all-start.4 = ((f32[128,11,4,128]{3,2,1,0:T(4,128)}), f32[128,11,4,128]{3,2,1,0:T(4,128)S(1)}, u32[]{:S(2)}, u32[]{:S(2)}) async-start(f32[128,11,4,128]{3,2,1,0:T(4,128)} %bitcast.41), calls=%async_computation.4 | async-start | bytes 5767168 | tf_op jit(solution)/shard_map/all_to_all | solution.py:318
  38.4 9.6 %copy-start.2 = (f32[8,128]{1,0:T(8,128)S(1)}, f32[8,128]{1,0:T(8,128)}, u32[]{:S(2)}) copy-start(f32[8,128]{1,0:T(8,128)} %constant.51.clone.node_ref) | copy-start | bytes 12292
  38.4 9.6 %copy-start.7 = (f32[3,64]{1,0:T(4,128)S(1)}, f32[3,64]{1,0:T(4,128)}, u32[]{:S(2)}) copy-start(f32[3,64]{1,0:T(4,128)} %cen_ref.3) | copy-start | bytes 2308
  38.4 12.3 %copy-start.8 = (bf16[128,32]{1,0:T(8,128)(2,1)S(1)}, bf16[128,32]{1,0:T(8,128)(2,1)}, u32[]{:S(2)}) copy-start(bf16[128,32]{1,0:T(8,128)(2,1)} %constant.52.clone.fn_ref) | copy-start | bytes 24580
  50.7 1.0 copy-start
  92.6 15.2 %copy-start.4 = (f32[64,8,128]{2,1,0:T(8,128)S(1)}, f32[64,8,128]{2,1,0:T(8,128)}, u32[]{:S(2)}) copy-start(f32[64,8,128]{2,1,0:T(8,128)} %charge_ref.5) | copy-start | bytes 786436
  92.7 15.2 %copy-start.9 = (s32[64,9]{0,1:T(8,128)S(1)}, s32[64,9]{0,1:T(8,128)}, u32[]{:S(2)}) copy-start(s32[64,9]{0,1:T(8,128)} %param.17) | copy-start | bytes 6916
  92.7 15.2 %copy-start.10 = (s32[64,8]{0,1:T(8,128)S(1)}, s32[64,8]{0,1:T(8,128)}, u32[]{:S(2)}) copy-start(s32[64,8]{0,1:T(8,128)} %param.16) | copy-start | bytes 6148
  92.7 15.1 %all-to-all-start.5 = ((f32[128,1,128]{2,1,0:T(1,128)}), f32[128,1,128]{2,1,0:T(1,128)S(1)}, u32[]{:S(2)}, u32[]{:S(2)}) async-start(f32[128,1,128]{2,1,0:T(1,128)} %bitcast.31), calls=%async_computation.5 | async-start | bytes 131072 | tf_op jit(solution)/shard_map/all_to_all | solution.py:318

commit v6 on v5

--- a/solution.py
+++ b/solution.py
@@ -500,10 +500,7 @@
     return jnp.where(iota((8, 128), 1) < HALF, x, pltpu.roll(x, HALF, 1))
 
 
-def send_table_kernel(pos_ref, charge_ref, count_ref, cen_ref, near_ref, far_ref, basis_ref):
-    boxes = charge_ref.shape[0]
-    lane = iota((8, 128), 1)
-    sub = iota((8, 128), 0)
+def fill_basis(pos_ref, basis_ref):
     for d in range(3):
         x = pos_ref[d]
         second = 2.0 * x * x - 1.0
@@ -513,17 +510,29 @@
             value = math.cos(theta) * x + math.cos(2 * theta) * second + math.cos(3 * theta) * third
             basis_ref[4 * d + i] = 0.25 + 0.5 * value
 
+
+def basis_table(basis_ref, b):
+    sub = iota((8, 128), 0)
+    row = lambda i, d: jnp.broadcast_to(basis_ref[4 * d + i, pl.ds(b, 1), :], (8, 128))
+    sub4 = sub % 4
+    zs = jnp.where(sub4 == 0, row(0, 2), jnp.where(sub4 == 1, row(1, 2), jnp.where(sub4 == 2, row(2, 2), row(3, 2))))
+    ys = [jnp.where(sub < 4, row(0, 1), row(1, 1)) * zs, jnp.where(sub < 4, row(2, 1), row(3, 1)) * zs]
+    return jnp.concatenate([row(i, 0) * ys[j] for i in range(NODES) for j in range(2)], axis=0)
+
+
+def send_table_kernel(pos_ref, charge_ref, count_ref, cen_ref, near_ref, far_ref, basis_ref):
+    boxes = charge_ref.shape[0]
+    lane = iota((8, 128), 1)
+    sub = iota((8, 128), 0)
+    fill_basis(pos_ref, basis_ref)
+
     def body(b, carry):
         q = jnp.where(lane < count_ref[b], charge_ref[b], 0.0)
         near_ref[b, 0:8] = doubled(q)
         x, y, z = [doubled(cen_ref[d, b] + 0.5 * jnp.broadcast_to(pos_ref[d, pl.ds(b, 1), :], (8, 128))) for d in range(3)]
         near_ref[b, 8:16] = jnp.where(sub == 4, x, jnp.where(sub == 5, y, z))
         near_ref[b, 16:24] = jnp.where(sub == 7, x, jnp.where((sub == 3) | (sub == 5), y, z))
-        row = lambda i, d: jnp.broadcast_to(basis_ref[4 * d + i, pl.ds(b, 1), :], (8, 128))
-        sub4 = sub % 4
-        zs = jnp.where(sub4 == 0, row(0, 2), jnp.where(sub4 == 1, row(1, 2), jnp.where(sub4 == 2, row(2, 2), row(3, 2))))
-        ys = [jnp.where(sub < 4, row(0, 1), row(1, 1)) * zs, jnp.where(sub < 4, row(2, 1), row(3, 1)) * zs]
-        table = jnp.concatenate([row(i, 0) * ys[j] for i in range(NODES) for j in range(2)], axis=0)
+        table = basis_table(basis_ref, b)
         qs = jnp.concatenate(split(q), axis=0)
         weight = fold(dot(qs, stack_kernel(table), NT))
         far_ref[b] = weight + pltpu.roll(weight, 64, 1)
@@ -532,7 +541,7 @@
     lax.fori_loop(0, boxes, body, 0, unroll=32)
 
 
-def own_table_kernel(pos_ref, charge_ref, count_ref, q_ref, f_ref, base_ref, t_ref):
+def own_table_kernel(pos_ref, charge_ref, count_ref, q_ref, f_ref, base_ref):
     boxes = charge_ref.shape[0]
     sub = iota((8, 128), 0)
     lane = iota((8, 128), 1)
@@ -541,7 +550,6 @@
         q = jnp.where(lane < count_ref[b], charge_ref[b], 0.0)
         q_ref[b] = q
         x = point_rows(pos_ref, b)
-        t_ref[b] = stack_kernel(cheb_rows(x))
         rel = (0.5 * ROOT3) * x
         tgt = planes(rel, False)
         for unit in range(2):
@@ -656,7 +664,7 @@
             buf_ref[at(32), :] = jnp.where(keep, rows(ex_ref, 8, 0), jnp.where(second, p[1], p[0]))
         return carry
 
-    chunks = 4
+    chunks = 8
     each = peers // chunks
     stores = []
     for c in range(chunks):
@@ -669,8 +677,8 @@
 
 
 def duo_kernel(
-    scale, got_ref, want_hbm, nc_hbm, ec_hbm, f_hbm, base_hbm, q_hbm, w_hbm, v_hbm, near_hbm, far_hbm, term_ref,
-    tgt_ref, nc_ref, ec_ref, f_ref, base_ref, q_ref, w_ref, v_ref, near_ref, far_ref, sems, *bufs
+    scale, got_ref, want_hbm, nc_hbm, ec_hbm, f_hbm, base_hbm, q_hbm, w_hbm, v_hbm, near0_hbm, near1_hbm, far0_hbm, far1_hbm, term_ref,
+    tgt_ref, nc_ref, ec_ref, f_ref, base_ref, q_ref, w_ref, v_ref, sems, *bufs
 ):
     whole = [(want_hbm, tgt_ref), (nc_hbm, nc_ref), (ec_hbm, ec_ref), (f_hbm, f_ref)]
     whole += [(base_hbm, base_ref), (q_hbm, q_ref), (w_hbm, w_ref)]
@@ -790,26 +798,19 @@
     values(dist_refs[1], value_refs[0])
     products(duos - 1, value_refs[0])
 
+    sums = (near0_hbm, near1_hbm, far0_hbm, far1_hbm)
+    stores = [pltpu.make_async_copy(a, b, sems.at[8 + i]) for i, (a, b) in enumerate(zip(near_accs + far_accs, sums))]
+    for copy in stores:
+        copy.start()
     for copy in loads[4:]:
         copy.wait()
 
     def finish(b, total):
         near = near_accs[0][b] + near_accs[1][b] + base_ref[b]
         far = jnp.where(left, far_accs[0][b], far_accs[1][b])
-        near_ref[b] = near
-        far_ref[b] = far
         return total + near * q_ref[b] + far * w_ref[b]
 
-    total = jnp.zeros((8, 128), F32)
-    stores = []
-    quarter = boxes // 4
-    for part in range(4):
-        total = lax.fori_loop(part * quarter, part * quarter + quarter, finish, total, unroll=16)
-        at = pl.ds(part * quarter, quarter)
-        for source, target, sem in ((near_ref, near_hbm, 8 + part), (far_ref, far_hbm, 12 + part)):
-            copy = pltpu.make_async_copy(source.at[at], target.at[at], sems.at[sem])
-            copy.start()
-            stores.append(copy)
+    total = lax.fori_loop(0, boxes, finish, jnp.zeros((8, 128), F32), unroll=16)
     ones = jnp.ones((128, 128), F32)
     sums = lax.dot_general(ones, total, NT, precision=lax.Precision.HIGHEST, preferred_element_type=F32)
     term_ref[...] = jnp.concatenate([sums * scale, jnp.zeros((128, 120), F32)], axis=1)
@@ -817,15 +818,18 @@
         copy.wait()
 
 
-def finish_kernel(count_ref, near_ref, far_ref, t_ref, out_ref):
-    boxes = near_ref.shape[0]
+def finish_kernel(count_ref, pos_ref, near0_ref, near1_ref, far0_ref, far1_ref, base_ref, out_ref, basis_ref):
+    boxes = base_ref.shape[0]
     lane = iota((8, 128), 1)
+    fill_basis(pos_ref, basis_ref)
 
     def body(b, carry):
-        ls = jnp.concatenate(split(far_ref[b]), axis=0)
-        high, low = t_ref[b, 0:64], t_ref[b, 64:128]
+        locs = jnp.where(lane < HALF, far0_ref[b], far1_ref[b])
+        ls = jnp.concatenate(split(locs), axis=0)
+        high, low = split(basis_table(basis_ref, b))
         far = fold(dot(jnp.concatenate([ls, ls], axis=1), jnp.concatenate([high, high, low, low], axis=0)))
-        out_ref[b] = jnp.where(lane < count_ref[b], near_ref[b] + far, 0.0)
+        near = near0_ref[b] + near1_ref[b] + base_ref[b]
+        out_ref[b] = jnp.where(lane < count_ref[b], near + far, 0.0)
         return carry
 
     lax.fori_loop(0, boxes, body, 0, unroll=16)
@@ -882,23 +886,18 @@
             pltpu.VMEM((16, devices), jnp.int32),
             pltpu.VMEM((boxes * 8, 128), F32),
             pltpu.VMEM((devices * ROWS, 128), F32),
-            pltpu.SemaphoreType.DMA((5,)),
+            pltpu.SemaphoreType.DMA((9,)),
         ],
         compiler_params=params(12),
         name="send",
     )(member, served, flat(near_tab), flat(far_tab), ex_own, *moved)
     got = flat(exchange(send.reshape(devices, ROWS // 4, 4, 128)))
 
-    q_tab, f_tab, base, cheb = pl.pallas_call(
+    q_tab, f_tab, base = pl.pallas_call(
         own_table_kernel,
-        out_shape=(
-            hbm((boxes, 8, 128), F32),
-            hbm((boxes, 2, 32, 128), BF),
-            hbm((boxes, 8, 128), F32),
-            hbm((boxes, 128, 128), BF),
-        ),
+        out_shape=(hbm((boxes, 8, 128), F32), hbm((boxes, 2, 32, 128), BF), hbm((boxes, 8, 128), F32)),
         in_specs=[vmem(), vmem(), SMEM],
-        out_specs=(vmem(), vmem(), vmem(), vmem()),
+        out_specs=(vmem(), vmem(), vmem()),
         compiler_params=params(8),
         cost_estimate=pl.CostEstimate(flops=200_000_000, bytes_accessed=4_000_000, transcendentals=2_000_000),
         name="own_tables",
@@ -933,11 +932,11 @@
     )(far_gap, jnp.asarray(far_sources(), BF))
 
     big = lambda dtype, rows: pltpu.VMEM((rows, 128), dtype)
-    near, far, term = pl.pallas_call(
+    *sums, term = pl.pallas_call(
         functools.partial(duo_kernel, 1.0 / (devices * boxes * slots)),
-        out_shape=(hbm((boxes, 8, 128), F32), hbm((boxes, 8, 128), F32), struct((devices, 128), F32)),
+        out_shape=(hbm((boxes, 8, 128), F32),) * 4 + (struct((devices, 128), F32),),
         in_specs=[vmem()] + [anywhere] * 8,
-        out_specs=(anywhere, anywhere, vmem()),
+        out_specs=(anywhere,) * 4 + (vmem(),),
         scratch_shapes=[
             pltpu.SMEM((16, devices), jnp.int32),
             pltpu.VMEM((devices, 8, 128), F32),
@@ -947,8 +946,6 @@
             pltpu.VMEM((boxes, 8, 128), F32),
             pltpu.VMEM((boxes, 8, 128), F32),
             pltpu.VMEM((devices, 256, 128), BF),
-            pltpu.VMEM((boxes, 8, 128), F32),
-            pltpu.VMEM((boxes, 8, 128), F32),
             pltpu.SemaphoreType.DMA((20,)),
         ]
         + [big(BF, 128)] * 2
@@ -965,12 +962,13 @@
     product = pl.pallas_call(
         finish_kernel,
         out_shape=table,
-        in_specs=[SMEM] + [vmem()] * 3,
+        in_specs=[SMEM] + [vmem()] * 6,
         out_specs=vmem(),
+        scratch_shapes=[pltpu.VMEM((12, boxes, 128), F32)],
         compiler_params=params(8),
         cost_estimate=pl.CostEstimate(flops=50_000_000, bytes_accessed=3_000_000, transcendentals=0),
         name="finish",
-    )(counts, stay(near), stay(far), stay(cheb))
+    )(counts, pos, *[stay(x) for x in (*sums, base)])
     over = jnp.any((served.reshape(devices, 2, 128)[:, 0, 9] > HALF) & (jnp.arange(devices) % 4 != 0))
     whole = (local_pos, charges, counts, box_centers, far_list, near_list)
     return lax.cond(over, lambda: general(*whole), lambda: (product, curvature))

time: 109 us -> 108 us (level)
  Pallas kernels: 51.9 us -> 50.3 us
where the time goes in v6:
time: 108 us; the launch traced here: 107 us
  Pallas kernels  50.3 us (47%)
  waiting for transfers between devices  25.4 us (24%)
  starting transfers between devices  25.3 us (23%)
  other arithmetic  3.82 us (4%)
  between operations  1.45 us (1%)
  local copies, waits for them, and re-layouts  1.09 us (1%)
    all_to_all x3, waiting for transfers between devices, exchange(): return lax.all_to_all(x, AXES, split_axis=0, concat_axis=0, tiled=True)  25.4 us
    all_to_all x3, starting transfers between devices, exchange(): return lax.all_to_all(x, AXES, split_axis=0, concat_axis=0, tiled=True)  17.7 us
    pallas_call x1, Pallas kernels, on_device(): pl.pallas_call(functools.partial(duo_kernel, 1.0 / (devices * boxes * slo...  16.8 us
    pallas_call x1, Pallas kernels, on_device(): pl.pallas_call(far_kernel, grid=(devices // group,), out_shape=hbm((devic...  9.77 us
    pallas_call x1, Pallas kernels, on_device(): pl.pallas_call(own_table_kernel, out_shape=(hbm((boxes, 8, 128), F32), hb...  8.92 us
    ppermute x3, starting transfers between devices, on_device(): lax.ppermute(ex_own, 'gy', [(4 * z, 4 * z + k) for z in range(4)])  7.63 us
    pallas_call x1, Pallas kernels, on_device(): pl.pallas_call(finish_kernel, out_shape=table, in_specs=[SMEM] + [vmem()]...  3.17 us
    pallas_call x1, Pallas kernels, on_device(): pl.pallas_call(goal_kernel, out_shape=(hbm((devices * 8, 128), F32), hbm(...  2.68 us
  transfers between devices with their start and end apart: 6, of which 3 were waited for; matrix products, arithmetic and copies ran while one was open for 3% of the time, Pallas kernels for 28%

profile of v6, /device:TPU:1, one launch (start us, length us, event | category | flops | bytes accessed | tf_op | source)
XLA Modules:
  0.0 107.4 jit_solution(14307953777336577633)
XLA Ops:
  0.6 1.4 %upper_halves.1.own_ref = f32[352,128]{1,0:T(8,128)S(1)} custom-call(f32[3,64,128]{2,1,0:T(8,128)} %bitcast.44, f32[64,8,128]{2,1,0:T(8,128)} %charge_ref.5, s32[64]{0:T(128)} %count_ref.7, f32[3,64]{1,0:T(4,128)} %cen_ref.3), custom_call_target="tpu_custom_call" | custom-call | tf_op jit(solution)/shard_map/upper_halves/pallas_call | solution.py:849
  2.0 4.0 %collective-permute-start = (f32[352,128]{1,0:T(8,128)S(1)}, f32[352,128]{1,0:T(8,128)S(1)}, u32[]{:S(2)}, u32[]{:S(2)}) collective-permute-start(f32[352,128]{1,0:T(8,128)S(1)} %upper_halves.1.own_ref), channel_id=1, source_target_pairs={{0,1},{4,5},{8,9},{12,13},{16,17},{20,21},{24,25},{28,29},{32,33},... | collective-permute-start | bytes 540680 | tf_op jit(solution)/shard_map/ppermute | solution.py:865
  6.1 2.3 %collective-permute-start.1 = (f32[352,128]{1,0:T(8,128)S(1)}, f32[352,128]{1,0:T(8,128)S(1)}, u32[]{:S(2)}, u32[]{:S(2)}) collective-permute-start(f32[352,128]{1,0:T(8,128)S(1)} %upper_halves.1.own_ref), channel_id=1, source_target_pairs={{0,2},{4,6},{8,10},{12,14},{16,18},{20,22},{24,26},{28,30},{32,34}... | collective-permute-start | bytes 540680 | tf_op jit(solution)/shard_map/ppermute | solution.py:865
  8.4 1.3 %collective-permute-start.2 = (f32[352,128]{1,0:T(8,128)S(1)}, f32[352,128]{1,0:T(8,128)S(1)}, u32[]{:S(2)}, u32[]{:S(2)}) collective-permute-start(f32[352,128]{1,0:T(8,128)S(1)} %upper_halves.1.own_ref), channel_id=1, source_target_pairs={{0,3},{4,7},{8,11},{12,15},{16,19},{20,23},{24,27},{28,31},{32,35}... | collective-permute-start | bytes 540680 | tf_op jit(solution)/shard_map/ppermute | solution.py:865
  9.7 2.5 %start.1 = (f32[256,128]{1,0:T(8,128)}, s32[128,128]{1,0:T(8,128)S(1)}) custom-call(s32[8,64]{1,0:T(8,128)} %bitcast.56, s32[9,64]{1,0:T(8,128)} %bitcast.54, s32[1,64]{1,0:T(1,128)} %bitcast.57, f32[3,64]{1,0:T(4,128)} %cen_ref.3), custom_call_target="tpu_custom_call" | custom-call | tf_op jit(solution)/shard_map/start/pallas_call | solution.py:857
  12.2 8.3 %all-to-all-start.3 = ((f32[128,2,128]{2,1,0:T(2,128)}), f32[128,2,128]{2,1,0:T(2,128)S(1)}, u32[]{:S(2)}, u32[]{:S(2)}) async-start(f32[128,2,128]{2,1,0:T(2,128)} %bitcast.19), calls=%async_computation.3 | async-start | bytes 262144 | tf_op jit(solution)/shard_map/all_to_all | solution.py:318
  20.5 2.6 %send_tables.1 = (f32[64,24,128]{2,1,0:T(8,128)S(1)}, f32[64,8,128]{2,1,0:T(8,128)S(1)}) custom-call(f32[3,64,128]{2,1,0:T(8,128)} %bitcast.45, f32[64,8,128]{2,1,0:T(8,128)} %charge_ref.5, s32[64]{0:T(128)} %count_ref.7, f32[3,64]{1,0:T(4,128)} %cen_ref.3), custom_call_target="tpu_custom_call" | custom-call | flops 50000000 | bytes 1200000 | tf_op jit(solution)/shard_map/send_tables/pallas_call | solution.py:868
  23.1 0.0 copy-start.1
  23.1 7.6 %all-to-all-done.3 = f32[128,2,128]{2,1,0:T(2,128)S(1)} async-done(((f32[128,2,128]{2,1,0:T(2,128)}), f32[128,2,128]{2,1,0:T(2,128)S(1)}, u32[]{:S(2)}, u32[]{:S(2)}) %all-to-all-start.3) | async-done | bytes 131104 | tf_op jit(solution)/shard_map/all_to_all | solution.py:318
  30.7 0.0 collective-permute-done.refs_0_
  30.7 0.0 collective-permute-done.1.refs_1_
  30.7 0.0 collective-permute-done.2.refs_2_
  30.7 0.0 copy-start.4
  30.7 0.0 copy-start.11
  30.7 2.6 %send.1 = f32[5632,128]{1,0:T(8,128)} custom-call(s32[1]{0:T(128)} %bitcast.20.member_ref, f32[256,128]{1,0:T(8,128)S(1)} %bitcast.34, f32[1536,128]{1,0:T(8,128)S(1)} %bitcast.36, f32[512,128]{1,0:T(8,128)S(1)} %bitcast.38, f32[352,128]{1,0:T(8,128)S(1)} %upper_halves.1.own_ref, f32[352,128]{1,0:T(8,128)S(1)} %collective-permute-done.refs_0_, ...), custom_call_target="tpu_custom_call" | custom-call | tf_op jit(solution)/shard_map/send/pallas_call | solution.py:879
  33.3 0.0 copy-start.2
  33.3 0.0 copy-start.7
  33.3 0.0 copy-start.8
  33.3 0.0 copy-done.1
  33.3 4.0 %all-to-all-start.4 = ((f32[128,11,4,128]{3,2,1,0:T(4,128)}), f32[128,11,4,128]{3,2,1,0:T(4,128)S(1)}, u32[]{:S(2)}, u32[]{:S(2)}) async-start(f32[128,11,4,128]{3,2,1,0:T(4,128)} %bitcast.41), calls=%async_computation.4 | async-start | bytes 5767168 | tf_op jit(solution)/shard_map/all_to_all | solution.py:318
  37.3 0.0 copy-done.4
  37.4 0.0 copy-done.11
  37.4 8.9 %own_tables.1 = (f32[64,8,128]{2,1,0:T(8,128)}, bf16[64,2,32,128]{3,2,1,0:T(8,128)(2,1)}, f32[64,8,128]{2,1,0:T(8,128)}) custom-call(f32[3,64,128]{2,1,0:T(8,128)S(1)} %bitcast.46, f32[64,8,128]{2,1,0:T(8,128)} %charge_ref.5, s32[64]{0:T(128)S(1)} %copy-done.11), custom_call_target="tpu_custom_call" | custom-call | flops 200000000 | bytes 4000000 | tf_op jit(solution)/shard_map/own_tables/pallas_call | solution.py:896
  46.3 0.0 copy-done.2
  46.3 0.0 copy-done.7
  46.3 2.7 %goals.1 = (f32[1024,128]{1,0:T(8,128)}, f32[1024,128]{1,0:T(8,128)}, f32[512,128]{1,0:T(8,128)}, s32[16,128]{1,0:T(8,128)}) custom-call(s32[128,128]{1,0:T(8,128)S(1)} %get-tuple-element.64.want_ref, f32[256,128]{1,0:T(8,128)S(1)} %bitcast.35, f32[3,64]{1,0:T(4,128)S(1)} %copy-done.7, f32[8,128]{1,0:T(8,128)S(1)} %copy-done.2), custom_call_target="tpu_custom_call" | custom-call | flops 50000000 | bytes 2000000 | tf_op jit(solution)/shard_map/goals/pallas_call | solution.py:906
  49.0 0.0 copy-done.8
  49.0 0.0 copy-start
  49.0 1.0 copy-done
  50.0 9.8 %far_values.1.v_hbm = bf16[128,256,128]{2,1,0:T(8,128)(2,1)} custom-call(f32[128,8,128]{2,1,0:T(8,128)S(1)} %bitcast.37, bf16[128,32]{1,0:T(8,128)(2,1)S(1)} %copy-done.8), custom_call_target="tpu_custom_call" | custom-call | flops 200000000 | bytes 9000000 | tf_op jit(solution)/shard_map/far_values/pallas_call | solution.py:923
  59.8 2.5 %compare_reduce_fusion = pred[128]{0:T(512)(128)(4,1)S(1)} fusion(f32[128,2,128]{2,1,0:T(2,128)S(1)} %all-to-all-done.3), kind=kLoop, calls=%fused_computation.10 | loop fusion | flops 128 | bytes 640 | tf_op jit(solution)/shard_map/gt | solution.py:972
  62.3 12.5 %all-to-all-done.4 = f32[128,11,4,128]{3,2,1,0:T(4,128)S(1)} async-done(((f32[128,11,4,128]{3,2,1,0:T(4,128)}), f32[128,11,4,128]{3,2,1,0:T(4,128)S(1)}, u32[]{:S(2)}, u32[]{:S(2)}) %all-to-all-start.4) | async-done | bytes 2883616 | tf_op jit(solution)/shard_map/all_to_all | solution.py:318
  74.8 0.0 copy-start.5
  74.8 0.0 copy-start.9
  74.8 0.0 copy-start.10
  74.8 16.8 %pairs.3 = (f32[64,8,128]{2,1,0:T(8,128)}, f32[64,8,128]{2,1,0:T(8,128)}, f32[64,8,128]{2,1,0:T(8,128)}, f32[64,8,128]{2,1,0:T(8,128)}, f32[128,128]{1,0:T(8,128)}) custom-call(f32[5632,128]{1,0:T(8,128)S(1)} %bitcast.33, s32[16,128]{1,0:T(8,128)} %get-tuple-element.65.want_hbm, f32[128,8,128]{2,1,0:T(8,128)} %bitcast.58, f32[64,8,128]{2,1,0:T(8,128)} %bitcast.59, ...), custom_call_target="tpu_custom_call" | custom-call | flops 1000000000 | bytes 12000000 | tf_op jit(solution)/shard_map/pairs/pallas_call | solution.py:935
  91.6 5.4 %all-to-all-start.5 = ((f32[128,1,128]{2,1,0:T(1,128)}), f32[128,1,128]{2,1,0:T(1,128)S(1)}, u32[]{:S(2)}, u32[]{:S(2)}) async-start(f32[128,1,128]{2,1,0:T(1,128)} %bitcast.31), calls=%async_computation.5 | async-start | bytes 131072 | tf_op jit(solution)/shard_map/all_to_all | solution.py:318
  97.0 0.6 and_reduce_fusion
  98.2 3.2 %finish.1 = f32[64,8,128]{2,1,0:T(8,128)} custom-call(s32[64]{0:T(128)S(1)} %copy-done.11, f32[3,64,128]{2,1,0:T(8,128)S(1)} %bitcast.47, f32[64,8,128]{2,1,0:T(8,128)} %get-tuple-element.73.near0_ref, f32[64,8,128]{2,1,0:T(8,128)} %get-tuple-element.74.near1_ref, f32[64,8,128]{2,1,0:T(8,128)} %get-tuple-element.75.far0_ref, ...), custom_call_target="tpu_custom_call" | custom-call | flops 50000000 | bytes 3000000 | tf_op jit(solution)/shard_map/finish/pallas_call | solution.py:962
  101.4 5.3 %all-to-all-done.5 = f32[128,1,128]{2,1,0:T(1,128)S(1)} async-done(((f32[128,1,128]{2,1,0:T(1,128)}), f32[128,1,128]{2,1,0:T(1,128)S(1)}, u32[]{:S(2)}, u32[]{:S(2)}) %all-to-all-start.5) | async-done | bytes 65568 | tf_op jit(solution)/shard_map/all_to_all | solution.py:318
  106.7 0.0 copy-done.5
  106.7 0.0 copy-done.9
  106.7 0.0 copy-done.10
  106.7 0.7 conditional.1
  106.8 0.7 slice_reduce_fusion
Async XLA Ops:
  2.0 28.7 %collective-permute-start = (f32[352,128]{1,0:T(8,128)S(1)}, f32[352,128]{1,0:T(8,128)S(1)}, u32[]{:S(2)}, u32[]{:S(2)}) collective-permute-start(f32[352,128]{1,0:T(8,128)S(1)} %upper_halves.1.own_ref), channel_id=1, source_target_pairs={{0,1},{4,5},{8,9},{12,13},{16,17},{20,21},{24,25},{28,29},{32,33},... | collective-permute-start | bytes 540680 | tf_op jit(solution)/shard_map/ppermute | solution.py:865
  6.1 24.6 %collective-permute-start.1 = (f32[352,128]{1,0:T(8,128)S(1)}, f32[352,128]{1,0:T(8,128)S(1)}, u32[]{:S(2)}, u32[]{:S(2)}) collective-permute-start(f32[352,128]{1,0:T(8,128)S(1)} %upper_halves.1.own_ref), channel_id=1, source_target_pairs={{0,2},{4,6},{8,10},{12,14},{16,18},{20,22},{24,26},{28,30},{32,34}... | collective-permute-start | bytes 540680 | tf_op jit(solution)/shard_map/ppermute | solution.py:865
  8.4 22.3 %collective-permute-start.2 = (f32[352,128]{1,0:T(8,128)S(1)}, f32[352,128]{1,0:T(8,128)S(1)}, u32[]{:S(2)}, u32[]{:S(2)}) collective-permute-start(f32[352,128]{1,0:T(8,128)S(1)} %upper_halves.1.own_ref), channel_id=1, source_target_pairs={{0,3},{4,7},{8,11},{12,15},{16,19},{20,23},{24,27},{28,31},{32,35}... | collective-permute-start | bytes 540680 | tf_op jit(solution)/shard_map/ppermute | solution.py:865
  12.2 18.5 %all-to-all-start.3 = ((f32[128,2,128]{2,1,0:T(2,128)}), f32[128,2,128]{2,1,0:T(2,128)S(1)}, u32[]{:S(2)}, u32[]{:S(2)}) async-start(f32[128,2,128]{2,1,0:T(2,128)} %bitcast.19), calls=%async_computation.3 | async-start | bytes 262144 | tf_op jit(solution)/shard_map/all_to_all | solution.py:318
  23.1 10.3 %copy-start.1 = (f32[64,8,128]{2,1,0:T(8,128)}, f32[64,8,128]{2,1,0:T(8,128)S(1)}, u32[]{:S(2)}) copy-start(f32[64,8,128]{2,1,0:T(8,128)S(1)} %get-tuple-element.63.w_hbm) | copy-start | bytes 786436
  30.7 6.7 %copy-start.4 = (f32[64,3,128]{2,0,1:T(8,128)S(1)}, f32[64,3,128]{2,0,1:T(8,128)}, u32[]{:S(2)}) copy-start(f32[64,3,128]{2,0,1:T(8,128)} %param.12) | copy-start | bytes 294916
  30.7 6.7 %copy-start.11 = (s32[64]{0:T(128)S(1)}, s32[64]{0:T(128)}, u32[]{:S(2)}) copy-start(s32[64]{0:T(128)} %count_ref.7) | copy-start | bytes 772
  33.3 13.0 %copy-start.2 = (f32[8,128]{1,0:T(8,128)S(1)}, f32[8,128]{1,0:T(8,128)}, u32[]{:S(2)}) copy-start(f32[8,128]{1,0:T(8,128)} %constant.51.clone.node_ref) | copy-start | bytes 12292
  33.3 13.0 %copy-start.7 = (f32[3,64]{1,0:T(4,128)S(1)}, f32[3,64]{1,0:T(4,128)}, u32[]{:S(2)}) copy-start(f32[3,64]{1,0:T(4,128)} %cen_ref.3) | copy-start | bytes 2308
  33.3 15.7 %copy-start.8 = (bf16[128,32]{1,0:T(8,128)(2,1)S(1)}, bf16[128,32]{1,0:T(8,128)(2,1)}, u32[]{:S(2)}) copy-start(bf16[128,32]{1,0:T(8,128)(2,1)} %constant.52.clone.fn_ref) | copy-start | bytes 24580
  33.3 41.5 %all-to-all-start.4 = ((f32[128,11,4,128]{3,2,1,0:T(4,128)}), f32[128,11,4,128]{3,2,1,0:T(4,128)S(1)}, u32[]{:S(2)}, u32[]{:S(2)}) async-start(f32[128,11,4,128]{3,2,1,0:T(4,128)} %bitcast.41), calls=%async_computation.4 | async-start | bytes 5767168 | tf_op jit(solution)/shard_map/all_to_all | solution.py:318
  49.0 1.0 copy-start
  74.8 31.9 %copy-start.5 = (f32[64,8,128]{2,1,0:T(8,128)S(1)}, f32[64,8,128]{2,1,0:T(8,128)}, u32[]{:S(2)}) copy-start(f32[64,8,128]{2,1,0:T(8,128)} %charge_ref.5) | copy-start | bytes 786436
  74.8 31.9 %copy-start.9 = (s32[64,9]{0,1:T(8,128)S(1)}, s32[64,9]{0,1:T(8,128)}, u32[]{:S(2)}) copy-start(s32[64,9]{0,1:T(8,128)} %param.17) | copy-start | bytes 6916
  74.8 31.9 %copy-start.10 = (s32[64,8]{0,1:T(8,128)S(1)}, s32[64,8]{0,1:T(8,128)}, u32[]{:S(2)}) copy-start(s32[64,8]{0,1:T(8,128)} %param.16) | copy-start | bytes 6148
  91.6 15.1 %all-to-all-start.5 = ((f32[128,1,128]{2,1,0:T(1,128)}), f32[128,1,128]{2,1,0:T(1,128)S(1)}, u32[]{:S(2)}, u32[]{:S(2)}) async-start(f32[128,1,128]{2,1,0:T(1,128)} %bitcast.31), calls=%async_computation.5 | async-start | bytes 131072 | tf_op jit(solution)/shard_map/all_to_all | solution.py:318

commit v7 on v6

--- a/solution.py
+++ b/solution.py
@@ -429,7 +429,13 @@
     lax.fori_loop(0, half, body, 0, unroll=16)
 
 
-def start_kernel(far_ref, near_ref, most_ref, row_ref, msg_ref, want_ref):
+def start_kernel(
+    far_ref, near_ref, most_ref, row_ref, count_ref, pos_hbm, charge_hbm, msg_hbm, want_ref, ex_ref,
+    pos_ref, charge_ref, msg_ref, sems
+):
+    loads = [pltpu.make_async_copy(pos_hbm, pos_ref, sems.at[0]), pltpu.make_async_copy(charge_hbm, charge_ref, sems.at[1])]
+    for copy in loads:
+        copy.start()
     boxes = far_ref.shape[1]
     slots = far_ref.shape[0]
     peer = iota((128, 128), 0)
@@ -471,6 +477,12 @@
     rows = [jnp.broadcast_to(row, (128, 128)) for row in rows]
     msg_ref[pl.ds(0, 128, stride=2), :] = jnp.where(line < HALF, result, rows[2])
     msg_ref[pl.ds(1, 128, stride=2), :] = jnp.where(line < HALF, rows[0], rows[1])
+    store = pltpu.make_async_copy(msg_ref, msg_hbm, sems.at[2])
+    store.start()
+    for copy in loads:
+        copy.wait()
+    upper_kernel(pos_ref, charge_ref, count_ref, row_ref, ex_ref)
+    store.wait()
 
 
 def cheb_rows(x):
@@ -846,22 +858,24 @@
     table = struct((boxes, 8, 128), F32)
     flat = lambda x: x.reshape(-1, 128)
     member = (lax.axis_index("gy") % 4).astype(jnp.int32).reshape(1)
-    ex_own = pl.pallas_call(
-        upper_kernel,
-        out_shape=struct((boxes * 11 // 2, 128), F32),
-        in_specs=[vmem(), vmem(), SMEM, vmem()],
-        out_specs=vmem(),
-        compiler_params=params(8),
-        name="upper_halves",
-    )(pos, charges, counts, box_centers)
-    msg, want = pl.pallas_call(
+    msg, want, ex_own = pl.pallas_call(
         start_kernel,
-        out_shape=(struct((devices * 2, 128), F32), struct((devices, 128), jnp.int32)),
-        in_specs=[vmem()] * 4,
-        out_specs=(vmem(), vmem()),
+        out_shape=(
+            hbm((devices * 2, 128), F32),
+            struct((devices, 128), jnp.int32),
+            struct((boxes * 11 // 2, 128), F32),
+        ),
+        in_specs=[vmem()] * 4 + [SMEM, anywhere, anywhere],
+        out_specs=(anywhere, vmem(), vmem()),
+        scratch_shapes=[
+            pltpu.VMEM((3, boxes, 128), F32),
+            pltpu.VMEM((boxes, 8, 128), F32),
+            pltpu.VMEM((devices * 2, 128), F32),
+            pltpu.SemaphoreType.DMA((3,)),
+        ],
         compiler_params=params(8),
         name="start",
-    )(far_list.T, near_list.T, counts.reshape(1, boxes), box_centers)
+    )(far_list.T, near_list.T, counts.reshape(1, boxes), box_centers, counts, stay(pos), stay(charges))
     moved = [lax.ppermute(ex_own, "gy", [(4 * z, 4 * z + k) for z in range(4)]) for k in range(1, 4)]
     served = flat(exchange(msg.reshape(devices, 2, 128)))
 

time: 108 us -> 107 us (level)
  Pallas kernels: 50.3 us -> 49.1 us
    pallas_call x2 -> x1, Pallas kernels: 3.87 us -> 2.58 us  [on_device(): pl.pallas_call(start_kernel, out_shape=(hbm((devices * 2, 128), F32), str...]
  transfers between devices with their start and end apart: 6 -> 6, of which waited for: 3 -> 3; matrix products, arithmetic and copies ran while one was open for 3% -> 3% of each run, Pallas kernels for 28% -> 26%
where the time goes in v7:
time: 107 us; the launch traced here: 106 us
  Pallas kernels  49.1 us (46%)
  waiting for transfers between devices  25.4 us (24%)
  starting transfers between devices  25.3 us (24%)
  other arithmetic  3.82 us (4%)
  between operations  1.45 us (1%)
  local copies, waits for them, and re-layouts  1.09 us (1%)
    all_to_all x3, waiting for transfers between devices, exchange(): return lax.all_to_all(x, AXES, split_axis=0, concat_axis=0, tiled=True)  25.4 us
    all_to_all x3, starting transfers between devices, exchange(): return lax.all_to_all(x, AXES, split_axis=0, concat_axis=0, tiled=True)  17.7 us
    pallas_call x1, Pallas kernels, on_device(): pl.pallas_call(functools.partial(duo_kernel, 1.0 / (devices * boxes * slo...  16.8 us
    pallas_call x1, Pallas kernels, on_device(): pl.pallas_call(far_kernel, grid=(devices // group,), out_shape=hbm((devic...  9.77 us
    pallas_call x1, Pallas kernels, on_device(): pl.pallas_call(own_table_kernel, out_shape=(hbm((boxes, 8, 128), F32), hb...  8.92 us
    ppermute x3, starting transfers between devices, on_device(): lax.ppermute(ex_own, 'gy', [(4 * z, 4 * z + k) for z in range(4)])  7.63 us
    pallas_call x1, Pallas kernels, on_device(): pl.pallas_call(finish_kernel, out_shape=table, in_specs=[SMEM] + [vmem()]...  3.17 us
    pallas_call x1, Pallas kernels, on_device(): pl.pallas_call(goal_kernel, out_shape=(hbm((devices * 8, 128), F32), hbm(...  2.68 us
  transfers between devices with their start and end apart: 6, of which 3 were waited for; matrix products, arithmetic and copies ran while one was open for 3% of the time, Pallas kernels for 26%

profile of v7, /device:TPU:1, one launch (start us, length us, event | category | flops | bytes accessed | tf_op | source)
XLA Modules:
  0.0 106.1 jit_solution(16752210373860176019)
XLA Ops:
  0.6 2.6 %start.1 = (f32[256,128]{1,0:T(8,128)}, s32[128,128]{1,0:T(8,128)S(1)}, f32[352,128]{1,0:T(8,128)S(1)}) custom-call(s32[8,64]{1,0:T(8,128)} %bitcast.57, s32[9,64]{1,0:T(8,128)} %bitcast.55, s32[1,64]{1,0:T(1,128)} %bitcast.58, f32[3,64]{1,0:T(4,128)} %cen_ref.3, s32[64]{0:T(128)} %count_ref.7, f32[3,64,128]{2,1,0:T(8,128)} %bitcast.44, f32[64,8,128]{2,1,0:T(8,128)} %charge_ref.3), custom_call_target="tpu_custom_call" | custom-call | tf_op jit(solution)/shard_map/start/pallas_call | solution.py:861
  3.2 4.0 %collective-permute-start = (f32[352,128]{1,0:T(8,128)S(1)}, f32[352,128]{1,0:T(8,128)S(1)}, u32[]{:S(2)}, u32[]{:S(2)}) collective-permute-start(f32[352,128]{1,0:T(8,128)S(1)} %get-tuple-element.65.own_ref), channel_id=1, source_target_pairs={{0,1},{4,5},{8,9},{12,13},{16,17},{20,21},{24,25},{28,29},{32,33},... | collective-permute-start | bytes 540680 | tf_op jit(solution)/shard_map/ppermute | solution.py:879
  7.3 2.3 %collective-permute-start.1 = (f32[352,128]{1,0:T(8,128)S(1)}, f32[352,128]{1,0:T(8,128)S(1)}, u32[]{:S(2)}, u32[]{:S(2)}) collective-permute-start(f32[352,128]{1,0:T(8,128)S(1)} %get-tuple-element.65.own_ref), channel_id=1, source_target_pairs={{0,2},{4,6},{8,10},{12,14},{16,18},{20,22},{24,26},{28,30},{32,34}... | collective-permute-start | bytes 540680 | tf_op jit(solution)/shard_map/ppermute | solution.py:879
  9.6 1.3 %collective-permute-start.2 = (f32[352,128]{1,0:T(8,128)S(1)}, f32[352,128]{1,0:T(8,128)S(1)}, u32[]{:S(2)}, u32[]{:S(2)}) collective-permute-start(f32[352,128]{1,0:T(8,128)S(1)} %get-tuple-element.65.own_ref), channel_id=1, source_target_pairs={{0,3},{4,7},{8,11},{12,15},{16,19},{20,23},{24,27},{28,31},{32,35}... | collective-permute-start | bytes 540680 | tf_op jit(solution)/shard_map/ppermute | solution.py:879
  10.9 8.3 %all-to-all-start.3 = ((f32[128,2,128]{2,1,0:T(2,128)}), f32[128,2,128]{2,1,0:T(2,128)S(1)}, u32[]{:S(2)}, u32[]{:S(2)}) async-start(f32[128,2,128]{2,1,0:T(2,128)} %bitcast.52), calls=%async_computation.3 | async-start | bytes 262144 | tf_op jit(solution)/shard_map/all_to_all | solution.py:318
  19.2 2.6 %send_tables.1 = (f32[64,24,128]{2,1,0:T(8,128)S(1)}, f32[64,8,128]{2,1,0:T(8,128)S(1)}) custom-call(f32[3,64,128]{2,1,0:T(8,128)} %bitcast.45, f32[64,8,128]{2,1,0:T(8,128)} %charge_ref.3, s32[64]{0:T(128)} %count_ref.7, f32[3,64]{1,0:T(4,128)} %cen_ref.3), custom_call_target="tpu_custom_call" | custom-call | flops 50000000 | bytes 1200000 | tf_op jit(solution)/shard_map/send_tables/pallas_call | solution.py:882
  21.8 0.0 copy-start.1
  21.8 7.6 %all-to-all-done.3 = f32[128,2,128]{2,1,0:T(2,128)S(1)} async-done(((f32[128,2,128]{2,1,0:T(2,128)}), f32[128,2,128]{2,1,0:T(2,128)S(1)}, u32[]{:S(2)}, u32[]{:S(2)}) %all-to-all-start.3) | async-done | bytes 131104 | tf_op jit(solution)/shard_map/all_to_all | solution.py:318
  29.4 0.0 collective-permute-done.refs_0_
  29.4 0.0 collective-permute-done.1.refs_1_
  29.4 0.0 collective-permute-done.2.refs_2_
  29.4 0.0 copy-start.4
  29.4 0.0 copy-start.11
  29.4 2.6 %send.1 = f32[5632,128]{1,0:T(8,128)} custom-call(s32[1]{0:T(128)} %bitcast.21.member_ref, f32[256,128]{1,0:T(8,128)S(1)} %bitcast.34, f32[1536,128]{1,0:T(8,128)S(1)} %bitcast.36, f32[512,128]{1,0:T(8,128)S(1)} %bitcast.38, f32[352,128]{1,0:T(8,128)S(1)} %get-tuple-element.65.own_ref, f32[352,128]{1,0:T(8,128)S(1)} %collective-permute-done.refs_0_, ...), custom_call_target="tpu_custom_call" | custom-call | tf_op jit(solution)/shard_map/send/pallas_call | solution.py:893
  32.0 0.0 copy-start.2
  32.0 0.0 copy-start.8
  32.0 0.0 copy-start.7
  32.0 0.0 copy-done.1
  32.1 4.0 %all-to-all-start.4 = ((f32[128,11,4,128]{3,2,1,0:T(4,128)}), f32[128,11,4,128]{3,2,1,0:T(4,128)S(1)}, u32[]{:S(2)}, u32[]{:S(2)}) async-start(f32[128,11,4,128]{3,2,1,0:T(4,128)} %bitcast.41), calls=%async_computation.4 | async-start | bytes 5767168 | tf_op jit(solution)/shard_map/all_to_all | solution.py:318
  36.1 0.0 copy-done.4
  36.1 0.0 copy-done.11
  36.1 8.9 %own_tables.1 = (f32[64,8,128]{2,1,0:T(8,128)}, bf16[64,2,32,128]{3,2,1,0:T(8,128)(2,1)}, f32[64,8,128]{2,1,0:T(8,128)}) custom-call(f32[3,64,128]{2,1,0:T(8,128)S(1)} %bitcast.46, f32[64,8,128]{2,1,0:T(8,128)} %charge_ref.3, s32[64]{0:T(128)S(1)} %copy-done.11), custom_call_target="tpu_custom_call" | custom-call | flops 200000000 | bytes 4000000 | tf_op jit(solution)/shard_map/own_tables/pallas_call | solution.py:910
  45.0 0.0 copy-done.2
  45.0 0.0 copy-done.8
  45.0 2.7 %goals.1 = (f32[1024,128]{1,0:T(8,128)}, f32[1024,128]{1,0:T(8,128)}, f32[512,128]{1,0:T(8,128)}, s32[16,128]{1,0:T(8,128)}) custom-call(s32[128,128]{1,0:T(8,128)S(1)} %get-tuple-element.66.want_ref, f32[256,128]{1,0:T(8,128)S(1)} %bitcast.35, f32[3,64]{1,0:T(4,128)S(1)} %copy-done.8, f32[8,128]{1,0:T(8,128)S(1)} %copy-done.2), custom_call_target="tpu_custom_call" | custom-call | flops 50000000 | bytes 2000000 | tf_op jit(solution)/shard_map/goals/pallas_call | solution.py:920
  47.7 0.0 copy-done.7
  47.7 0.0 copy-start
  47.7 1.0 copy-done
  48.8 9.8 %far_values.1.v_hbm = bf16[128,256,128]{2,1,0:T(8,128)(2,1)} custom-call(f32[128,8,128]{2,1,0:T(8,128)S(1)} %bitcast.37, bf16[128,32]{1,0:T(8,128)(2,1)S(1)} %copy-done.7), custom_call_target="tpu_custom_call" | custom-call | flops 200000000 | bytes 9000000 | tf_op jit(solution)/shard_map/far_values/pallas_call | solution.py:937
  58.5 2.5 %compare_reduce_fusion = pred[128]{0:T(512)(128)(4,1)S(1)} fusion(f32[128,2,128]{2,1,0:T(2,128)S(1)} %all-to-all-done.3), kind=kLoop, calls=%fused_computation.10 | loop fusion | flops 128 | bytes 640 | tf_op jit(solution)/shard_map/gt | solution.py:986
  61.0 12.5 %all-to-all-done.4 = f32[128,11,4,128]{3,2,1,0:T(4,128)S(1)} async-done(((f32[128,11,4,128]{3,2,1,0:T(4,128)}), f32[128,11,4,128]{3,2,1,0:T(4,128)S(1)}, u32[]{:S(2)}, u32[]{:S(2)}) %all-to-all-start.4) | async-done | bytes 2883616 | tf_op jit(solution)/shard_map/all_to_all | solution.py:318
  73.5 0.0 copy-start.5
  73.5 0.0 copy-start.9
  73.5 0.0 copy-start.10
  73.5 16.8 %pairs.3 = (f32[64,8,128]{2,1,0:T(8,128)}, f32[64,8,128]{2,1,0:T(8,128)}, f32[64,8,128]{2,1,0:T(8,128)}, f32[64,8,128]{2,1,0:T(8,128)}, f32[128,128]{1,0:T(8,128)}) custom-call(f32[5632,128]{1,0:T(8,128)S(1)} %bitcast.33, s32[16,128]{1,0:T(8,128)} %get-tuple-element.67.want_hbm, f32[128,8,128]{2,1,0:T(8,128)} %bitcast.59, f32[64,8,128]{2,1,0:T(8,128)} %bitcast.60, ...), custom_call_target="tpu_custom_call" | custom-call | flops 1000000000 | bytes 12000000 | tf_op jit(solution)/shard_map/pairs/pallas_call | solution.py:949
  90.3 5.3 %all-to-all-start.5 = ((f32[128,1,128]{2,1,0:T(1,128)}), f32[128,1,128]{2,1,0:T(1,128)S(1)}, u32[]{:S(2)}, u32[]{:S(2)}) async-start(f32[128,1,128]{2,1,0:T(1,128)} %bitcast.31), calls=%async_computation.5 | async-start | bytes 131072 | tf_op jit(solution)/shard_map/all_to_all | solution.py:318
  95.7 0.6 and_reduce_fusion
  97.0 3.2 %finish.1 = f32[64,8,128]{2,1,0:T(8,128)} custom-call(s32[64]{0:T(128)S(1)} %copy-done.11, f32[3,64,128]{2,1,0:T(8,128)S(1)} %bitcast.47, f32[64,8,128]{2,1,0:T(8,128)} %get-tuple-element.75.near0_ref, f32[64,8,128]{2,1,0:T(8,128)} %get-tuple-element.76.near1_ref, f32[64,8,128]{2,1,0:T(8,128)} %get-tuple-element.77.far0_ref, ...), custom_call_target="tpu_custom_call" | custom-call | flops 50000000 | bytes 3000000 | tf_op jit(solution)/shard_map/finish/pallas_call | solution.py:976
  100.1 5.3 %all-to-all-done.5 = f32[128,1,128]{2,1,0:T(1,128)S(1)} async-done(((f32[128,1,128]{2,1,0:T(1,128)}), f32[128,1,128]{2,1,0:T(1,128)S(1)}, u32[]{:S(2)}, u32[]{:S(2)}) %all-to-all-start.5) | async-done | bytes 65568 | tf_op jit(solution)/shard_map/all_to_all | solution.py:318
  105.4 0.0 copy-done.5
  105.5 0.0 copy-done.9
  105.5 0.0 copy-done.10
  105.5 0.7 conditional.1
  105.5 0.7 slice_reduce_fusion
Async XLA Ops:
  3.2 26.2 %collective-permute-start = (f32[352,128]{1,0:T(8,128)S(1)}, f32[352,128]{1,0:T(8,128)S(1)}, u32[]{:S(2)}, u32[]{:S(2)}) collective-permute-start(f32[352,128]{1,0:T(8,128)S(1)} %get-tuple-element.65.own_ref), channel_id=1, source_target_pairs={{0,1},{4,5},{8,9},{12,13},{16,17},{20,21},{24,25},{28,29},{32,33},... | collective-permute-start | bytes 540680 | tf_op jit(solution)/shard_map/ppermute | solution.py:879
  7.3 22.1 %collective-permute-start.1 = (f32[352,128]{1,0:T(8,128)S(1)}, f32[352,128]{1,0:T(8,128)S(1)}, u32[]{:S(2)}, u32[]{:S(2)}) collective-permute-start(f32[352,128]{1,0:T(8,128)S(1)} %get-tuple-element.65.own_ref), channel_id=1, source_target_pairs={{0,2},{4,6},{8,10},{12,14},{16,18},{20,22},{24,26},{28,30},{32,34}... | collective-permute-start | bytes 540680 | tf_op jit(solution)/shard_map/ppermute | solution.py:879
  9.6 19.9 %collective-permute-start.2 = (f32[352,128]{1,0:T(8,128)S(1)}, f32[352,128]{1,0:T(8,128)S(1)}, u32[]{:S(2)}, u32[]{:S(2)}) collective-permute-start(f32[352,128]{1,0:T(8,128)S(1)} %get-tuple-element.65.own_ref), channel_id=1, source_target_pairs={{0,3},{4,7},{8,11},{12,15},{16,19},{20,23},{24,27},{28,31},{32,35}... | collective-permute-start | bytes 540680 | tf_op jit(solution)/shard_map/ppermute | solution.py:879
  10.9 18.5 %all-to-all-start.3 = ((f32[128,2,128]{2,1,0:T(2,128)}), f32[128,2,128]{2,1,0:T(2,128)S(1)}, u32[]{:S(2)}, u32[]{:S(2)}) async-start(f32[128,2,128]{2,1,0:T(2,128)} %bitcast.52), calls=%async_computation.3 | async-start | bytes 262144 | tf_op jit(solution)/shard_map/all_to_all | solution.py:318
  21.8 10.3 %copy-start.1 = (f32[64,8,128]{2,1,0:T(8,128)}, f32[64,8,128]{2,1,0:T(8,128)S(1)}, u32[]{:S(2)}) copy-start(f32[64,8,128]{2,1,0:T(8,128)S(1)} %get-tuple-element.64.w_hbm) | copy-start | bytes 786436
  29.4 6.7 %copy-start.4 = (f32[64,3,128]{2,0,1:T(8,128)S(1)}, f32[64,3,128]{2,0,1:T(8,128)}, u32[]{:S(2)}) copy-start(f32[64,3,128]{2,0,1:T(8,128)} %param.12) | copy-start | bytes 294916
  29.4 6.7 %copy-start.11 = (s32[64]{0:T(128)S(1)}, s32[64]{0:T(128)}, u32[]{:S(2)}) copy-start(s32[64]{0:T(128)} %count_ref.7) | copy-start | bytes 772
  32.0 13.0 %copy-start.2 = (f32[8,128]{1,0:T(8,128)S(1)}, f32[8,128]{1,0:T(8,128)}, u32[]{:S(2)}) copy-start(f32[8,128]{1,0:T(8,128)} %constant.51.clone.node_ref) | copy-start | bytes 12292
  32.0 13.0 %copy-start.8 = (f32[3,64]{1,0:T(4,128)S(1)}, f32[3,64]{1,0:T(4,128)}, u32[]{:S(2)}) copy-start(f32[3,64]{1,0:T(4,128)} %cen_ref.3) | copy-start | bytes 2308
  32.0 15.7 %copy-start.7 = (bf16[128,32]{1,0:T(8,128)(2,1)S(1)}, bf16[128,32]{1,0:T(8,128)(2,1)}, u32[]{:S(2)}) copy-start(bf16[128,32]{1,0:T(8,128)(2,1)} %constant.52.clone.fn_ref) | copy-start | bytes 24580
  32.1 41.5 %all-to-all-start.4 = ((f32[128,11,4,128]{3,2,1,0:T(4,128)}), f32[128,11,4,128]{3,2,1,0:T(4,128)S(1)}, u32[]{:S(2)}, u32[]{:S(2)}) async-start(f32[128,11,4,128]{3,2,1,0:T(4,128)} %bitcast.41), calls=%async_computation.4 | async-start | bytes 5767168 | tf_op jit(solution)/shard_map/all_to_all | solution.py:318
  47.7 1.0 copy-start
  73.5 31.9 %copy-start.5 = (f32[64,8,128]{2,1,0:T(8,128)S(1)}, f32[64,8,128]{2,1,0:T(8,128)}, u32[]{:S(2)}) copy-start(f32[64,8,128]{2,1,0:T(8,128)} %charge_ref.3) | copy-start | bytes 786436
  73.5 31.9 %copy-start.9 = (s32[64,9]{0,1:T(8,128)S(1)}, s32[64,9]{0,1:T(8,128)}, u32[]{:S(2)}) copy-start(s32[64,9]{0,1:T(8,128)} %param.17) | copy-start | bytes 6916
  73.5 31.9 %copy-start.10 = (s32[64,8]{0,1:T(8,128)S(1)}, s32[64,8]{0,1:T(8,128)}, u32[]{:S(2)}) copy-start(s32[64,8]{0,1:T(8,128)} %param.16) | copy-start | bytes 6148
  90.3 15.1 %all-to-all-start.5 = ((f32[128,1,128]{2,1,0:T(1,128)}), f32[128,1,128]{2,1,0:T(1,128)S(1)}, u32[]{:S(2)}, u32[]{:S(2)}) async-start(f32[128,1,128]{2,1,0:T(1,128)} %bitcast.31), calls=%async_computation.5 | async-start | bytes 131072 | tf_op jit(solution)/shard_map/all_to_all | solution.py:318

commit v8 on v6

--- a/solution.py
+++ b/solution.py
@@ -429,7 +429,7 @@
     lax.fori_loop(0, half, body, 0, unroll=16)
 
 
-def start_kernel(far_ref, near_ref, most_ref, row_ref, msg_ref, want_ref):
+def sort_ids(far_ref, near_ref, most_ref, row_ref, msg_ref, want_ref):
     boxes = far_ref.shape[1]
     slots = far_ref.shape[0]
     peer = iota((128, 128), 0)
@@ -473,6 +473,39 @@
     msg_ref[pl.ds(1, 128, stride=2), :] = jnp.where(line < HALF, rows[0], rows[1])
 
 
+def first_kernel(
+    member_ref, count_ref, far_ref, near_ref, most_ref, row_ref, pos_hbm, charge_hbm, msg_hbm, want_hbm, ex_ref,
+    pos_ref, charge_ref, msg_ref, want_ref, sems
+):
+    @pl.when(member_ref[0] == 0)
+    def _():
+        loads = [pltpu.make_async_copy(pos_hbm, pos_ref, sems.at[0]), pltpu.make_async_copy(charge_hbm, charge_ref, sems.at[1])]
+        for copy in loads:
+            copy.start()
+        sort_ids(far_ref, near_ref, most_ref, row_ref, msg_ref, want_ref)
+        stores = [pltpu.make_async_copy(msg_ref, msg_hbm, sems.at[2]), pltpu.make_async_copy(want_ref, want_hbm, sems.at[3])]
+        for copy in stores:
+            copy.start()
+        for copy in loads:
+            copy.wait()
+        upper_kernel(pos_ref, charge_ref, count_ref, row_ref, ex_ref)
+        for copy in stores:
+            copy.wait()
+
+
+def second_kernel(
+    member_ref, far_ref, near_ref, most_ref, row_ref, msg_in, want_in, msg_hbm, want_hbm, msg_ref, want_ref, sems
+):
+    @pl.when(member_ref[0] != 0)
+    def _():
+        sort_ids(far_ref, near_ref, most_ref, row_ref, msg_ref, want_ref)
+        stores = [pltpu.make_async_copy(msg_ref, msg_hbm, sems.at[0]), pltpu.make_async_copy(want_ref, want_hbm, sems.at[1])]
+        for copy in stores:
+            copy.start()
+        for copy in stores:
+            copy.wait()
+
+
 def cheb_rows(x):
     sub = iota((8, 128), 0)
     second = 2.0 * x * x - 1.0
@@ -677,8 +710,8 @@
 
 
 def duo_kernel(
-    scale, got_ref, want_hbm, nc_hbm, ec_hbm, f_hbm, base_hbm, q_hbm, w_hbm, v_hbm, near0_hbm, near1_hbm, far0_hbm, far1_hbm, term_ref,
-    tgt_ref, nc_ref, ec_ref, f_ref, base_ref, q_ref, w_ref, v_ref, sems, *bufs
+    scale, got_ref, want_hbm, nc_hbm, ec_hbm, f_hbm, base_hbm, q_hbm, w_hbm, v_hbm, near0_hbm, near1_hbm, far0_hbm, far1_hbm, term_hbm,
+    tgt_ref, nc_ref, ec_ref, f_ref, base_ref, q_ref, w_ref, v_ref, term_ref, sems, *bufs
 ):
     whole = [(want_hbm, tgt_ref), (nc_hbm, nc_ref), (ec_hbm, ec_ref), (f_hbm, f_ref)]
     whole += [(base_hbm, base_ref), (q_hbm, q_ref), (w_hbm, w_ref)]
@@ -811,9 +844,14 @@
         return total + near * q_ref[b] + far * w_ref[b]
 
     total = lax.fori_loop(0, boxes, finish, jnp.zeros((8, 128), F32), unroll=16)
-    ones = jnp.ones((128, 128), F32)
-    sums = lax.dot_general(ones, total, NT, precision=lax.Precision.HIGHEST, preferred_element_type=F32)
+    high = total.astype(BF)
+    rest = total - high.astype(F32)
+    mid = rest.astype(BF)
+    parts = jnp.concatenate([high, mid, (rest - mid.astype(F32)).astype(BF)], axis=1)
+    sums = dot(jnp.ones((128, 384), BF), parts, NT)
     term_ref[...] = jnp.concatenate([sums * scale, jnp.zeros((128, 120), F32)], axis=1)
+    stores.append(pltpu.make_async_copy(term_ref, term_hbm, sems.at[12]))
+    stores[-1].start()
     for copy in stores:
         copy.wait()
 
@@ -846,22 +884,30 @@
     table = struct((boxes, 8, 128), F32)
     flat = lambda x: x.reshape(-1, 128)
     member = (lax.axis_index("gy") % 4).astype(jnp.int32).reshape(1)
-    ex_own = pl.pallas_call(
-        upper_kernel,
-        out_shape=struct((boxes * 11 // 2, 128), F32),
-        in_specs=[vmem(), vmem(), SMEM, vmem()],
-        out_specs=vmem(),
+    lists = (far_list.T, near_list.T, counts.reshape(1, boxes), box_centers)
+    ids_shape = (hbm((devices * 2, 128), F32), hbm((devices, 128), jnp.int32))
+    ids_scratch = [pltpu.VMEM((devices * 2, 128), F32), pltpu.VMEM((devices, 128), jnp.int32)]
+    msg, want, ex_own = pl.pallas_call(
+        first_kernel,
+        out_shape=ids_shape + (struct((boxes * 11 // 2, 128), F32),),
+        in_specs=[SMEM, SMEM] + [vmem()] * 4 + [anywhere] * 2,
+        out_specs=(anywhere, anywhere, vmem()),
+        scratch_shapes=[pltpu.VMEM((3, boxes, 128), F32), pltpu.VMEM((boxes, 8, 128), F32)]
+        + ids_scratch
+        + [pltpu.SemaphoreType.DMA((4,))],
         compiler_params=params(8),
-        name="upper_halves",
-    )(pos, charges, counts, box_centers)
+        name="first",
+    )(member, counts, *lists, stay(pos), stay(charges))
     msg, want = pl.pallas_call(
-        start_kernel,
-        out_shape=(struct((devices * 2, 128), F32), struct((devices, 128), jnp.int32)),
-        in_specs=[vmem()] * 4,
-        out_specs=(vmem(), vmem()),
+        second_kernel,
+        out_shape=ids_shape,
+        in_specs=[SMEM] + [vmem()] * 4 + [anywhere] * 2,
+        out_specs=(anywhere, anywhere),
+        scratch_shapes=ids_scratch + [pltpu.SemaphoreType.DMA((2,))],
+        input_output_aliases={5: 0, 6: 1},
         compiler_params=params(8),
-        name="start",
-    )(far_list.T, near_list.T, counts.reshape(1, boxes), box_centers)
+        name="second",
+    )(member, *lists, stay(msg), stay(want))
     moved = [lax.ppermute(ex_own, "gy", [(4 * z, 4 * z + k) for z in range(4)]) for k in range(1, 4)]
     served = flat(exchange(msg.reshape(devices, 2, 128)))
 
@@ -934,9 +980,9 @@
     big = lambda dtype, rows: pltpu.VMEM((rows, 128), dtype)
     *sums, term = pl.pallas_call(
         functools.partial(duo_kernel, 1.0 / (devices * boxes * slots)),
-        out_shape=(hbm((boxes, 8, 128), F32),) * 4 + (struct((devices, 128), F32),),
+        out_shape=(hbm((boxes, 8, 128), F32),) * 4 + (hbm((devices, 128), F32),),
         in_specs=[vmem()] + [anywhere] * 8,
-        out_specs=(anywhere,) * 4 + (vmem(),),
+        out_specs=(anywhere,) * 5,
         scratch_shapes=[
             pltpu.SMEM((16, devices), jnp.int32),
             pltpu.VMEM((devices, 8, 128), F32),
@@ -946,6 +992,7 @@
             pltpu.VMEM((boxes, 8, 128), F32),
             pltpu.VMEM((boxes, 8, 128), F32),
             pltpu.VMEM((devices, 256, 128), BF),
+            pltpu.VMEM((devices, 128), F32),
             pltpu.SemaphoreType.DMA((20,)),
         ]
         + [big(BF, 128)] * 2

time: 108 us -> 105 us (0.972)
  starting transfers between devices: 25.3 us -> 23.6 us
    ppermute x3, starting transfers between devices: 7.63 us -> 5.88 us  [on_device(): lax.ppermute(ex_own, 'gy', [(4 * z, 4 * z + k) for z in range(4)])]
  transfers between devices with their start and end apart: 6 -> 6, of which waited for: 3 -> 3; matrix products, arithmetic and copies ran while one was open for 3% -> 3% of each run, Pallas kernels for 28% -> 27%
where the time goes in v8:
time: 105 us
  Pallas kernels  49.3 us (47%)
  waiting for transfers between devices  25.4 us (24%)
  starting transfers between devices  23.6 us (22%)
  other arithmetic  3.82 us (4%)
  between operations  1.47 us (1%)
  local copies, waits for them, and re-layouts  1.09 us (1%)
    all_to_all x3, waiting for transfers between devices, exchange(): return lax.all_to_all(x, AXES, split_axis=0, concat_axis=0, tiled=True)  25.4 us
    all_to_all x3, starting transfers between devices, exchange(): return lax.all_to_all(x, AXES, split_axis=0, concat_axis=0, tiled=True)  17.7 us
    pallas_call x1, Pallas kernels, on_device(): pl.pallas_call(functools.partial(duo_kernel, 1.0 / (devices * boxes * slo...  16.3 us
    pallas_call x1, Pallas kernels, on_device(): pl.pallas_call(far_kernel, grid=(devices // group,), out_shape=hbm((devic...  9.82 us
    pallas_call x1, Pallas kernels, on_device(): pl.pallas_call(own_table_kernel, out_shape=(hbm((boxes, 8, 128), F32), hb...  8.9 us
    ppermute x3, starting transfers between devices, on_device(): lax.ppermute(ex_own, 'gy', [(4 * z, 4 * z + k) for z in range(4)])  5.88 us
    pallas_call x1, Pallas kernels, on_device(): pl.pallas_call(finish_kernel, out_shape=table, in_specs=[SMEM] + [vmem()]...  3.17 us
    pallas_call x1, Pallas kernels, on_device(): pl.pallas_call(goal_kernel, out_shape=(hbm((devices * 8, 128), F32), hbm(...  2.68 us
  transfers between devices with their start and end apart: 6, of which 3 were waited for; matrix products, arithmetic and copies ran while one was open for 3% of the time, Pallas kernels for 27%

profile of v8, /device:TPU:1, one launch (start us, length us, event | category | flops | bytes accessed | tf_op | source)
XLA Modules:
  0.0 104.8 jit_solution(13966158775307277752)
XLA Ops:
  0.6 2.6 %first.1 = (f32[256,128]{1,0:T(8,128)}, s32[128,128]{1,0:T(8,128)}, f32[352,128]{1,0:T(8,128)S(1)}) custom-call(s32[1]{0:T(128)} %bitcast.16.member_ref, s32[64]{0:T(128)} %count_ref.7, s32[8,64]{1,0:T(8,128)} %bitcast.57, s32[9,64]{1,0:T(8,128)} %bitcast.53, s32[1,64]{1,0:T(1,128)} %bitcast.61, f32[3,64]{1,0:T(4,128)} %cen_ref.3, f32[3,64,128]{2,1,0:T(8,128)} %bitcast.44, ...), custom_call_target="tpu_custom_call" | custom-call | tf_op jit(solution)/shard_map/first/pallas_call | solution.py:890
  3.2 2.3 %collective-permute-start = (f32[352,128]{1,0:T(8,128)S(1)}, f32[352,128]{1,0:T(8,128)S(1)}, u32[]{:S(2)}, u32[]{:S(2)}) collective-permute-start(f32[352,128]{1,0:T(8,128)S(1)} %get-tuple-element.69.own_ref), channel_id=1, source_target_pairs={{0,1},{4,5},{8,9},{12,13},{16,17},{20,21},{24,25},{28,29},{32,33},... | collective-permute-start | bytes 540680 | tf_op jit(solution)/shard_map/ppermute | solution.py:911
  5.5 2.3 %collective-permute-start.1 = (f32[352,128]{1,0:T(8,128)S(1)}, f32[352,128]{1,0:T(8,128)S(1)}, u32[]{:S(2)}, u32[]{:S(2)}) collective-permute-start(f32[352,128]{1,0:T(8,128)S(1)} %get-tuple-element.69.own_ref), channel_id=1, source_target_pairs={{0,2},{4,6},{8,10},{12,14},{16,18},{20,22},{24,26},{28,30},{32,34}... | collective-permute-start | bytes 540680 | tf_op jit(solution)/shard_map/ppermute | solution.py:911
  7.8 1.3 %collective-permute-start.2 = (f32[352,128]{1,0:T(8,128)S(1)}, f32[352,128]{1,0:T(8,128)S(1)}, u32[]{:S(2)}, u32[]{:S(2)}) collective-permute-start(f32[352,128]{1,0:T(8,128)S(1)} %get-tuple-element.69.own_ref), channel_id=1, source_target_pairs={{0,3},{4,7},{8,11},{12,15},{16,19},{20,23},{24,27},{28,31},{32,35}... | collective-permute-start | bytes 540680 | tf_op jit(solution)/shard_map/ppermute | solution.py:911
  9.2 0.8 second.1
  9.9 8.3 %all-to-all-start.3 = ((f32[128,2,128]{2,1,0:T(2,128)}), f32[128,2,128]{2,1,0:T(2,128)S(1)}, u32[]{:S(2)}, u32[]{:S(2)}) async-start(f32[128,2,128]{2,1,0:T(2,128)} %bitcast.51), calls=%async_computation.3 | async-start | bytes 262144 | tf_op jit(solution)/shard_map/all_to_all | solution.py:318
  18.2 2.6 %send_tables.1 = (f32[64,24,128]{2,1,0:T(8,128)S(1)}, f32[64,8,128]{2,1,0:T(8,128)S(1)}) custom-call(f32[3,64,128]{2,1,0:T(8,128)} %bitcast.45, f32[64,8,128]{2,1,0:T(8,128)} %charge_ref.3, s32[64]{0:T(128)} %count_ref.7, f32[3,64]{1,0:T(4,128)} %cen_ref.3), custom_call_target="tpu_custom_call" | custom-call | flops 50000000 | bytes 1200000 | tf_op jit(solution)/shard_map/send_tables/pallas_call | solution.py:914
  20.8 0.0 copy-start.1
  20.8 7.6 %all-to-all-done.3 = f32[128,2,128]{2,1,0:T(2,128)S(1)} async-done(((f32[128,2,128]{2,1,0:T(2,128)}), f32[128,2,128]{2,1,0:T(2,128)S(1)}, u32[]{:S(2)}, u32[]{:S(2)}) %all-to-all-start.3) | async-done | bytes 131104 | tf_op jit(solution)/shard_map/all_to_all | solution.py:318
  28.4 0.0 collective-permute-done.refs_0_
  28.5 0.0 collective-permute-done.1.refs_1_
  28.5 0.0 collective-permute-done.2.refs_2_
  28.5 0.0 copy-start.5
  28.5 0.0 copy-start.12
  28.5 2.6 %send.1 = f32[5632,128]{1,0:T(8,128)} custom-call(s32[1]{0:T(128)} %bitcast.16.member_ref, f32[256,128]{1,0:T(8,128)S(1)} %bitcast.34, f32[1536,128]{1,0:T(8,128)S(1)} %bitcast.36, f32[512,128]{1,0:T(8,128)S(1)} %bitcast.38, f32[352,128]{1,0:T(8,128)S(1)} %get-tuple-element.69.own_ref, f32[352,128]{1,0:T(8,128)S(1)} %collective-permute-done.refs_0_, ...), custom_call_target="tpu_custom_call" | custom-call | tf_op jit(solution)/shard_map/send/pallas_call | solution.py:925
  31.1 0.0 copy-start.2
  31.1 0.0 copy-start.3
  31.1 0.0 copy-start.9
  31.1 0.0 copy-start.11
  31.1 0.0 copy-done.1
  31.1 4.1 %all-to-all-start.4 = ((f32[128,11,4,128]{3,2,1,0:T(4,128)}), f32[128,11,4,128]{3,2,1,0:T(4,128)S(1)}, u32[]{:S(2)}, u32[]{:S(2)}) async-start(f32[128,11,4,128]{3,2,1,0:T(4,128)} %bitcast.41), calls=%async_computation.4 | async-start | bytes 5767168 | tf_op jit(solution)/shard_map/all_to_all | solution.py:318
  35.2 0.0 copy-done.5
  35.2 0.0 copy-done.12
  35.2 8.9 %own_tables.1 = (f32[64,8,128]{2,1,0:T(8,128)}, bf16[64,2,32,128]{3,2,1,0:T(8,128)(2,1)}, f32[64,8,128]{2,1,0:T(8,128)}) custom-call(f32[3,64,128]{2,1,0:T(8,128)S(1)} %bitcast.46, f32[64,8,128]{2,1,0:T(8,128)} %charge_ref.3, s32[64]{0:T(128)S(1)} %copy-done.12), custom_call_target="tpu_custom_call" | custom-call | flops 200000000 | bytes 4000000 | tf_op jit(solution)/shard_map/own_tables/pallas_call | solution.py:942
  44.1 0.0 copy-done.2
  44.1 0.0 copy-done.3
  44.1 0.0 copy-done.9
  44.1 2.7 %goals.1 = (f32[1024,128]{1,0:T(8,128)}, f32[1024,128]{1,0:T(8,128)}, f32[512,128]{1,0:T(8,128)}, s32[16,128]{1,0:T(8,128)}) custom-call(s32[128,128]{1,0:T(8,128)S(1)} %copy-done.2, f32[256,128]{1,0:T(8,128)S(1)} %bitcast.35, f32[3,64]{1,0:T(4,128)S(1)} %copy-done.9, f32[8,128]{1,0:T(8,128)S(1)} %copy-done.3), custom_call_target="tpu_custom_call" | custom-call | flops 50000000 | bytes 2000000 | tf_op jit(solution)/shard_map/goals/pallas_call | solution.py:952
  46.8 0.0 copy-done.11
  46.8 0.0 copy-start
  46.8 1.0 copy-done
  47.8 9.8 %far_values.1.v_hbm = bf16[128,256,128]{2,1,0:T(8,128)(2,1)} custom-call(f32[128,8,128]{2,1,0:T(8,128)S(1)} %bitcast.37, bf16[128,32]{1,0:T(8,128)(2,1)S(1)} %copy-done.11), custom_call_target="tpu_custom_call" | custom-call | flops 200000000 | bytes 9000000 | tf_op jit(solution)/shard_map/far_values/pallas_call | solution.py:969
  57.7 2.5 %compare_reduce_fusion = pred[128]{0:T(512)(128)(4,1)S(1)} fusion(f32[128,2,128]{2,1,0:T(2,128)S(1)} %all-to-all-done.3), kind=kLoop, calls=%fused_computation.10 | loop fusion | flops 128 | bytes 640 | tf_op jit(solution)/shard_map/gt | solution.py:1019
  60.2 12.5 %all-to-all-done.4 = f32[128,11,4,128]{3,2,1,0:T(4,128)S(1)} async-done(((f32[128,11,4,128]{3,2,1,0:T(4,128)}), f32[128,11,4,128]{3,2,1,0:T(4,128)S(1)}, u32[]{:S(2)}, u32[]{:S(2)}) %all-to-all-start.4) | async-done | bytes 2883616 | tf_op jit(solution)/shard_map/all_to_all | solution.py:318
  72.7 0.0 copy-start.6
  72.7 0.0 copy-start.8
  72.7 0.0 copy-start.10
  72.7 16.3 %pairs.3 = (f32[64,8,128]{2,1,0:T(8,128)}, f32[64,8,128]{2,1,0:T(8,128)}, f32[64,8,128]{2,1,0:T(8,128)}, f32[64,8,128]{2,1,0:T(8,128)}, f32[128,128]{1,0:T(8,128)}) custom-call(f32[5632,128]{1,0:T(8,128)S(1)} %bitcast.33, s32[16,128]{1,0:T(8,128)} %get-tuple-element.71.want_hbm, f32[128,8,128]{2,1,0:T(8,128)} %bitcast.63, f32[64,8,128]{2,1,0:T(8,128)} %bitcast.64, ...), custom_call_target="tpu_custom_call" | custom-call | flops 1000000000 | bytes 12000000 | tf_op jit(solution)/shard_map/pairs/pallas_call | solution.py:981
  89.0 5.4 %all-to-all-start.5 = ((f32[128,1,128]{2,1,0:T(1,128)}), f32[128,1,128]{2,1,0:T(1,128)S(1)}, u32[]{:S(2)}, u32[]{:S(2)}) async-start(f32[128,1,128]{2,1,0:T(1,128)} %bitcast.55), calls=%async_computation.5 | async-start | bytes 131072 | tf_op jit(solution)/shard_map/all_to_all | solution.py:318
  94.3 0.6 and_reduce_fusion
  95.6 3.2 %finish.1 = f32[64,8,128]{2,1,0:T(8,128)} custom-call(s32[64]{0:T(128)S(1)} %copy-done.12, f32[3,64,128]{2,1,0:T(8,128)S(1)} %bitcast.47, f32[64,8,128]{2,1,0:T(8,128)} %get-tuple-element.79.near0_ref, f32[64,8,128]{2,1,0:T(8,128)} %get-tuple-element.80.near1_ref, f32[64,8,128]{2,1,0:T(8,128)} %get-tuple-element.81.far0_ref, ...), custom_call_target="tpu_custom_call" | custom-call | flops 50000000 | bytes 3000000 | tf_op jit(solution)/shard_map/finish/pallas_call | solution.py:1009
  98.8 5.3 %all-to-all-done.5 = f32[128,1,128]{2,1,0:T(1,128)S(1)} async-done(((f32[128,1,128]{2,1,0:T(1,128)}), f32[128,1,128]{2,1,0:T(1,128)S(1)}, u32[]{:S(2)}, u32[]{:S(2)}) %all-to-all-start.5) | async-done | bytes 65568 | tf_op jit(solution)/shard_map/all_to_all | solution.py:318
  104.1 0.0 copy-done.6
  104.1 0.0 copy-done.8
  104.1 0.0 copy-done.10
  104.1 0.7 conditional.1
  104.1 0.7 slice_reduce_fusion
Async XLA Ops:
  3.2 25.2 %collective-permute-start = (f32[352,128]{1,0:T(8,128)S(1)}, f32[352,128]{1,0:T(8,128)S(1)}, u32[]{:S(2)}, u32[]{:S(2)}) collective-permute-start(f32[352,128]{1,0:T(8,128)S(1)} %get-tuple-element.69.own_ref), channel_id=1, source_target_pairs={{0,1},{4,5},{8,9},{12,13},{16,17},{20,21},{24,25},{28,29},{32,33},... | collective-permute-start | bytes 540680 | tf_op jit(solution)/shard_map/ppermute | solution.py:911
  5.5 22.9 %collective-permute-start.1 = (f32[352,128]{1,0:T(8,128)S(1)}, f32[352,128]{1,0:T(8,128)S(1)}, u32[]{:S(2)}, u32[]{:S(2)}) collective-permute-start(f32[352,128]{1,0:T(8,128)S(1)} %get-tuple-element.69.own_ref), channel_id=1, source_target_pairs={{0,2},{4,6},{8,10},{12,14},{16,18},{20,22},{24,26},{28,30},{32,34}... | collective-permute-start | bytes 540680 | tf_op jit(solution)/shard_map/ppermute | solution.py:911
  7.8 20.6 %collective-permute-start.2 = (f32[352,128]{1,0:T(8,128)S(1)}, f32[352,128]{1,0:T(8,128)S(1)}, u32[]{:S(2)}, u32[]{:S(2)}) collective-permute-start(f32[352,128]{1,0:T(8,128)S(1)} %get-tuple-element.69.own_ref), channel_id=1, source_target_pairs={{0,3},{4,7},{8,11},{12,15},{16,19},{20,23},{24,27},{28,31},{32,35}... | collective-permute-start | bytes 540680 | tf_op jit(solution)/shard_map/ppermute | solution.py:911
  9.9 18.5 %all-to-all-start.3 = ((f32[128,2,128]{2,1,0:T(2,128)}), f32[128,2,128]{2,1,0:T(2,128)S(1)}, u32[]{:S(2)}, u32[]{:S(2)}) async-start(f32[128,2,128]{2,1,0:T(2,128)} %bitcast.51), calls=%async_computation.3 | async-start | bytes 262144 | tf_op jit(solution)/shard_map/all_to_all | solution.py:318
  20.8 10.3 %copy-start.1 = (f32[64,8,128]{2,1,0:T(8,128)}, f32[64,8,128]{2,1,0:T(8,128)S(1)}, u32[]{:S(2)}) copy-start(f32[64,8,128]{2,1,0:T(8,128)S(1)} %get-tuple-element.68.w_hbm) | copy-start | bytes 786436
  28.5 6.7 %copy-start.5 = (f32[64,3,128]{2,0,1:T(8,128)S(1)}, f32[64,3,128]{2,0,1:T(8,128)}, u32[]{:S(2)}) copy-start(f32[64,3,128]{2,0,1:T(8,128)} %param.12) | copy-start | bytes 294916
  28.5 6.7 %copy-start.12 = (s32[64]{0:T(128)S(1)}, s32[64]{0:T(128)}, u32[]{:S(2)}) copy-start(s32[64]{0:T(128)} %count_ref.7) | copy-start | bytes 772
  31.1 13.1 %copy-start.2 = (s32[128,128]{1,0:T(8,128)S(1)}, s32[128,128]{1,0:T(8,128)}, u32[]{:S(2)}) copy-start(s32[128,128]{1,0:T(8,128)} %get-tuple-element.70.want_ref) | copy-start | bytes 196612
  31.1 13.0 %copy-start.3 = (f32[8,128]{1,0:T(8,128)S(1)}, f32[8,128]{1,0:T(8,128)}, u32[]{:S(2)}) copy-start(f32[8,128]{1,0:T(8,128)} %constant.51.clone.node_ref) | copy-start | bytes 12292
  31.1 13.0 %copy-start.9 = (f32[3,64]{1,0:T(4,128)S(1)}, f32[3,64]{1,0:T(4,128)}, u32[]{:S(2)}) copy-start(f32[3,64]{1,0:T(4,128)} %cen_ref.3) | copy-start | bytes 2308
  31.1 15.7 %copy-start.11 = (bf16[128,32]{1,0:T(8,128)(2,1)S(1)}, bf16[128,32]{1,0:T(8,128)(2,1)}, u32[]{:S(2)}) copy-start(bf16[128,32]{1,0:T(8,128)(2,1)} %constant.52.clone.fn_ref) | copy-start | bytes 24580
  31.1 41.6 %all-to-all-start.4 = ((f32[128,11,4,128]{3,2,1,0:T(4,128)}), f32[128,11,4,128]{3,2,1,0:T(4,128)S(1)}, u32[]{:S(2)}, u32[]{:S(2)}) async-start(f32[128,11,4,128]{3,2,1,0:T(4,128)} %bitcast.41), calls=%async_computation.4 | async-start | bytes 5767168 | tf_op jit(solution)/shard_map/all_to_all | solution.py:318
  46.8 1.0 copy-start
  72.7 31.4 %copy-start.6 = (f32[64,8,128]{2,1,0:T(8,128)S(1)}, f32[64,8,128]{2,1,0:T(8,128)}, u32[]{:S(2)}) copy-start(f32[64,8,128]{2,1,0:T(8,128)} %charge_ref.3) | copy-start | bytes 786436
  72.7 31.4 %copy-start.8 = (s32[64,9]{0,1:T(8,128)S(1)}, s32[64,9]{0,1:T(8,128)}, u32[]{:S(2)}) copy-start(s32[64,9]{0,1:T(8,128)} %param.17) | copy-start | bytes 6916
  72.7 31.4 %copy-start.10 = (s32[64,8]{0,1:T(8,128)S(1)}, s32[64,8]{0,1:T(8,128)}, u32[]{:S(2)}) copy-start(s32[64,8]{0,1:T(8,128)} %param.16) | copy-start | bytes 6148
  89.0 15.1 %all-to-all-start.5 = ((f32[128,1,128]{2,1,0:T(1,128)}), f32[128,1,128]{2,1,0:T(1,128)S(1)}, u32[]{:S(2)}, u32[]{:S(2)}) async-start(f32[128,1,128]{2,1,0:T(1,128)} %bitcast.55), calls=%async_computation.5 | async-start | bytes 131072 | tf_op jit(solution)/shard_map/all_to_all | solution.py:318

commit v9 on v8

--- a/solution.py
+++ b/solution.py
@@ -402,9 +402,9 @@
 HALF = 64
 ROWS = 44
 NEAR_ROWS = 24
-UNROLL = 4
-CHUNKS = 16
-AHEAD = 4
+UNROLL = 16
+CHUNKS = 4
+AHEAD = 1
 
 
 def upper_kernel(pos_ref, charge_ref, count_ref, row_ref, ex_ref):

time: 105 us -> 105 us (level)
  no operation moved by 1% of the time
where the time goes in v9:
time: 105 us; the launch traced here: 104 us
  Pallas kernels  48.7 us (46%)
  waiting for transfers between devices  25.4 us (24%)
  starting transfers between devices  23.6 us (22%)
  other arithmetic  3.82 us (4%)
  between operations  1.47 us (1%)
  local copies, waits for them, and re-layouts  1.09 us (1%)
    all_to_all x3, waiting for transfers between devices, exchange(): return lax.all_to_all(x, AXES, split_axis=0, concat_axis=0, tiled=True)  25.4 us
    all_to_all x3, starting transfers between devices, exchange(): return lax.all_to_all(x, AXES, split_axis=0, concat_axis=0, tiled=True)  17.7 us
    pallas_call x1, Pallas kernels, on_device(): pl.pallas_call(functools.partial(duo_kernel, 1.0 / (devices * boxes * slo...  15.6 us
    pallas_call x1, Pallas kernels, on_device(): pl.pallas_call(far_kernel, grid=(devices // group,), out_shape=hbm((devic...  9.82 us
    pallas_call x1, Pallas kernels, on_device(): pl.pallas_call(own_table_kernel, out_shape=(hbm((boxes, 8, 128), F32), hb...  8.9 us
    ppermute x3, starting transfers between devices, on_device(): lax.ppermute(ex_own, 'gy', [(4 * z, 4 * z + k) for z in range(4)])  5.88 us
    pallas_call x1, Pallas kernels, on_device(): pl.pallas_call(finish_kernel, out_shape=table, in_specs=[SMEM] + [vmem()]...  3.17 us
    pallas_call x1, Pallas kernels, on_device(): pl.pallas_call(goal_kernel, out_shape=(hbm((devices * 8, 128), F32), hbm(...  2.68 us
  transfers between devices with their start and end apart: 6, of which 3 were waited for; matrix products, arithmetic and copies ran while one was open for 3% of the time, Pallas kernels for 27%

profile of v9, /device:TPU:1, one launch (start us, length us, event | category | flops | bytes accessed | tf_op | source)
XLA Modules:
  0.0 104.2 jit_solution(10940235373477805083)
XLA Ops:
  0.6 2.6 %first.1 = (f32[256,128]{1,0:T(8,128)}, s32[128,128]{1,0:T(8,128)}, f32[352,128]{1,0:T(8,128)S(1)}) custom-call(s32[1]{0:T(128)} %bitcast.16.member_ref, s32[64]{0:T(128)} %count_ref.7, s32[8,64]{1,0:T(8,128)} %bitcast.57, s32[9,64]{1,0:T(8,128)} %bitcast.53, s32[1,64]{1,0:T(1,128)} %bitcast.61, f32[3,64]{1,0:T(4,128)} %cen_ref.3, f32[3,64,128]{2,1,0:T(8,128)} %bitcast.44, ...), custom_call_target="tpu_custom_call" | custom-call | tf_op jit(solution)/shard_map/first/pallas_call | solution.py:890
  3.2 2.3 %collective-permute-start = (f32[352,128]{1,0:T(8,128)S(1)}, f32[352,128]{1,0:T(8,128)S(1)}, u32[]{:S(2)}, u32[]{:S(2)}) collective-permute-start(f32[352,128]{1,0:T(8,128)S(1)} %get-tuple-element.69.own_ref), channel_id=1, source_target_pairs={{0,1},{4,5},{8,9},{12,13},{16,17},{20,21},{24,25},{28,29},{32,33},... | collective-permute-start | bytes 540680 | tf_op jit(solution)/shard_map/ppermute | solution.py:911
  5.5 2.3 %collective-permute-start.1 = (f32[352,128]{1,0:T(8,128)S(1)}, f32[352,128]{1,0:T(8,128)S(1)}, u32[]{:S(2)}, u32[]{:S(2)}) collective-permute-start(f32[352,128]{1,0:T(8,128)S(1)} %get-tuple-element.69.own_ref), channel_id=1, source_target_pairs={{0,2},{4,6},{8,10},{12,14},{16,18},{20,22},{24,26},{28,30},{32,34}... | collective-permute-start | bytes 540680 | tf_op jit(solution)/shard_map/ppermute | solution.py:911
  7.8 1.3 %collective-permute-start.2 = (f32[352,128]{1,0:T(8,128)S(1)}, f32[352,128]{1,0:T(8,128)S(1)}, u32[]{:S(2)}, u32[]{:S(2)}) collective-permute-start(f32[352,128]{1,0:T(8,128)S(1)} %get-tuple-element.69.own_ref), channel_id=1, source_target_pairs={{0,3},{4,7},{8,11},{12,15},{16,19},{20,23},{24,27},{28,31},{32,35}... | collective-permute-start | bytes 540680 | tf_op jit(solution)/shard_map/ppermute | solution.py:911
  9.2 0.8 second.1
  9.9 8.3 %all-to-all-start.3 = ((f32[128,2,128]{2,1,0:T(2,128)}), f32[128,2,128]{2,1,0:T(2,128)S(1)}, u32[]{:S(2)}, u32[]{:S(2)}) async-start(f32[128,2,128]{2,1,0:T(2,128)} %bitcast.51), calls=%async_computation.3 | async-start | bytes 262144 | tf_op jit(solution)/shard_map/all_to_all | solution.py:318
  18.2 2.6 %send_tables.1 = (f32[64,24,128]{2,1,0:T(8,128)S(1)}, f32[64,8,128]{2,1,0:T(8,128)S(1)}) custom-call(f32[3,64,128]{2,1,0:T(8,128)} %bitcast.45, f32[64,8,128]{2,1,0:T(8,128)} %charge_ref.3, s32[64]{0:T(128)} %count_ref.7, f32[3,64]{1,0:T(4,128)} %cen_ref.3), custom_call_target="tpu_custom_call" | custom-call | flops 50000000 | bytes 1200000 | tf_op jit(solution)/shard_map/send_tables/pallas_call | solution.py:914
  20.8 0.0 copy-start.1
  20.8 7.6 %all-to-all-done.3 = f32[128,2,128]{2,1,0:T(2,128)S(1)} async-done(((f32[128,2,128]{2,1,0:T(2,128)}), f32[128,2,128]{2,1,0:T(2,128)S(1)}, u32[]{:S(2)}, u32[]{:S(2)}) %all-to-all-start.3) | async-done | bytes 131104 | tf_op jit(solution)/shard_map/all_to_all | solution.py:318
  28.4 0.0 collective-permute-done.refs_0_
  28.5 0.0 collective-permute-done.1.refs_1_
  28.5 0.0 collective-permute-done.2.refs_2_
  28.5 0.0 copy-start.5
  28.5 0.0 copy-start.12
  28.5 2.6 %send.1 = f32[5632,128]{1,0:T(8,128)} custom-call(s32[1]{0:T(128)} %bitcast.16.member_ref, f32[256,128]{1,0:T(8,128)S(1)} %bitcast.34, f32[1536,128]{1,0:T(8,128)S(1)} %bitcast.36, f32[512,128]{1,0:T(8,128)S(1)} %bitcast.38, f32[352,128]{1,0:T(8,128)S(1)} %get-tuple-element.69.own_ref, f32[352,128]{1,0:T(8,128)S(1)} %collective-permute-done.refs_0_, ...), custom_call_target="tpu_custom_call" | custom-call | tf_op jit(solution)/shard_map/send/pallas_call | solution.py:925
  31.1 0.0 copy-start.2
  31.1 0.0 copy-start.3
  31.1 0.0 copy-start.9
  31.1 0.0 copy-start.11
  31.1 0.0 copy-done.1
  31.1 4.1 %all-to-all-start.4 = ((f32[128,11,4,128]{3,2,1,0:T(4,128)}), f32[128,11,4,128]{3,2,1,0:T(4,128)S(1)}, u32[]{:S(2)}, u32[]{:S(2)}) async-start(f32[128,11,4,128]{3,2,1,0:T(4,128)} %bitcast.41), calls=%async_computation.4 | async-start | bytes 5767168 | tf_op jit(solution)/shard_map/all_to_all | solution.py:318
  35.2 0.0 copy-done.5
  35.2 0.0 copy-done.12
  35.2 8.9 %own_tables.1 = (f32[64,8,128]{2,1,0:T(8,128)}, bf16[64,2,32,128]{3,2,1,0:T(8,128)(2,1)}, f32[64,8,128]{2,1,0:T(8,128)}) custom-call(f32[3,64,128]{2,1,0:T(8,128)S(1)} %bitcast.46, f32[64,8,128]{2,1,0:T(8,128)} %charge_ref.3, s32[64]{0:T(128)S(1)} %copy-done.12), custom_call_target="tpu_custom_call" | custom-call | flops 200000000 | bytes 4000000 | tf_op jit(solution)/shard_map/own_tables/pallas_call | solution.py:942
  44.1 0.0 copy-done.2
  44.1 0.0 copy-done.3
  44.1 0.0 copy-done.9
  44.1 2.7 %goals.1 = (f32[1024,128]{1,0:T(8,128)}, f32[1024,128]{1,0:T(8,128)}, f32[512,128]{1,0:T(8,128)}, s32[16,128]{1,0:T(8,128)}) custom-call(s32[128,128]{1,0:T(8,128)S(1)} %copy-done.2, f32[256,128]{1,0:T(8,128)S(1)} %bitcast.35, f32[3,64]{1,0:T(4,128)S(1)} %copy-done.9, f32[8,128]{1,0:T(8,128)S(1)} %copy-done.3), custom_call_target="tpu_custom_call" | custom-call | flops 50000000 | bytes 2000000 | tf_op jit(solution)/shard_map/goals/pallas_call | solution.py:952
  46.8 0.0 copy-done.11
  46.8 0.0 copy-start
  46.8 1.0 copy-done
  47.8 9.8 %far_values.1.v_hbm = bf16[128,256,128]{2,1,0:T(8,128)(2,1)} custom-call(f32[128,8,128]{2,1,0:T(8,128)S(1)} %bitcast.37, bf16[128,32]{1,0:T(8,128)(2,1)S(1)} %copy-done.11), custom_call_target="tpu_custom_call" | custom-call | flops 200000000 | bytes 9000000 | tf_op jit(solution)/shard_map/far_values/pallas_call | solution.py:969
  57.7 2.5 %compare_reduce_fusion = pred[128]{0:T(512)(128)(4,1)S(1)} fusion(f32[128,2,128]{2,1,0:T(2,128)S(1)} %all-to-all-done.3), kind=kLoop, calls=%fused_computation.10 | loop fusion | flops 128 | bytes 640 | tf_op jit(solution)/shard_map/gt | solution.py:1019
  60.2 12.5 %all-to-all-done.4 = f32[128,11,4,128]{3,2,1,0:T(4,128)S(1)} async-done(((f32[128,11,4,128]{3,2,1,0:T(4,128)}), f32[128,11,4,128]{3,2,1,0:T(4,128)S(1)}, u32[]{:S(2)}, u32[]{:S(2)}) %all-to-all-start.4) | async-done | bytes 2883616 | tf_op jit(solution)/shard_map/all_to_all | solution.py:318
  72.7 0.0 copy-start.6
  72.7 0.0 copy-start.8
  72.7 0.0 copy-start.10
  72.7 15.6 %pairs.3 = (f32[64,8,128]{2,1,0:T(8,128)}, f32[64,8,128]{2,1,0:T(8,128)}, f32[64,8,128]{2,1,0:T(8,128)}, f32[64,8,128]{2,1,0:T(8,128)}, f32[128,128]{1,0:T(8,128)}) custom-call(f32[5632,128]{1,0:T(8,128)S(1)} %bitcast.33, s32[16,128]{1,0:T(8,128)} %get-tuple-element.71.want_hbm, f32[128,8,128]{2,1,0:T(8,128)} %bitcast.63, f32[64,8,128]{2,1,0:T(8,128)} %bitcast.64, ...), custom_call_target="tpu_custom_call" | custom-call | flops 1000000000 | bytes 12000000 | tf_op jit(solution)/shard_map/pairs/pallas_call | solution.py:981
  88.4 5.4 %all-to-all-start.5 = ((f32[128,1,128]{2,1,0:T(1,128)}), f32[128,1,128]{2,1,0:T(1,128)S(1)}, u32[]{:S(2)}, u32[]{:S(2)}) async-start(f32[128,1,128]{2,1,0:T(1,128)} %bitcast.55), calls=%async_computation.5 | async-start | bytes 131072 | tf_op jit(solution)/shard_map/all_to_all | solution.py:318
  93.7 0.6 and_reduce_fusion
  95.0 3.2 %finish.1 = f32[64,8,128]{2,1,0:T(8,128)} custom-call(s32[64]{0:T(128)S(1)} %copy-done.12, f32[3,64,128]{2,1,0:T(8,128)S(1)} %bitcast.47, f32[64,8,128]{2,1,0:T(8,128)} %get-tuple-element.79.near0_ref, f32[64,8,128]{2,1,0:T(8,128)} %get-tuple-element.80.near1_ref, f32[64,8,128]{2,1,0:T(8,128)} %get-tuple-element.81.far0_ref, ...), custom_call_target="tpu_custom_call" | custom-call | flops 50000000 | bytes 3000000 | tf_op jit(solution)/shard_map/finish/pallas_call | solution.py:1009
  98.2 5.3 %all-to-all-done.5 = f32[128,1,128]{2,1,0:T(1,128)S(1)} async-done(((f32[128,1,128]{2,1,0:T(1,128)}), f32[128,1,128]{2,1,0:T(1,128)S(1)}, u32[]{:S(2)}, u32[]{:S(2)}) %all-to-all-start.5) | async-done | bytes 65568 | tf_op jit(solution)/shard_map/all_to_all | solution.py:318
  103.5 0.0 copy-done.6
  103.5 0.0 copy-done.8
  103.5 0.0 copy-done.10
  103.5 0.7 conditional.1
  103.5 0.7 slice_reduce_fusion
Async XLA Ops:
  3.2 25.2 %collective-permute-start = (f32[352,128]{1,0:T(8,128)S(1)}, f32[352,128]{1,0:T(8,128)S(1)}, u32[]{:S(2)}, u32[]{:S(2)}) collective-permute-start(f32[352,128]{1,0:T(8,128)S(1)} %get-tuple-element.69.own_ref), channel_id=1, source_target_pairs={{0,1},{4,5},{8,9},{12,13},{16,17},{20,21},{24,25},{28,29},{32,33},... | collective-permute-start | bytes 540680 | tf_op jit(solution)/shard_map/ppermute | solution.py:911
  5.5 22.9 %collective-permute-start.1 = (f32[352,128]{1,0:T(8,128)S(1)}, f32[352,128]{1,0:T(8,128)S(1)}, u32[]{:S(2)}, u32[]{:S(2)}) collective-permute-start(f32[352,128]{1,0:T(8,128)S(1)} %get-tuple-element.69.own_ref), channel_id=1, source_target_pairs={{0,2},{4,6},{8,10},{12,14},{16,18},{20,22},{24,26},{28,30},{32,34}... | collective-permute-start | bytes 540680 | tf_op jit(solution)/shard_map/ppermute | solution.py:911
  7.8 20.6 %collective-permute-start.2 = (f32[352,128]{1,0:T(8,128)S(1)}, f32[352,128]{1,0:T(8,128)S(1)}, u32[]{:S(2)}, u32[]{:S(2)}) collective-permute-start(f32[352,128]{1,0:T(8,128)S(1)} %get-tuple-element.69.own_ref), channel_id=1, source_target_pairs={{0,3},{4,7},{8,11},{12,15},{16,19},{20,23},{24,27},{28,31},{32,35}... | collective-permute-start | bytes 540680 | tf_op jit(solution)/shard_map/ppermute | solution.py:911
  9.9 18.5 %all-to-all-start.3 = ((f32[128,2,128]{2,1,0:T(2,128)}), f32[128,2,128]{2,1,0:T(2,128)S(1)}, u32[]{:S(2)}, u32[]{:S(2)}) async-start(f32[128,2,128]{2,1,0:T(2,128)} %bitcast.51), calls=%async_computation.3 | async-start | bytes 262144 | tf_op jit(solution)/shard_map/all_to_all | solution.py:318
  20.8 10.3 %copy-start.1 = (f32[64,8,128]{2,1,0:T(8,128)}, f32[64,8,128]{2,1,0:T(8,128)S(1)}, u32[]{:S(2)}) copy-start(f32[64,8,128]{2,1,0:T(8,128)S(1)} %get-tuple-element.68.w_hbm) | copy-start | bytes 786436
  28.5 6.7 %copy-start.5 = (f32[64,3,128]{2,0,1:T(8,128)S(1)}, f32[64,3,128]{2,0,1:T(8,128)}, u32[]{:S(2)}) copy-start(f32[64,3,128]{2,0,1:T(8,128)} %param.12) | copy-start | bytes 294916
  28.5 6.7 %copy-start.12 = (s32[64]{0:T(128)S(1)}, s32[64]{0:T(128)}, u32[]{:S(2)}) copy-start(s32[64]{0:T(128)} %count_ref.7) | copy-start | bytes 772
  31.1 13.0 %copy-start.2 = (s32[128,128]{1,0:T(8,128)S(1)}, s32[128,128]{1,0:T(8,128)}, u32[]{:S(2)}) copy-start(s32[128,128]{1,0:T(8,128)} %get-tuple-element.70.want_ref) | copy-start | bytes 196612
  31.1 13.0 %copy-start.3 = (f32[8,128]{1,0:T(8,128)S(1)}, f32[8,128]{1,0:T(8,128)}, u32[]{:S(2)}) copy-start(f32[8,128]{1,0:T(8,128)} %constant.51.clone.node_ref) | copy-start | bytes 12292
  31.1 13.0 %copy-start.9 = (f32[3,64]{1,0:T(4,128)S(1)}, f32[3,64]{1,0:T(4,128)}, u32[]{:S(2)}) copy-start(f32[3,64]{1,0:T(4,128)} %cen_ref.3) | copy-start | bytes 2308
  31.1 15.7 %copy-start.11 = (bf16[128,32]{1,0:T(8,128)(2,1)S(1)}, bf16[128,32]{1,0:T(8,128)(2,1)}, u32[]{:S(2)}) copy-start(bf16[128,32]{1,0:T(8,128)(2,1)} %constant.52.clone.fn_ref) | copy-start | bytes 24580
  31.1 41.6 %all-to-all-start.4 = ((f32[128,11,4,128]{3,2,1,0:T(4,128)}), f32[128,11,4,128]{3,2,1,0:T(4,128)S(1)}, u32[]{:S(2)}, u32[]{:S(2)}) async-start(f32[128,11,4,128]{3,2,1,0:T(4,128)} %bitcast.41), calls=%async_computation.4 | async-start | bytes 5767168 | tf_op jit(solution)/shard_map/all_to_all | solution.py:318
  46.8 1.0 %copy-start = (f32[1024,128]{1,0:T(8,128)S(1)}, f32[1024,128]{1,0:T(8,128)}, u32[]{:S(2)}) copy-start(f32[1024,128]{1,0:T(8,128)} %get-tuple-element.77) | copy-start | bytes 1572868
  72.7 30.8 %copy-start.6 = (f32[64,8,128]{2,1,0:T(8,128)S(1)}, f32[64,8,128]{2,1,0:T(8,128)}, u32[]{:S(2)}) copy-start(f32[64,8,128]{2,1,0:T(8,128)} %charge_ref.3) | copy-start | bytes 786436
  72.7 30.8 %copy-start.8 = (s32[64,9]{0,1:T(8,128)S(1)}, s32[64,9]{0,1:T(8,128)}, u32[]{:S(2)}) copy-start(s32[64,9]{0,1:T(8,128)} %param.17) | copy-start | bytes 6916
  72.7 30.8 %copy-start.10 = (s32[64,8]{0,1:T(8,128)S(1)}, s32[64,8]{0,1:T(8,128)}, u32[]{:S(2)}) copy-start(s32[64,8]{0,1:T(8,128)} %param.16) | copy-start | bytes 6148
  88.4 15.1 %all-to-all-start.5 = ((f32[128,1,128]{2,1,0:T(1,128)}), f32[128,1,128]{2,1,0:T(1,128)S(1)}, u32[]{:S(2)}, u32[]{:S(2)}) async-start(f32[128,1,128]{2,1,0:T(1,128)} %bitcast.55), calls=%async_computation.5 | async-start | bytes 131072 | tf_op jit(solution)/shard_map/all_to_all | solution.py:318

commit v10 on v9

--- a/solution.py
+++ b/solution.py
@@ -870,7 +870,7 @@
         out_ref[b] = jnp.where(lane < count_ref[b], near + far, 0.0)
         return carry
 
-    lax.fori_loop(0, boxes, body, 0, unroll=16)
+    lax.fori_loop(0, boxes, body, 0, unroll=32)
 
 
 def on_device(local_pos, charges, counts, box_centers, far_list, near_list):

time: 105 us -> 105 us (level)
  no operation moved by 1% of the time
where the time goes in v10:
time: 105 us; the launch traced here: 104 us
  Pallas kernels  48.4 us (46%)
  waiting for transfers between devices  25.7 us (24%)
  starting transfers between devices  23.6 us (22%)
  other arithmetic  3.82 us (4%)
  between operations  1.47 us (1%)
  local copies, waits for them, and re-layouts  1.09 us (1%)
    all_to_all x3, waiting for transfers between devices, exchange(): return lax.all_to_all(x, AXES, split_axis=0, concat_axis=0, tiled=True)  25.7 us
    all_to_all x3, starting transfers between devices, exchange(): return lax.all_to_all(x, AXES, split_axis=0, concat_axis=0, tiled=True)  17.7 us
    pallas_call x1, Pallas kernels, on_device(): pl.pallas_call(functools.partial(duo_kernel, 1.0 / (devices * boxes * slo...  15.6 us
    pallas_call x1, Pallas kernels, on_device(): pl.pallas_call(far_kernel, grid=(devices // group,), out_shape=hbm((devic...  9.82 us
    pallas_call x1, Pallas kernels, on_device(): pl.pallas_call(own_table_kernel, out_shape=(hbm((boxes, 8, 128), F32), hb...  8.9 us
    ppermute x3, starting transfers between devices, on_device(): lax.ppermute(ex_own, 'gy', [(4 * z, 4 * z + k) for z in range(4)])  5.88 us
    pallas_call x1, Pallas kernels, on_device(): pl.pallas_call(finish_kernel, out_shape=table, in_specs=[SMEM] + [vmem()]...  2.9 us
    pallas_call x1, Pallas kernels, on_device(): pl.pallas_call(goal_kernel, out_shape=(hbm((devices * 8, 128), F32), hbm(...  2.68 us
  transfers between devices with their start and end apart: 6, of which 3 were waited for; matrix products, arithmetic and copies ran while one was open for 3% of the time, Pallas kernels for 27%

profile of v10, /device:TPU:1, one launch (start us, length us, event | category | flops | bytes accessed | tf_op | source)
XLA Modules:
  0.0 104.2 jit_solution(1416459871099694470)
XLA Ops:
  0.6 2.6 %first.1 = (f32[256,128]{1,0:T(8,128)}, s32[128,128]{1,0:T(8,128)}, f32[352,128]{1,0:T(8,128)S(1)}) custom-call(s32[1]{0:T(128)} %bitcast.16.member_ref, s32[64]{0:T(128)} %count_ref.7, s32[8,64]{1,0:T(8,128)} %bitcast.57, s32[9,64]{1,0:T(8,128)} %bitcast.53, s32[1,64]{1,0:T(1,128)} %bitcast.61, f32[3,64]{1,0:T(4,128)} %cen_ref.3, f32[3,64,128]{2,1,0:T(8,128)} %bitcast.44, ...), custom_call_target="tpu_custom_call" | custom-call | tf_op jit(solution)/shard_map/first/pallas_call | solution.py:890
  3.2 2.3 %collective-permute-start = (f32[352,128]{1,0:T(8,128)S(1)}, f32[352,128]{1,0:T(8,128)S(1)}, u32[]{:S(2)}, u32[]{:S(2)}) collective-permute-start(f32[352,128]{1,0:T(8,128)S(1)} %get-tuple-element.69.own_ref), channel_id=1, source_target_pairs={{0,1},{4,5},{8,9},{12,13},{16,17},{20,21},{24,25},{28,29},{32,33},... | collective-permute-start | bytes 540680 | tf_op jit(solution)/shard_map/ppermute | solution.py:911
  5.5 2.3 %collective-permute-start.1 = (f32[352,128]{1,0:T(8,128)S(1)}, f32[352,128]{1,0:T(8,128)S(1)}, u32[]{:S(2)}, u32[]{:S(2)}) collective-permute-start(f32[352,128]{1,0:T(8,128)S(1)} %get-tuple-element.69.own_ref), channel_id=1, source_target_pairs={{0,2},{4,6},{8,10},{12,14},{16,18},{20,22},{24,26},{28,30},{32,34}... | collective-permute-start | bytes 540680 | tf_op jit(solution)/shard_map/ppermute | solution.py:911
  7.8 1.3 %collective-permute-start.2 = (f32[352,128]{1,0:T(8,128)S(1)}, f32[352,128]{1,0:T(8,128)S(1)}, u32[]{:S(2)}, u32[]{:S(2)}) collective-permute-start(f32[352,128]{1,0:T(8,128)S(1)} %get-tuple-element.69.own_ref), channel_id=1, source_target_pairs={{0,3},{4,7},{8,11},{12,15},{16,19},{20,23},{24,27},{28,31},{32,35}... | collective-permute-start | bytes 540680 | tf_op jit(solution)/shard_map/ppermute | solution.py:911
  9.2 0.8 second.1
  9.9 8.3 %all-to-all-start.3 = ((f32[128,2,128]{2,1,0:T(2,128)}), f32[128,2,128]{2,1,0:T(2,128)S(1)}, u32[]{:S(2)}, u32[]{:S(2)}) async-start(f32[128,2,128]{2,1,0:T(2,128)} %bitcast.51), calls=%async_computation.3 | async-start | bytes 262144 | tf_op jit(solution)/shard_map/all_to_all | solution.py:318
  18.2 2.6 %send_tables.1 = (f32[64,24,128]{2,1,0:T(8,128)S(1)}, f32[64,8,128]{2,1,0:T(8,128)S(1)}) custom-call(f32[3,64,128]{2,1,0:T(8,128)} %bitcast.45, f32[64,8,128]{2,1,0:T(8,128)} %charge_ref.3, s32[64]{0:T(128)} %count_ref.7, f32[3,64]{1,0:T(4,128)} %cen_ref.3), custom_call_target="tpu_custom_call" | custom-call | flops 50000000 | bytes 1200000 | tf_op jit(solution)/shard_map/send_tables/pallas_call | solution.py:914
  20.8 0.0 copy-start.1
  20.8 7.6 %all-to-all-done.3 = f32[128,2,128]{2,1,0:T(2,128)S(1)} async-done(((f32[128,2,128]{2,1,0:T(2,128)}), f32[128,2,128]{2,1,0:T(2,128)S(1)}, u32[]{:S(2)}, u32[]{:S(2)}) %all-to-all-start.3) | async-done | bytes 131104 | tf_op jit(solution)/shard_map/all_to_all | solution.py:318
  28.4 0.0 collective-permute-done.refs_0_
  28.5 0.0 collective-permute-done.1.refs_1_
  28.5 0.0 collective-permute-done.2.refs_2_
  28.5 0.0 copy-start.5
  28.5 0.0 copy-start.12
  28.5 2.6 %send.1 = f32[5632,128]{1,0:T(8,128)} custom-call(s32[1]{0:T(128)} %bitcast.16.member_ref, f32[256,128]{1,0:T(8,128)S(1)} %bitcast.34, f32[1536,128]{1,0:T(8,128)S(1)} %bitcast.36, f32[512,128]{1,0:T(8,128)S(1)} %bitcast.38, f32[352,128]{1,0:T(8,128)S(1)} %get-tuple-element.69.own_ref, f32[352,128]{1,0:T(8,128)S(1)} %collective-permute-done.refs_0_, ...), custom_call_target="tpu_custom_call" | custom-call | tf_op jit(solution)/shard_map/send/pallas_call | solution.py:925
  31.1 0.0 copy-start.2
  31.1 0.0 copy-start.3
  31.1 0.0 copy-start.9
  31.1 0.0 copy-start.11
  31.1 0.0 copy-done.1
  31.1 4.1 %all-to-all-start.4 = ((f32[128,11,4,128]{3,2,1,0:T(4,128)}), f32[128,11,4,128]{3,2,1,0:T(4,128)S(1)}, u32[]{:S(2)}, u32[]{:S(2)}) async-start(f32[128,11,4,128]{3,2,1,0:T(4,128)} %bitcast.41), calls=%async_computation.4 | async-start | bytes 5767168 | tf_op jit(solution)/shard_map/all_to_all | solution.py:318
  35.2 0.0 copy-done.5
  35.2 0.0 copy-done.12
  35.2 8.9 %own_tables.1 = (f32[64,8,128]{2,1,0:T(8,128)}, bf16[64,2,32,128]{3,2,1,0:T(8,128)(2,1)}, f32[64,8,128]{2,1,0:T(8,128)}) custom-call(f32[3,64,128]{2,1,0:T(8,128)S(1)} %bitcast.46, f32[64,8,128]{2,1,0:T(8,128)} %charge_ref.3, s32[64]{0:T(128)S(1)} %copy-done.12), custom_call_target="tpu_custom_call" | custom-call | flops 200000000 | bytes 4000000 | tf_op jit(solution)/shard_map/own_tables/pallas_call | solution.py:942
  44.1 0.0 copy-done.2
  44.1 0.0 copy-done.3
  44.1 0.0 copy-done.9
  44.1 2.7 %goals.1 = (f32[1024,128]{1,0:T(8,128)}, f32[1024,128]{1,0:T(8,128)}, f32[512,128]{1,0:T(8,128)}, s32[16,128]{1,0:T(8,128)}) custom-call(s32[128,128]{1,0:T(8,128)S(1)} %copy-done.2, f32[256,128]{1,0:T(8,128)S(1)} %bitcast.35, f32[3,64]{1,0:T(4,128)S(1)} %copy-done.9, f32[8,128]{1,0:T(8,128)S(1)} %copy-done.3), custom_call_target="tpu_custom_call" | custom-call | flops 50000000 | bytes 2000000 | tf_op jit(solution)/shard_map/goals/pallas_call | solution.py:952
  46.8 0.0 copy-done.11
  46.8 0.0 copy-start
  46.8 1.0 copy-done
  47.8 9.8 %far_values.1.v_hbm = bf16[128,256,128]{2,1,0:T(8,128)(2,1)} custom-call(f32[128,8,128]{2,1,0:T(8,128)S(1)} %bitcast.37, bf16[128,32]{1,0:T(8,128)(2,1)S(1)} %copy-done.11), custom_call_target="tpu_custom_call" | custom-call | flops 200000000 | bytes 9000000 | tf_op jit(solution)/shard_map/far_values/pallas_call | solution.py:969
  57.7 2.5 %compare_reduce_fusion = pred[128]{0:T(512)(128)(4,1)S(1)} fusion(f32[128,2,128]{2,1,0:T(2,128)S(1)} %all-to-all-done.3), kind=kLoop, calls=%fused_computation.10 | loop fusion | flops 128 | bytes 640 | tf_op jit(solution)/shard_map/gt | solution.py:1019
  60.2 12.5 %all-to-all-done.4 = f32[128,11,4,128]{3,2,1,0:T(4,128)S(1)} async-done(((f32[128,11,4,128]{3,2,1,0:T(4,128)}), f32[128,11,4,128]{3,2,1,0:T(4,128)S(1)}, u32[]{:S(2)}, u32[]{:S(2)}) %all-to-all-start.4) | async-done | bytes 2883616 | tf_op jit(solution)/shard_map/all_to_all | solution.py:318
  72.7 0.0 copy-start.6
  72.7 0.0 copy-start.8
  72.7 0.0 copy-start.10
  72.7 15.6 %pairs.3 = (f32[64,8,128]{2,1,0:T(8,128)}, f32[64,8,128]{2,1,0:T(8,128)}, f32[64,8,128]{2,1,0:T(8,128)}, f32[64,8,128]{2,1,0:T(8,128)}, f32[128,128]{1,0:T(8,128)}) custom-call(f32[5632,128]{1,0:T(8,128)S(1)} %bitcast.33, s32[16,128]{1,0:T(8,128)} %get-tuple-element.71.want_hbm, f32[128,8,128]{2,1,0:T(8,128)} %bitcast.63, f32[64,8,128]{2,1,0:T(8,128)} %bitcast.64, ...), custom_call_target="tpu_custom_call" | custom-call | flops 1000000000 | bytes 12000000 | tf_op jit(solution)/shard_map/pairs/pallas_call | solution.py:981
  88.4 5.4 %all-to-all-start.5 = ((f32[128,1,128]{2,1,0:T(1,128)}), f32[128,1,128]{2,1,0:T(1,128)S(1)}, u32[]{:S(2)}, u32[]{:S(2)}) async-start(f32[128,1,128]{2,1,0:T(1,128)} %bitcast.55), calls=%async_computation.5 | async-start | bytes 131072 | tf_op jit(solution)/shard_map/all_to_all | solution.py:318
  93.7 0.6 and_reduce_fusion
  95.0 2.9 %finish.1 = f32[64,8,128]{2,1,0:T(8,128)} custom-call(s32[64]{0:T(128)S(1)} %copy-done.12, f32[3,64,128]{2,1,0:T(8,128)S(1)} %bitcast.47, f32[64,8,128]{2,1,0:T(8,128)} %get-tuple-element.79.near0_ref, f32[64,8,128]{2,1,0:T(8,128)} %get-tuple-element.80.near1_ref, f32[64,8,128]{2,1,0:T(8,128)} %get-tuple-element.81.far0_ref, ...), custom_call_target="tpu_custom_call" | custom-call | flops 50000000 | bytes 3000000 | tf_op jit(solution)/shard_map/finish/pallas_call | solution.py:1009
  97.9 5.6 %all-to-all-done.5 = f32[128,1,128]{2,1,0:T(1,128)S(1)} async-done(((f32[128,1,128]{2,1,0:T(1,128)}), f32[128,1,128]{2,1,0:T(1,128)S(1)}, u32[]{:S(2)}, u32[]{:S(2)}) %all-to-all-start.5) | async-done | bytes 65568 | tf_op jit(solution)/shard_map/all_to_all | solution.py:318
  103.5 0.0 copy-done.6
  103.5 0.0 copy-done.8
  103.5 0.0 copy-done.10
  103.5 0.7 conditional.1
  103.5 0.7 slice_reduce_fusion
Async XLA Ops:
  3.2 25.2 %collective-permute-start = (f32[352,128]{1,0:T(8,128)S(1)}, f32[352,128]{1,0:T(8,128)S(1)}, u32[]{:S(2)}, u32[]{:S(2)}) collective-permute-start(f32[352,128]{1,0:T(8,128)S(1)} %get-tuple-element.69.own_ref), channel_id=1, source_target_pairs={{0,1},{4,5},{8,9},{12,13},{16,17},{20,21},{24,25},{28,29},{32,33},... | collective-permute-start | bytes 540680 | tf_op jit(solution)/shard_map/ppermute | solution.py:911
  5.5 22.9 %collective-permute-start.1 = (f32[352,128]{1,0:T(8,128)S(1)}, f32[352,128]{1,0:T(8,128)S(1)}, u32[]{:S(2)}, u32[]{:S(2)}) collective-permute-start(f32[352,128]{1,0:T(8,128)S(1)} %get-tuple-element.69.own_ref), channel_id=1, source_target_pairs={{0,2},{4,6},{8,10},{12,14},{16,18},{20,22},{24,26},{28,30},{32,34}... | collective-permute-start | bytes 540680 | tf_op jit(solution)/shard_map/ppermute | solution.py:911
  7.8 20.6 %collective-permute-start.2 = (f32[352,128]{1,0:T(8,128)S(1)}, f32[352,128]{1,0:T(8,128)S(1)}, u32[]{:S(2)}, u32[]{:S(2)}) collective-permute-start(f32[352,128]{1,0:T(8,128)S(1)} %get-tuple-element.69.own_ref), channel_id=1, source_target_pairs={{0,3},{4,7},{8,11},{12,15},{16,19},{20,23},{24,27},{28,31},{32,35}... | collective-permute-start | bytes 540680 | tf_op jit(solution)/shard_map/ppermute | solution.py:911
  9.9 18.5 %all-to-all-start.3 = ((f32[128,2,128]{2,1,0:T(2,128)}), f32[128,2,128]{2,1,0:T(2,128)S(1)}, u32[]{:S(2)}, u32[]{:S(2)}) async-start(f32[128,2,128]{2,1,0:T(2,128)} %bitcast.51), calls=%async_computation.3 | async-start | bytes 262144 | tf_op jit(solution)/shard_map/all_to_all | solution.py:318
  20.8 10.3 %copy-start.1 = (f32[64,8,128]{2,1,0:T(8,128)}, f32[64,8,128]{2,1,0:T(8,128)S(1)}, u32[]{:S(2)}) copy-start(f32[64,8,128]{2,1,0:T(8,128)S(1)} %get-tuple-element.68.w_hbm) | copy-start | bytes 786436
  28.5 6.7 %copy-start.5 = (f32[64,3,128]{2,0,1:T(8,128)S(1)}, f32[64,3,128]{2,0,1:T(8,128)}, u32[]{:S(2)}) copy-start(f32[64,3,128]{2,0,1:T(8,128)} %param.12) | copy-start | bytes 294916
  28.5 6.7 %copy-start.12 = (s32[64]{0:T(128)S(1)}, s32[64]{0:T(128)}, u32[]{:S(2)}) copy-start(s32[64]{0:T(128)} %count_ref.7) | copy-start | bytes 772
  31.1 13.0 %copy-start.2 = (s32[128,128]{1,0:T(8,128)S(1)}, s32[128,128]{1,0:T(8,128)}, u32[]{:S(2)}) copy-start(s32[128,128]{1,0:T(8,128)} %get-tuple-element.70.want_ref) | copy-start | bytes 196612
  31.1 13.0 %copy-start.3 = (f32[8,128]{1,0:T(8,128)S(1)}, f32[8,128]{1,0:T(8,128)}, u32[]{:S(2)}) copy-start(f32[8,128]{1,0:T(8,128)} %constant.51.clone.node_ref) | copy-start | bytes 12292
  31.1 13.0 %copy-start.9 = (f32[3,64]{1,0:T(4,128)S(1)}, f32[3,64]{1,0:T(4,128)}, u32[]{:S(2)}) copy-start(f32[3,64]{1,0:T(4,128)} %cen_ref.3) | copy-start | bytes 2308
  31.1 15.7 %copy-start.11 = (bf16[128,32]{1,0:T(8,128)(2,1)S(1)}, bf16[128,32]{1,0:T(8,128)(2,1)}, u32[]{:S(2)}) copy-start(bf16[128,32]{1,0:T(8,128)(2,1)} %constant.52.clone.fn_ref) | copy-start | bytes 24580
  31.1 41.6 %all-to-all-start.4 = ((f32[128,11,4,128]{3,2,1,0:T(4,128)}), f32[128,11,4,128]{3,2,1,0:T(4,128)S(1)}, u32[]{:S(2)}, u32[]{:S(2)}) async-start(f32[128,11,4,128]{3,2,1,0:T(4,128)} %bitcast.41), calls=%async_computation.4 | async-start | bytes 5767168 | tf_op jit(solution)/shard_map/all_to_all | solution.py:318
  46.8 1.0 %copy-start = (f32[1024,128]{1,0:T(8,128)S(1)}, f32[1024,128]{1,0:T(8,128)}, u32[]{:S(2)}) copy-start(f32[1024,128]{1,0:T(8,128)} %get-tuple-element.77) | copy-start | bytes 1572868
  72.7 30.8 %copy-start.6 = (f32[64,8,128]{2,1,0:T(8,128)S(1)}, f32[64,8,128]{2,1,0:T(8,128)}, u32[]{:S(2)}) copy-start(f32[64,8,128]{2,1,0:T(8,128)} %charge_ref.3) | copy-start | bytes 786436
  72.7 30.8 %copy-start.8 = (s32[64,9]{0,1:T(8,128)S(1)}, s32[64,9]{0,1:T(8,128)}, u32[]{:S(2)}) copy-start(s32[64,9]{0,1:T(8,128)} %param.17) | copy-start | bytes 6916
  72.7 30.8 %copy-start.10 = (s32[64,8]{0,1:T(8,128)S(1)}, s32[64,8]{0,1:T(8,128)}, u32[]{:S(2)}) copy-start(s32[64,8]{0,1:T(8,128)} %param.16) | copy-start | bytes 6148
  88.4 15.1 %all-to-all-start.5 = ((f32[128,1,128]{2,1,0:T(1,128)}), f32[128,1,128]{2,1,0:T(1,128)S(1)}, u32[]{:S(2)}, u32[]{:S(2)}) async-start(f32[128,1,128]{2,1,0:T(1,128)} %bitcast.55), calls=%async_computation.5 | async-start | bytes 131072 | tf_op jit(solution)/shard_map/all_to_all | solution.py:318
